TPU v7x, 32 devices: a whole 2x2x4 slice. The times are simulated.
32 devices in a mesh: feat: 4 (over y, core), ex: 8 (over z, x).
Axes of the slice: x: 2, y: 2, z: 4, core: 2. Of those that a mesh axis runs over, the one named last changes fastest.
Arguments:
- gradients: bfloat16 [8, 67108864], P('ex', 'feat'), may hold values from -6 to 6
- sign_words: int32 [4194304], P('feat'), may hold values from 0 to 65535
- sub_index: int32 [8192], replicated, may hold values from 0 to 67108863, as said below
- test_sketch: bfloat16 [1024, 8192], P('ex'), may hold values from -6 to 6
Outputs:
- scores: float32 [8, 1024], P('ex')
Inputs may be any that keep to these rules, and one draw needn't show every extreme that they name: `sub_index`: strictly increasing; entry k lies in [k * 8192, (k + 1) * 8192); the first entry is 0 and the last is 67108863.
All inputs are finite; a program needn't handle non-finite values.
Results may differ from a plain program's by a relative error of at most 0.0051.
Values may be sent and summed in bfloat16 or wider, within the bound.
No kernel may reach another device: no remote copies, remote signals or barrier semaphores. Data moves between devices by JAX's collectives and lax.ppermute only.
A program may use at most 832 MiB of HBM per device.

v0:
```python
import jax
import jax.numpy as jnp
from jax import lax
from jax.sharding import PartitionSpec as P

NHIGH = 1024
NMID = 256
NLOW = 256
K = 8192


def parity_sign(left, right, nbits):
    common = jnp.bitwise_and(left, right)
    total = jnp.zeros_like(common)
    for position in range(nbits):
        total = total + jnp.bitwise_and(jnp.right_shift(common, position), 1)
    return (1 - 2 * (total % 2)).astype(jnp.float32)


def hadamard_table(order):
    places = jnp.arange(order, dtype=jnp.int32)
    return parity_sign(places[:, None], places[None, :], order.bit_length() - 1)


def on_device(gradients, sign_words, sub_index, test_sketch):
    ex_rows = gradients.shape[0]
    local_features = gradients.shape[1]
    feat_place = lax.axis_index("feat")
    high_dev = local_features // (NMID * NLOW)
    all_rows = ex_rows * high_dev
    feature_scale = float(NHIGH * NMID * NLOW) ** (-0.5)
    score_scale = float(K) ** (-0.5)
    lane_rows = local_features // 128
    word_rows = jnp.repeat(sign_words.reshape(lane_rows, 8), 16, axis=1)
    lane_bits = jnp.arange(128, dtype=jnp.int32) % 16
    flags = jnp.bitwise_and(jnp.right_shift(word_rows, lane_bits[None, :]), 1)
    signs = (2 * flags - 1).astype(jnp.bfloat16)
    signed = (gradients.reshape(ex_rows, lane_rows, 128) * signs[None, :, :]).reshape(
        all_rows, NMID, NLOW
    )
    low_table = hadamard_table(NLOW).astype(jnp.bfloat16)
    mid_table = hadamard_table(NMID).astype(jnp.bfloat16)
    first = jnp.einsum("rml,pl->rmp", signed, low_table, preferred_element_type=jnp.float32).astype(
        jnp.bfloat16
    )
    second = jnp.einsum("qm,rmp->rqp", mid_table, first, preferred_element_type=jnp.float32).astype(
        jnp.bfloat16
    )
    second = second.reshape(ex_rows, high_dev, NMID * NLOW)
    high_of = sub_index // (NMID * NLOW)
    col_of = sub_index % (NMID * NLOW)
    high_bits = NHIGH.bit_length() - 1
    rows = feat_place * high_dev + jnp.arange(high_dev, dtype=jnp.int32)
    select = parity_sign(rows[:, None], high_of[None, :], high_bits).astype(jnp.bfloat16)
    picked = jnp.take(second, col_of, axis=2)
    partial_sketch = jnp.einsum("ehk,hk->ek", picked, select, preferred_element_type=jnp.float32)
    sketch = lax.psum(partial_sketch, "feat") * feature_scale
    sketch_rounded = sketch.astype(jnp.bfloat16)
    return (
        jnp.einsum(
            "ek,tk->et",
            sketch_rounded,
            lax.all_gather(test_sketch, "ex", axis=0, tiled=True),
            preferred_element_type=jnp.float32,
        )
        * score_scale
    )


def solution(mesh):
    return jax.shard_map(
        on_device,
        mesh=mesh,
        in_specs=(P("ex", "feat"), P("feat"), P(), P("ex", None)),
        out_specs=P("ex", None),
        check_vma=False,
    )
```

profile of v0, /device:TPU:0, one launch (start us, length us, event | category | flops | bytes accessed | tf_op | source)
XLA Modules:
  0.0 1154.3 jit_solution(15878785164954902644)
XLA Ops:
  6.5 0.0 all-gather.2.cloned.1.call-start
  6.5 0.7 all-gather.2.cloned.1.call-update
  7.3 42.4 %reshape.66 = s32[131072,8]{1,0:T(8,128)} reshape(s32[1048576]{0:T(1024)} %param.5) | data formatting | bytes 8388608 | tf_op jit(solution)/shard_map/reshape | solution.py:34
  49.7 224.3 %broadcast_in_dim.24 = s32[131072,8,16]{2,1,0:T(8,128)} broadcast(s32[131072,8]{1,0:T(8,128)} %reshape.66), dimensions={0,1} | broadcast | bytes 71303168 | tf_op jit(solution)/shard_map/broadcast_in_dim | solution.py:34
  274.0 356.7 %reshape.67 = s32[256,256,256]{2,1,0:T(8,128)} reshape(s32[131072,8,16]{2,1,0:T(8,128)} %broadcast_in_dim.24) | data formatting | bytes 134217728 | tf_op jit(solution)/shard_map/reshape | solution.py:34
  630.6 194.9 %reduce.1 = bf16[16777216]{0:T(1024)(128)(2,1)} reduce(bf16[1,16777216]{1,0:T(2,128)(2,1)} %param.4, bf16[]{:T(256)} %constant.120), dimensions={0}, to_apply=%param.4.reduce_sub_computation | reduce | bytes 67108864 | tf_op args[0]
  825.6 47.7 %reshape.65 = bf16[256,256,256]{2,1,0:T(8,128)(2,1)} reshape(bf16[16777216]{0:T(1024)(128)(2,1)} %reduce.1) | data formatting | bytes 67108864 | tf_op jit(solution)/shard_map/reshape | solution.py:38
  873.2 50.0 %convert_bitcast_fusion = bf16[256,256,256]{1,2,0:T(8,128)(2,1)} fusion(bf16[256,256,256]{2,1,0:T(8,128)(2,1)} %reshape.65, s32[256,256,256]{2,1,0:T(8,128)} %reshape.67, s32[256]{0:T(256)S(1)} %broadcast_bitcast_fusion), kind=kOutput, calls=%fused_computation.14 | convolution fusion | flops 17369530368 | bytes 134218752 | tf_op jit(solution)/shard_map/qm,rmp->rqp/dot_general | solution.py:46
  923.2 0.0 copy-start
  923.2 47.3 %copy.5 = bf16[256,256,256]{0,2,1:T(8,128)(2,1)} copy(bf16[256,256,256]{1,2,0:T(8,128)(2,1)} %convert_bitcast_fusion) | data formatting | bytes 67108864 | tf_op jit(solution)/shard_map/convert_element_type | solution.py:46
  970.5 0.0 copy-done
  970.5 13.3 %fusion.42 = f32[8192,256]{0,1:T(8,128)} fusion(s32[8192]{0:T(1024)S(1)} %get-tuple-element.6, s32[256]{0:T(256)S(1)} %iota_add_fusion), kind=kLoop, calls=%fused_computation.50 | loop fusion | flops 96468992 | bytes 8422400
  983.8 9.0 copy.11
  992.8 124.7 %gather_fusion = bf16[8192,256]{1,0:T(8,128)(2,1)} fusion(bf16[256,65536]{0,1:T(8,128)(2,1)} %bitcast.31, s32[8192]{0:T(1024)S(1)} %get-tuple-element.5), kind=kCustom, calls=%fused_computation | custom fusion | bytes 8421376 | tf_op jit(solution)/shard_map/jit(_take)/gather | solution.py:55
  1117.5 6.2 multiply_reduce_fusion
  1123.7 12.9 %psum.7 = f32[1,8192]{1,0:T(1,128)S(1)} all-reduce(f32[1,8192]{1,0:T(1,128)S(1)} %bitcast.32), channel_id=1, replica_groups=mesh['feat'=4,'ex'=8] {'feat'}, use_global_device_ids=true, to_apply=%region_0.1 | all-reduce | flops 8192 | bytes 65536 | tf_op jit(solution)/shard_map/psum | solution.py:57
  1136.6 0.0 all-gather.2.cloned.1.call-done
  1136.7 10.2 fusion.67
  1146.8 0.6 broadcast_multiply_fusion
  (5 shorter events, 0.1 us)
Async XLA Ops:
  6.5 1130.1 %all-gather.2.cloned.1.call-start = ((), (), s32[]{:S(2)}) async-start(), calls=%async_computation | async-start | bytes 18874368 | tf_op jit(solution)/shard_map/all_gather | solution.py:63
  923.2 47.3 %copy-start = (s32[8192]{0:T(1024)S(1)}, s32[8192]{0:T(1024)}, u32[]{:S(2)}) copy-start(s32[8192]{0:T(1024)} %param.6) | copy-start | bytes 98308
Sparse Core Ops, SparseCore 0:
  9.5 230.2 all-gather.1
where the time goes:
time: 1160 us; the launch traced here: 1150 us
  local copies, waits for them, and re-layouts  852 us (73%)
  other arithmetic  215 us (19%)
  matrix products  60.1 us (5%)
  between operations  13.4 us (1%)
  blocking collectives  12.9 us (1%)
    reshape x2, local copies, waits for them, and re-layouts, on_device(): word_rows = jnp.repeat(sign_words.reshape(lane_rows, 8), 16, axis=1)  399 us
    broadcast_in_dim x1, local copies, waits for them, and re-layouts, on_device(): word_rows = jnp.repeat(sign_words.reshape(lane_rows, 8), 16, axis=1)  224 us
    unnamed x2, other arithmetic  208 us
    gather x1, local copies, waits for them, and re-layouts, on_device(): picked = jnp.take(second, col_of, axis=2)  125 us
    dot_general x1, matrix products, on_device(): jnp.einsum('qm,rmp->rqp', mid_table, first, preferred_element_type=jnp.fl...  50 us
    reshape x1, local copies, waits for them, and re-layouts, on_device(): gradients.reshape(ex_rows, lane_rows, 128) * signs[None, :, :]  47.7 us
    convert_element_type x1, local copies, waits for them, and re-layouts, on_device(): jnp.einsum('qm,rmp->rqp', mid_table, first, preferred_element_type=jnp.fl...  47.3 us
  transfers between devices with their start and end apart: 1, of which 0 were waited for; matrix products, arithmetic and copies ran while one was open for 97% of the time, Pallas kernels for 0%

commit v1 on v0

v1 whole, which is shorter than its diff:
```python
import functools

import jax
import jax.numpy as jnp
from jax import lax
from jax.experimental import pallas as pl
from jax.experimental.pallas import tpu as pltpu
from jax.sharding import PartitionSpec as P

NMID = 256
NLOW = 256
TOP = 8
GROUP = 8
STEP = 4
SLOTS = 3
LANES = 128


def odd_common_bits(left, right):
    return jnp.bitwise_and(lax.population_count(jnp.bitwise_and(left, right)), 1) == 1


def iota(shape, axis):
    return lax.broadcasted_iota(jnp.int32, shape, axis)


def sketch_kernel(
    place_ref, grads, words, sub_ref, out_ref,
    xbuf, wbuf, wpair, table, ybuf, tbuf, picks, acc, sems, wsem,
    *, high_dev, scale,
):
    high_parts = out_ref.shape[0] * LANES // TOP // high_dev
    rest = NMID // TOP
    chunks = rest // GROUP
    steps = rest // STEP
    low_group = high_dev // 8
    points = high_parts * low_group
    depth = GROUP * low_group
    blocks = high_dev // 16 // 8
    copies = high_dev // (STEP * 8)
    half = LANES // 16

    def grad_copy(step, h):
        return pltpu.make_async_copy(
            grads.at[h, :, pl.ds(step * (2 * STEP), 2 * STEP)],
            xbuf.at[lax.rem(step, SLOTS), :, :, :, pl.ds(pl.multiple_of(h * LANES, LANES), LANES)],
            sems.at[lax.rem(step, SLOTS)],
        )

    def wait_step(step):
        slot = lax.rem(step, SLOTS)
        pltpu.make_async_copy(xbuf.at[slot], xbuf.at[slot], sems.at[slot]).wait()

    word_copy = pltpu.make_async_copy(words, wbuf, wsem)
    word_copy.start()

    @pl.loop(0, 2 * high_dev // 8)
    def _(n):
        for i in range(8):
            h = n * 8 + i
            step = h // high_dev
            grad_copy(step, h - step * high_dev).start()

    table[...] = jnp.where(
        odd_common_bits(iota(table.shape, 0), iota(table.shape, 1)), -1.0, 1.0
    ).astype(jnp.bfloat16)
    out_ref[...] = jnp.zeros_like(out_ref)
    lane8 = iota((8, LANES), 1)
    sub8 = iota((8, LANES), 0)

    def entry_columns(j, g):
        columns = []
        for hi in range(high_parts):
            for v in range(low_group // 8):
                row = (hi * high_dev + g * low_group) // 16 + v // 2
                line = jnp.broadcast_to(sub_ref[pl.ds(row, 1), :], (8, LANES))
                spot = ((v % 2) * 8 + sub8) * TOP + j
                columns.append((row, spot, jnp.take_along_axis(line, spot, axis=1, mode="promise_in_bounds")))
        return columns

    @pl.loop(0, TOP * 8)
    def _(e):
        j, g = e // 8, e % 8
        lane = iota((8, depth), 1)
        for n, (_, _, entry) in enumerate(entry_columns(j, g)):
            own = (n % (low_group // 8)) * 8 + iota((8, depth), 0)
            entry = jnp.concatenate([entry] * (depth // LANES), axis=1)
            odd = odd_common_bits(jnp.right_shift(entry, 8), lane // low_group)
            signs = jnp.where(lane % low_group == own, jnp.where(odd, -1.0, 1.0), 0.0)
            picks[e, n * 8 : n * 8 + 8, :] = signs

    word_copy.wait()
    per_high = NMID * NLOW // 16 // LANES

    @pl.loop(0, high_dev // 8)
    def _(n):
        for c in range(chunks):
            for pair in range(TOP // 2):
                one = wbuf[pl.ds(n * 8 * per_high + (2 * pair) * chunks + c, 8, per_high), :]
                two = wbuf[pl.ds(n * 8 * per_high + (2 * pair + 1) * chunks + c, 8, per_high), :]
                wpair[c, pair, pl.ds(pl.multiple_of(n * 8, 8), 8), :] = jnp.bitwise_or(
                    one, jnp.left_shift(two, 16)
                )

    def prepare(mid, u):
        slot = lax.rem(mid // STEP, SLOTS)
        chunk = mid // GROUP
        lane16 = iota((16, LANES), 1)
        bit_one = jnp.left_shift(1, lane16 % 16)
        bit_two = jnp.left_shift(1, lane16 % 16 + 16)
        for b in range(blocks):
            block = u * blocks + b
            rows = pl.ds(pl.multiple_of(block * 16, 16), 16)
            columns = pl.ds(pl.multiple_of(block * (16 * LANES), 16 * LANES), 16 * LANES)
            pairs = [wpair[chunk, pair, rows, :] for pair in range(TOP // 2)]
            for l_hi in range(2):
                spot = (mid % GROUP) * 16 + l_hi * half + lane16 // 16
                values = []
                for pair in range(TOP // 2):
                    word = jnp.take_along_axis(pairs[pair], spot, axis=1, mode="promise_in_bounds")
                    for which, bit in ((0, bit_one), (1, bit_two)):
                        value = xbuf[slot, 2 * pair + which, (mid % STEP) * 2 + l_hi, :, columns]
                        value = value.reshape(16, LANES).astype(jnp.float32)
                        values.append(jnp.where(jnp.bitwise_and(word, bit) != 0, value, -value))
                reach = 1
                while reach < TOP:
                    nxt = list(values)
                    for at in range(TOP):
                        if not at & reach:
                            nxt[at] = values[at] + values[at + reach]
                            nxt[at + reach] = values[at] - values[at + reach]
                    values, reach = nxt, reach * 2
                for j in range(TOP):
                    ybuf[lax.rem(mid, 2), j, rows, l_hi * LANES : (l_hi + 1) * LANES] = values[j].astype(
                        jnp.bfloat16
                    )

    def transform_high(mid, j):
        result = jnp.dot(table[...], ybuf[lax.rem(mid, 2), j], preferred_element_type=jnp.float32)
        return result.astype(jnp.bfloat16)

    def evaluate(chunk, e):
        j, g = e // 8, e % 8
        block = tbuf[chunk % 2, j, :, pl.ds(pl.multiple_of(g * low_group, low_group), low_group), :]
        found = jnp.dot(
            picks[e].astype(jnp.bfloat16), block.reshape(depth, NLOW), preferred_element_type=jnp.float32
        )
        for n, (row, spot, entry) in enumerate(entry_columns(j, g)):
            rows = slice(n * 8, n * 8 + 8)
            flip = jnp.bitwise_and(entry, 128) != 0
            total = found[rows, LANES:]
            total = found[rows, :LANES] + jnp.where(flip, -total, total)
            if chunk:
                odd = odd_common_bits(entry, chunk * GROUP * 256)
                total = acc[e, rows, :] + jnp.where(odd, -total, total)
            if chunk < chunks - 1:
                acc[e, rows, :] = total
            else:
                total = jnp.where(odd_common_bits(entry, lane8), -total, total)
                value = jnp.sum(total, axis=1, keepdims=True)
                value = jnp.sum(jnp.where(lane8 == spot, value, 0.0), axis=0, keepdims=True)
                out_ref[pl.ds(row, 1), :] += value

    def stretch(first, last, chunk, with_prepare, with_copies):
        @pl.loop(first, last)
        def _(i):
            mid = chunk * GROUP + i
            if with_prepare:

                @pl.when(lax.rem(mid + 1, STEP) == 0)
                def _():
                    wait_step((mid + 1) // STEP)

            @pl.loop(0, TOP)
            def _(u):
                high = transform_high(mid, u)
                if chunk:
                    evaluate(chunk - 1, i * 8 + u)
                if with_prepare:
                    prepare(mid + 1, u)
                if with_copies:
                    for n in range(copies):
                        ahead = (mid + 1) // STEP + 2
                        h = (((mid + 1) % STEP) * 8 + u) * copies + n
                        grad_copy(ahead, h).start()
                tbuf[chunk % 2, u, i] = high

    wait_step(0)

    @pl.loop(0, TOP)
    def _(u):
        prepare(0, u)
        for n in range(copies):
            grad_copy(2, u * copies + n).start()

    end_copies = (steps - 2) * STEP - 1
    for chunk in range(chunks):
        base = chunk * GROUP
        cuts = sorted({0, GROUP, min(max(end_copies - base, 0), GROUP), min(max(rest - 1 - base, 0), GROUP)})
        for first, last in zip(cuts[:-1], cuts[1:]):
            stretch(first, last, chunk, base + first < rest - 1, base + first < end_copies)

    @pl.loop(0, TOP * 8)
    def _(e):
        evaluate(chunks - 1, e)

    place = place_ref[0]
    rows = high_dev * TOP // LANES
    for hi in range(high_parts):
        common = jnp.bitwise_and(place, hi)
        odd = jnp.bitwise_and(common ^ (common >> 1) ^ (common >> 2) ^ (common >> 3), 1)
        sign = jnp.where(odd == 1, -scale, scale)
        out_ref[hi * rows : (hi + 1) * rows, :] = out_ref[hi * rows : (hi + 1) * rows, :] * sign


def partial_sketch(gradients, sign_words, sub_index, place, high_dev, scale):
    kept = sub_index.shape[0]
    rest = NMID // TOP
    low_group = high_dev // 8
    points = kept // (TOP * 8)
    grads = gradients.reshape(high_dev, TOP, rest * 2, 1, LANES)
    words = sign_words.reshape(-1, LANES)
    return pl.pallas_call(
        functools.partial(sketch_kernel, high_dev=high_dev, scale=scale),
        out_shape=jax.ShapeDtypeStruct((kept // LANES, LANES), jnp.float32),
        in_specs=[
            pl.BlockSpec(memory_space=pltpu.SMEM),
            pl.BlockSpec(memory_space=pl.ANY),
            pl.BlockSpec(memory_space=pl.ANY),
            pl.BlockSpec(memory_space=pltpu.VMEM),
        ],
        out_specs=pl.BlockSpec(memory_space=pltpu.VMEM),
        scratch_shapes=[
            pltpu.VMEM((SLOTS, TOP, 2 * STEP, 1, high_dev * LANES), jnp.bfloat16),
            pltpu.VMEM(words.shape, jnp.int32),
            pltpu.VMEM((rest // GROUP, TOP // 2, high_dev, LANES), jnp.int32),
            pltpu.VMEM((high_dev, high_dev), jnp.bfloat16),
            pltpu.VMEM((2, TOP, high_dev, NLOW), jnp.bfloat16),
            pltpu.VMEM((2, TOP, GROUP, high_dev, NLOW), jnp.bfloat16),
            pltpu.VMEM((TOP * 8, points, GROUP * low_group), jnp.float32),
            pltpu.VMEM((TOP * 8, points, LANES), jnp.float32),
            pltpu.SemaphoreType.DMA((SLOTS,)),
            pltpu.SemaphoreType.DMA,
        ],
        compiler_params=pltpu.CompilerParams(vmem_limit_bytes=62 * 1024 * 1024),
        name="sketch",
    )(place, grads, words, sub_index.reshape(kept // LANES, LANES))


def on_device(gradients, sign_words, sub_index, test_sketch, *, feat_size):
    local_features = gradients.shape[1]
    kept = sub_index.shape[0]
    high_dev = local_features // (NMID * NLOW)
    feature_scale = float(local_features * feat_size) ** (-0.5)
    score_scale = float(kept) ** (-0.5)
    place = lax.axis_index("feat").astype(jnp.int32).reshape(1)
    share = partial_sketch(gradients, sign_words, sub_index, place, high_dev, feature_scale)
    sketch = lax.psum(share, "feat").astype(jnp.bfloat16).reshape(1, kept)
    sketches = lax.all_gather(sketch, "ex", axis=0, tiled=True)
    scores = jnp.einsum("ek,tk->et", sketches, test_sketch, preferred_element_type=jnp.float32)
    scores = lax.all_to_all(scores, "ex", split_axis=0, concat_axis=1, tiled=True)
    return scores * score_scale


def solution(mesh):
    return jax.shard_map(
        functools.partial(on_device, feat_size=mesh.shape["feat"]),
        mesh=mesh,
        in_specs=(P("ex", "feat"), P("feat"), P(), P("ex", None)),
        out_specs=P("ex", None),
        check_vma=False,
    )
```

time: 1160 us -> 160 us (0.14)
  local copies, waits for them, and re-layouts: 852 us -> 0.02 us
  other arithmetic: 215 us -> 0.6 us
  Pallas kernels: 0 us -> 101 us
  matrix products: 60.1 us -> 2.25 us
  blocking collectives: 12.9 us -> 56.4 us
  between operations: 13.4 us -> 0.01 us
    reshape x3 -> x0, local copies, waits for them, and re-layouts: 447 us -> none  [the longest x2 399 us: on_device(): word_rows = jnp.repeat(sign_words.reshape(lane_rows, 8), 16, axis=1)]
    broadcast_in_dim x1 -> x0, local copies, waits for them, and re-layouts: 224 us -> none  [on_device(): word_rows = jnp.repeat(sign_words.reshape(lane_rows, 8), 16, axis=1)]
    unnamed x2 -> x0, other arithmetic: 208 us -> none
    gather x1 -> x0, local copies, waits for them, and re-layouts: 125 us -> none  [on_device(): picked = jnp.take(second, col_of, axis=2)]
    pallas_call x0 -> x1, Pallas kernels: none -> 101 us  [partial_sketch(): pl.pallas_call(functools.partial(sketch_kernel, high_dev=high_dev, scale=...]
    dot_general x2 -> x1, matrix products: 60.1 us -> 2.25 us  [on_device(): jnp.einsum('ek,tk->et', sketches, test_sketch, preferred_element_type=jnp...]
    convert_element_type x1 -> x0, local copies, waits for them, and re-layouts: 47.3 us -> none  [on_device(): jnp.einsum('qm,rmp->rqp', mid_table, first, preferred_element_type=jnp.fl...]
    all_gather x0 -> x1, blocking collectives: none -> 31.1 us  [on_device(): sketches = lax.all_gather(sketch, 'ex', axis=0, tiled=True)]
  transfers between devices with their start and end apart: 1 -> 0, of which waited for: 0 -> 0; matrix products, arithmetic and copies ran while one was open for 97% -> 0% of each run, Pallas kernels for 0% -> 0%
where the time goes in v1:
time: 160 us
  Pallas kernels  101 us (63%)
  blocking collectives  56.4 us (35%)
  matrix products  2.25 us (1%)
    pallas_call x1, Pallas kernels, partial_sketch(): pl.pallas_call(functools.partial(sketch_kernel, high_dev=high_dev, scale=...  101 us
    all_gather x1, blocking collectives, on_device(): sketches = lax.all_gather(sketch, 'ex', axis=0, tiled=True)  31.1 us
    psum x1, blocking collectives, on_device(): sketch = lax.psum(share, 'feat').astype(jnp.bfloat16).reshape(1, kept)  13.5 us
    all_to_all x1, blocking collectives, on_device(): lax.all_to_all(scores, 'ex', split_axis=0, concat_axis=1, tiled=True)  11.7 us

profile of v1, /device:TPU:0, one launch (start us, length us, event | category | flops | bytes accessed | tf_op | source)
XLA Modules:
  0.0 159.8 jit_solution(17251751489056067118)
XLA Ops:
  0.0 100.6 %sketch.1 = f32[64,128]{1,0:T(8,128)} custom-call(s32[1]{0:T(128)} %bitcast.place_ref, bf16[256,8,64,1,128]{4,3,2,1,0:T(2,128)(2,1)} %bitcast.1.grads, s32[8192,128]{1,0:T(8,128)} %bitcast.13, s32[64,128]{1,0:T(8,128)} %bitcast.14), custom_call_target="tpu_custom_call" | custom-call | tf_op jit(solution)/shard_map/sketch/pallas_call | solution.py:223
  100.6 13.5 %psum.7 = bf16[64,128]{1,0:T(8,128)(2,1)S(1)} all-reduce(f32[64,128]{1,0:T(8,128)} %sketch.1), channel_id=1, replica_groups=mesh['feat'=4,'ex'=8] {'feat'}, use_global_device_ids=true, to_apply=%region_0.0 | all-reduce | flops 8192 | bytes 49152 | tf_op jit(solution)/shard_map/psum | solution.py:258
  114.1 31.1 %all-gather = bf16[8,1,8192]{2,1,0:T(2,128)(2,1)S(1)} all-gather(bf16[1,1,8192]{2,1,0:T(2,128)(2,1)S(1)} %reshape.40), channel_id=1, replica_groups=mesh['feat'=4,'ex'=8] {'ex'}, dimensions={0}, use_global_device_ids=true | all-gather | bytes 147456 | tf_op jit(solution)/shard_map/all_gather | solution.py:259
  145.2 2.3 %fusion = f32[8,128]{1,0:T(8,128)S(1)} fusion(bf16[128,8192]{1,0:T(8,128)(2,1)} %param.7, bf16[8,1,8192]{2,1,0:T(2,128)(2,1)S(1)} %all-gather), kind=kOutput, calls=%fused_computation | convolution fusion | flops 16777216 | bytes 2232320 | tf_op jit(solution)/shard_map/ek,tk->et/dot_general | solution.py:260
  147.5 11.7 %all_to_all.13 = f32[8,1,128]{2,1,0:T(1,128)S(1)} all-to-all(f32[8,1,128]{2,1,0:T(1,128)S(1)} %bitcast.15), channel_id=1, replica_groups=mesh['feat'=4,'ex'=8] {'ex'}, dimensions={0} | all-to-all | bytes 8192 | tf_op jit(solution)/shard_map/all_to_all | solution.py:261
  159.2 0.6 multiply_bitcast_fusion
  (1 shorter events, 0.0 us)

commit v2 on v1

v2 whole, which is shorter than its diff:
```python
import functools

import jax
import jax.numpy as jnp
from jax import lax
from jax.experimental import pallas as pl
from jax.experimental.pallas import tpu as pltpu
from jax.sharding import PartitionSpec as P

NMID = 256
NLOW = 256
TOP = 8
GROUP = 8
STEP = 4
SLOTS = 3
HALVED = TOP // 2
LANES = 128
PACK = 16


def odd_common_bits(left, right):
    return jnp.bitwise_and(lax.population_count(jnp.bitwise_and(left, right)), 1) == 1


def iota(shape, axis):
    return lax.broadcasted_iota(jnp.int32, shape, axis)


def sketch_kernel(
    place_ref, grads, words, sub_ref, out_ref,
    xbuf, wbuf, wpair, table, ybuf, tbuf, entries, weights, signs, acc, found_rows, sems, wsem,
    *, high_dev, scale,
):
    high_parts = out_ref.shape[0] * LANES // TOP // high_dev
    rest = NMID // TOP
    chunks = rest // GROUP
    steps = rest // STEP
    groups = high_dev // PACK
    points = entries.shape[2]
    pairs = HALVED * groups
    rounds = GROUP * TOP
    blocks = high_dev // PACK // TOP
    copies = high_dev // (STEP * TOP)
    half = LANES // 16

    def grad_copy(step, h):
        return pltpu.make_async_copy(
            grads.at[h, :, pl.ds(step * (2 * STEP), 2 * STEP)],
            xbuf.at[lax.rem(step, SLOTS), :, :, :, pl.ds(pl.multiple_of(h * LANES, LANES), LANES)],
            sems.at[lax.rem(step, SLOTS)],
        )

    def wait_step(step):
        slot = lax.rem(step, SLOTS)
        pltpu.make_async_copy(xbuf.at[slot], xbuf.at[slot], sems.at[slot]).wait()

    word_copy = pltpu.make_async_copy(words, wbuf, wsem)
    word_copy.start()

    @pl.loop(0, 2 * high_dev // 8)
    def _(n):
        for i in range(8):
            h = n * 8 + i
            step = h // high_dev
            grad_copy(step, h - step * high_dev).start()

    table[...] = jnp.where(
        odd_common_bits(iota(table.shape, 0), iota(table.shape, 1)), -1.0, 1.0
    ).astype(jnp.bfloat16)
    acc[...] = jnp.zeros_like(acc)
    lane = iota((groups, LANES), 1)
    for j in range(HALVED):
        spot = (lane // 2 % PACK) * TOP + 2 * j + lane % 2
        for part in range(points // LANES):
            line = jnp.zeros((groups, LANES), jnp.int32)
            for n in range(LANES // (2 * PACK)):
                hi = part * (LANES // (2 * PACK)) + n
                rows = sub_ref[hi * groups : (hi + 1) * groups, :]
                taken = jnp.take_along_axis(rows, spot, axis=1, mode="promise_in_bounds")
                line = jnp.where(lane // (2 * PACK) == n, taken, line)
            entries[j, :, part * LANES : (part + 1) * LANES] = line

    @pl.loop(0, pairs)
    def _(e):
        entry = entries[e // groups, pl.ds(e % groups, 1), :]
        row = iota((24, points), 0)
        mask = jnp.where(
            row < 2 * GROUP,
            jnp.bitwise_or(jnp.left_shift(row % GROUP, 8), jnp.left_shift(row // GROUP, 13)),
            jnp.left_shift(row - 2 * GROUP, 11),
        )
        signs[e] = jnp.where(odd_common_bits(entry, mask), -1.0, 1.0)
        weights[e] = jnp.where(
            odd_common_bits(entry, iota((NLOW, points), 0)), -1.0, 1.0
        ).astype(jnp.bfloat16)

    word_copy.wait()
    per_high = NMID * NLOW // 16 // LANES

    @pl.loop(0, high_dev // 8)
    def _(n):
        for c in range(chunks):
            for pair in range(TOP // 2):
                one = wbuf[pl.ds(n * 8 * per_high + (2 * pair) * chunks + c, 8, per_high), :]
                two = wbuf[pl.ds(n * 8 * per_high + (2 * pair + 1) * chunks + c, 8, per_high), :]
                wpair[c, pair, pl.ds(pl.multiple_of(n * 8, 8), 8), :] = jnp.bitwise_or(
                    one, jnp.left_shift(two, 16)
                )

    def prepare(mid, u):
        slot = lax.rem(mid // STEP, SLOTS)
        chunk = mid // GROUP
        lane16 = iota((PACK, LANES), 1)
        bit_one = jnp.left_shift(1, lane16 % 16)
        bit_two = jnp.left_shift(1, lane16 % 16 + 16)
        for b in range(blocks):
            block = u * blocks + b
            rows = pl.ds(pl.multiple_of(block * PACK, PACK), PACK)
            columns = pl.ds(pl.multiple_of(block * (PACK * LANES), PACK * LANES), PACK * LANES)
            both = [wpair[chunk, pair, rows, :] for pair in range(TOP // 2)]
            for l_hi in range(2):
                spot = (mid % GROUP) * 16 + l_hi * half + lane16 // 16
                values = []
                for pair in range(TOP // 2):
                    word = jnp.take_along_axis(both[pair], spot, axis=1, mode="promise_in_bounds")
                    for which, bit in ((0, bit_one), (1, bit_two)):
                        value = xbuf[slot, 2 * pair + which, (mid % STEP) * 2 + l_hi, :, columns]
                        value = value.reshape(PACK, LANES).astype(jnp.float32)
                        values.append(jnp.where(jnp.bitwise_and(word, bit) != 0, value, -value))
                for reach in (2, 4):
                    nxt = list(values)
                    for at in range(TOP):
                        if not at & reach:
                            nxt[at] = values[at] + values[at + reach]
                            nxt[at + reach] = values[at] - values[at + reach]
                    values = nxt
                for j in range(TOP):
                    ybuf[lax.rem(mid, 2), j, rows, l_hi * LANES : (l_hi + 1) * LANES] = values[j].astype(
                        jnp.bfloat16
                    )

    def transform_high(chunk, i, u):
        result = jnp.dot(table[...], ybuf[i % 2, u], preferred_element_type=jnp.float32)
        tbuf[chunk % 2, u // 2, (u % 2) * GROUP + i] = result.astype(jnp.bfloat16)

    def evaluate(chunk, e):
        j, g = e // groups, e % groups
        block = tbuf[chunk % 2, j, :, pl.ds(pl.multiple_of(g * PACK, PACK), PACK), :]
        found = jnp.dot(
            block.reshape(2 * GROUP * PACK, NLOW), weights[e], preferred_element_type=jnp.float32
        )
        total = found[:PACK] * signs[e, 0:1, :]
        for n in range(1, 2 * GROUP):
            total += found[n * PACK : (n + 1) * PACK] * signs[e, n : n + 1, :]
        acc[e] += total * signs[e, 2 * GROUP + chunk : 2 * GROUP + chunk + 1, :]

    def evaluate_round(chunk, n):
        if pairs >= rounds:
            for m in range(pairs // rounds):
                evaluate(chunk, n * (pairs // rounds) + m)
        else:
            pl.when(n < pairs)(lambda: evaluate(chunk, n))

    def stretch(first, last, chunk, with_prepare, with_copies):
        @pl.loop(first, last)
        def _(i):
            mid = chunk * GROUP + i
            if with_prepare:

                @pl.when(lax.rem(mid + 1, STEP) == 0)
                def _():
                    wait_step((mid + 1) // STEP)

            @pl.loop(0, TOP)
            def _(u):
                if with_copies:
                    for n in range(copies):
                        ahead = (mid + 1) // STEP + 2
                        h = (((mid + 1) % STEP) * TOP + u) * copies + n
                        grad_copy(ahead, h).start()
                if chunk:
                    evaluate_round(chunk - 1, i * TOP + u)
                transform_high(chunk, i, u)
                if with_prepare:
                    prepare(mid + 1, u)

    wait_step(0)

    @pl.loop(0, TOP)
    def _(u):
        prepare(0, u)
        for n in range(copies):
            grad_copy(2, u * copies + n).start()

    end_copies = (steps - 2) * STEP - 1
    for chunk in range(chunks):
        base = chunk * GROUP
        cuts = sorted({0, GROUP, min(max(end_copies - base, 0), GROUP), min(max(rest - 1 - base, 0), GROUP)})
        for first, last in zip(cuts[:-1], cuts[1:]):
            stretch(first, last, chunk, base + first < rest - 1, base + first < end_copies)

    @pl.loop(0, pairs)
    def _(e):
        evaluate(chunks - 1, e)
        own = iota((PACK, points), 1) // 2 % PACK == iota((PACK, points), 0)
        found_rows[e // groups, pl.ds(e % groups, 1), :] = jnp.sum(
            jnp.where(own, acc[e], 0.0), axis=0, keepdims=True
        )

    place = place_ref[0]
    shares = []
    for hi in range(high_parts):
        common = jnp.bitwise_and(place, hi)
        odd = jnp.bitwise_and(common ^ (common >> 1) ^ (common >> 2) ^ (common >> 3), 1)
        sign = jnp.where(odd == 1, -scale, scale)
        part, first = divmod(hi * 2 * PACK, LANES)
        spot = first + lane // TOP * 2 + lane % 2
        line = jnp.zeros((groups, LANES), jnp.float32)
        for j in range(HALVED):
            rows = found_rows[j, :, part * LANES : (part + 1) * LANES]
            taken = jnp.take_along_axis(rows, spot, axis=1, mode="promise_in_bounds")
            line = jnp.where(lane % TOP // 2 == j, taken, line)
        shares.append(line * sign)
    out_ref[...] = jnp.concatenate(shares, axis=0).astype(out_ref.dtype)


def partial_sketch(gradients, sign_words, sub_index, place, high_dev, scale):
    kept = sub_index.shape[0]
    rest = NMID // TOP
    groups = high_dev // PACK
    points = kept // (HALVED * groups)
    grads = gradients.reshape(high_dev, TOP, rest * 2, 1, LANES)
    words = sign_words.reshape(-1, LANES)
    return pl.pallas_call(
        functools.partial(sketch_kernel, high_dev=high_dev, scale=scale),
        out_shape=jax.ShapeDtypeStruct((kept // LANES, LANES), jnp.bfloat16),
        in_specs=[
            pl.BlockSpec(memory_space=pltpu.SMEM),
            pl.BlockSpec(memory_space=pl.ANY),
            pl.BlockSpec(memory_space=pl.ANY),
            pl.BlockSpec(memory_space=pltpu.VMEM),
        ],
        out_specs=pl.BlockSpec(memory_space=pltpu.VMEM),
        scratch_shapes=[
            pltpu.VMEM((SLOTS, TOP, 2 * STEP, 1, high_dev * LANES), jnp.bfloat16),
            pltpu.VMEM(words.shape, jnp.int32),
            pltpu.VMEM((rest // GROUP, TOP // 2, high_dev, LANES), jnp.int32),
            pltpu.VMEM((high_dev, high_dev), jnp.bfloat16),
            pltpu.VMEM((2, TOP, high_dev, NLOW), jnp.bfloat16),
            pltpu.VMEM((2, HALVED, 2 * GROUP, high_dev, NLOW), jnp.bfloat16),
            pltpu.VMEM((HALVED, groups, points), jnp.int32),
            pltpu.VMEM((HALVED * groups, NLOW, points), jnp.bfloat16),
            pltpu.VMEM((HALVED * groups, 24, points), jnp.float32),
            pltpu.VMEM((HALVED * groups, PACK, points), jnp.float32),
            pltpu.VMEM((HALVED, groups, points), jnp.float32),
            pltpu.SemaphoreType.DMA((SLOTS,)),
            pltpu.SemaphoreType.DMA,
        ],
        compiler_params=pltpu.CompilerParams(vmem_limit_bytes=62 * 1024 * 1024),
        name="sketch",
    )(place, grads, words, sub_index.reshape(kept // LANES, LANES))


def shifted(value, axis, size, shift):
    return lax.ppermute(value, axis, [(i, (i + shift) % size) for i in range(size)])


def on_device(gradients, sign_words, sub_index, test_sketch, *, feat_size, ex_size):
    local_features = gradients.shape[1]
    kept = sub_index.shape[0]
    high_dev = local_features // (NMID * NLOW)
    feature_scale = float(local_features * feat_size) ** (-0.5)
    score_scale = float(kept) ** (-0.5)
    place = lax.axis_index("feat").astype(jnp.int32).reshape(1)
    share = partial_sketch(gradients, sign_words, sub_index, place, high_dev, feature_scale)
    shares = [share] + [shifted(share, "ex", ex_size, s) for s in range(1, ex_size)]
    shares = jnp.stack(shares).reshape(ex_size, kept)
    scores = jnp.einsum("ek,tk->et", shares, test_sketch, preferred_element_type=jnp.float32)
    scores = jnp.stack(
        [scores[0]] + [shifted(scores[s], "ex", ex_size, -s) for s in range(1, ex_size)]
    )
    total = scores
    for s in range(1, feat_size):
        total = total + shifted(scores, "feat", feat_size, s)
    total = jnp.roll(total * score_scale, lax.axis_index("ex"), axis=0)
    return total.reshape(1, -1)


def solution(mesh):
    return jax.shard_map(
        functools.partial(on_device, feat_size=mesh.shape["feat"], ex_size=mesh.shape["ex"]),
        mesh=mesh,
        in_specs=(P("ex", "feat"), P("feat"), P(), P("ex", None)),
        out_specs=P("ex", None),
        check_vma=False,
    )
```

time: 160 us -> 130 us (0.81)
  blocking collectives: 56.4 us -> 0 us
  starting transfers between devices: 0 us -> 25.5 us
  Pallas kernels: 101 us -> 90.7 us
  waiting for transfers between devices: 0 us -> 8.81 us
    all_gather x1 -> x0, blocking collectives: 31.1 us -> none  [on_device(): sketches = lax.all_gather(sketch, 'ex', axis=0, tiled=True)]
    ppermute x0 -> x17, starting transfers between devices: none -> 25.5 us  [shifted(): lax.ppermute(value, axis, [(i, (i + shift) % size) for i in range(size)])]
    psum x1 -> x0, blocking collectives: 13.5 us -> none  [on_device(): sketch = lax.psum(share, 'feat').astype(jnp.bfloat16).reshape(1, kept)]
    all_to_all x1 -> x0, blocking collectives: 11.7 us -> none  [on_device(): lax.all_to_all(scores, 'ex', split_axis=0, concat_axis=1, tiled=True)]
    pallas_call x1, Pallas kernels: 101 us -> 90.7 us  [partial_sketch(): pl.pallas_call(functools.partial(sketch_kernel, high_dev=high_dev, scale=...]
    ppermute x0 -> x17, waiting for transfers between devices: none -> 8.81 us  [shifted(): lax.ppermute(value, axis, [(i, (i + shift) % size) for i in range(size)])]
  transfers between devices with their start and end apart: 0 -> 17, of which waited for: 0 -> 7; matrix products, arithmetic and copies ran while one was open for 0% -> 1% of each run, Pallas kernels for 0% -> 0%
where the time goes in v2:
time: 130 us; the launch traced here: 129 us
  Pallas kernels  90.7 us (70%)
  starting transfers between devices  25.5 us (20%)
  waiting for transfers between devices  8.81 us (7%)
  matrix products  2.23 us (2%)
  local copies, waits for them, and re-layouts  1.38 us (1%)
    pallas_call x1, Pallas kernels, partial_sketch(): pl.pallas_call(functools.partial(sketch_kernel, high_dev=high_dev, scale=...  90.7 us
    ppermute x17, starting transfers between devices, shifted(): lax.ppermute(value, axis, [(i, (i + shift) % size) for i in range(size)])  25.5 us
    ppermute x17, waiting for transfers between devices, shifted(): lax.ppermute(value, axis, [(i, (i + shift) % size) for i in range(size)])  8.81 us
  transfers between devices with their start and end apart: 17, of which 7 were waited for; matrix products, arithmetic and copies ran while one was open for 1% of the time, Pallas kernels for 0%

profile of v2, /device:TPU:0, one launch (start us, length us, event | category | flops | bytes accessed | tf_op | source)
XLA Modules:
  0.0 129.4 jit_solution(3192235301715066132)
XLA Ops:
  0.0 90.7 %sketch.1 = bf16[64,128]{1,0:T(8,128)(2,1)} custom-call(s32[1]{0:T(128)} %bitcast.place_ref, bf16[256,8,64,1,128]{4,3,2,1,0:T(2,128)(2,1)} %bitcast.1.grads, s32[8192,128]{1,0:T(8,128)} %bitcast.68, s32[64,128]{1,0:T(8,128)} %bitcast.78), custom_call_target="tpu_custom_call" | custom-call | tf_op jit(solution)/shard_map/sketch/pallas_call | solution.py:234
  90.7 6.0 %collective-permute-start.6 = (bf16[64,128]{1,0:T(8,128)(2,1)}, bf16[64,128]{1,0:T(8,128)(2,1)S(1)}, u32[]{:S(2)}, u32[]{:S(2)}) collective-permute-start(bf16[64,128]{1,0:T(8,128)(2,1)} %sketch.1), channel_id=1, source_target_pairs={{0,7},{1,0},{2,1},{3,2},{4,3},{5,4},{6,5},{7,6},{8,15},{9,8},{10,9... | collective-permute-start | bytes 49160 | tf_op jit(solution)/shard_map/ppermute | solution.py:265
  96.8 0.4 collective-permute-start.5
  97.2 0.0 collective-permute-start.4
  97.2 3.0 %collective-permute-start.3 = (bf16[64,128]{1,0:T(8,128)(2,1)}, bf16[64,128]{1,0:T(8,128)(2,1)S(1)}, u32[]{:S(2)}, u32[]{:S(2)}) collective-permute-start(bf16[64,128]{1,0:T(8,128)(2,1)} %sketch.1), channel_id=1, source_target_pairs={{0,4},{1,5},{2,6},{3,7},{4,0},{5,1},{6,2},{7,3},{8,12},{9,13},{10,... | collective-permute-start | bytes 49160 | tf_op jit(solution)/shard_map/ppermute | solution.py:265
  100.2 0.0 collective-permute-start.2
  100.2 0.0 collective-permute-done.6
  100.2 1.8 %collective-permute-start.1 = (bf16[64,128]{1,0:T(8,128)(2,1)}, bf16[64,128]{1,0:T(8,128)(2,1)S(1)}, u32[]{:S(2)}, u32[]{:S(2)}) collective-permute-start(bf16[64,128]{1,0:T(8,128)(2,1)} %sketch.1), channel_id=1, source_target_pairs={{0,2},{1,3},{2,4},{3,5},{4,6},{5,7},{6,0},{7,1},{8,10},{9,11},{10,... | collective-permute-start | bytes 49160 | tf_op jit(solution)/shard_map/ppermute | solution.py:265
  102.1 0.0 collective-permute-done.5
  102.1 1.1 collective-permute-start
  103.2 0.8 copy.28
  104.1 0.0 collective-permute-done.4
  104.1 0.0 collective-permute-done.3
  104.1 1.9 %collective-permute-done.2 = bf16[64,128]{1,0:T(8,128)(2,1)S(1)} collective-permute-done((bf16[64,128]{1,0:T(8,128)(2,1)}, bf16[64,128]{1,0:T(8,128)(2,1)S(1)}, u32[]{:S(2)}, u32[]{:S(2)}) %collective-permute-start.2) | collective-permute-done | bytes 16416 | tf_op jit(solution)/shard_map/ppermute | solution.py:265
  106.1 1.0 collective-permute-done.1
  107.1 1.6 %collective-permute-done = bf16[64,128]{1,0:T(8,128)(2,1)S(1)} collective-permute-done((bf16[64,128]{1,0:T(8,128)(2,1)}, bf16[64,128]{1,0:T(8,128)(2,1)S(1)}, u32[]{:S(2)}, u32[]{:S(2)}) %collective-permute-start) | collective-permute-done | bytes 16416 | tf_op jit(solution)/shard_map/ppermute | solution.py:265
  108.7 0.4 stack.59
  109.1 2.2 %fusion.1 = f32[8,128]{1,0:T(8,128)S(1)} fusion(bf16[8,8192]{1,0:T(8,128)(2,1)S(1)} %stack.59, bf16[128,8192]{1,0:T(8,128)(2,1)} %param.7), kind=kOutput, calls=%fused_computation.19 | convolution fusion | flops 16777216 | bytes 2232320 | tf_op jit(solution)/shard_map/ek,tk->et/dot_general | solution.py:278
  111.4 0.0 collective-permute-start.13
  111.4 0.5 collective-permute-start.12
  111.9 2.7 %collective-permute-start.11 = (f32[128]{0:T(128)S(1)}, f32[128]{0:T(128)S(1)}, u32[]{:S(2)}, u32[]{:S(2)}) collective-permute-start(f32[128]{0:T(128)S(1)} %get-tuple-element.7), channel_id=1, source_target_pairs={{0,3},{1,4},{2,5},{3,6},{4,7},{5,0},{6,1},{7,2},{8,11},{9,12},{10,... | collective-permute-start | bytes 1544 | tf_op jit(solution)/shard_map/ppermute | solution.py:265
  114.6 2.1 %collective-permute-start.10 = (f32[128]{0:T(128)S(1)}, f32[128]{0:T(128)S(1)}, u32[]{:S(2)}, u32[]{:S(2)}) collective-permute-start(f32[128]{0:T(128)S(1)} %get-tuple-element.8), channel_id=1, source_target_pairs={{0,4},{1,5},{2,6},{3,7},{4,0},{5,1},{6,2},{7,3},{8,12},{9,13},{10,... | collective-permute-start | bytes 1544 | tf_op jit(solution)/shard_map/ppermute | solution.py:265
  116.7 0.8 collective-permute-start.9
  117.5 0.1 collective-permute-done.13
  117.6 2.3 %collective-permute-start.8 = (f32[128]{0:T(128)S(1)}, f32[128]{0:T(128)S(1)}, u32[]{:S(2)}, u32[]{:S(2)}) collective-permute-start(f32[128]{0:T(128)S(1)} %get-tuple-element.10), channel_id=1, source_target_pairs={{0,6},{1,7},{2,0},{3,1},{4,2},{5,3},{6,4},{7,5},{8,14},{9,15},{10,... | collective-permute-start | bytes 1544 | tf_op jit(solution)/shard_map/ppermute | solution.py:265
  119.9 0.0 collective-permute-done.12
  119.9 2.9 %collective-permute-start.7 = (f32[128]{0:T(128)S(1)}, f32[128]{0:T(128)S(1)}, u32[]{:S(2)}, u32[]{:S(2)}) collective-permute-start(f32[128]{0:T(128)S(1)} %get-tuple-element.11), channel_id=1, source_target_pairs={{0,7},{1,0},{2,1},{3,2},{4,3},{5,4},{6,5},{7,6},{8,15},{9,8},{10,9... | collective-permute-start | bytes 1544 | tf_op jit(solution)/shard_map/ppermute | solution.py:265
  122.8 0.0 collective-permute-done.11
  122.8 0.0 collective-permute-done.10
  122.8 0.0 collective-permute-done.9
  122.8 0.0 collective-permute-done.8
  122.8 1.3 collective-permute-done.7
  124.1 0.1 collective-permute-start.16
  124.2 1.6 %collective-permute-start.15 = (f32[8,128]{1,0:T(8,128)S(1)}, f32[8,128]{1,0:T(8,128)S(1)}, u32[]{:S(2)}, u32[]{:S(2)}) collective-permute-start(f32[8,128]{1,0:T(8,128)S(1)} %stack.67), channel_id=1, source_target_pairs={{0,16},{8,24},{16,0},{24,8},{1,17},{9,25},{17,1},{25,9},{2,18},{10... | collective-permute-start | bytes 12296 | tf_op jit(solution)/shard_map/ppermute | solution.py:265
  125.7 0.2 collective-permute-start.14
  125.9 0.0 collective-permute-done.16
  125.9 1.9 %collective-permute-done.15 = f32[8,128]{1,0:T(8,128)S(1)} collective-permute-done((f32[8,128]{1,0:T(8,128)S(1)}, f32[8,128]{1,0:T(8,128)S(1)}, u32[]{:S(2)}, u32[]{:S(2)}) %collective-permute-start.15) | collective-permute-done | bytes 4128 | tf_op jit(solution)/shard_map/ppermute | solution.py:265
  127.8 0.9 collective-permute-done.14
  128.8 0.6 fusion
  (10 shorter events, 0.2 us)
Async XLA Ops:
  90.7 9.5 %collective-permute-start.6 = (bf16[64,128]{1,0:T(8,128)(2,1)}, bf16[64,128]{1,0:T(8,128)(2,1)S(1)}, u32[]{:S(2)}, u32[]{:S(2)}) collective-permute-start(bf16[64,128]{1,0:T(8,128)(2,1)} %sketch.1), channel_id=1, source_target_pairs={{0,7},{1,0},{2,1},{3,2},{4,3},{5,4},{6,5},{7,6},{8,15},{9,8},{10,9... | collective-permute-start | bytes 49160 | tf_op jit(solution)/shard_map/ppermute | solution.py:265
  96.8 5.3 %collective-permute-start.5 = (bf16[64,128]{1,0:T(8,128)(2,1)}, bf16[64,128]{1,0:T(8,128)(2,1)S(1)}, u32[]{:S(2)}, u32[]{:S(2)}) collective-permute-start(bf16[64,128]{1,0:T(8,128)(2,1)} %sketch.1), channel_id=1, source_target_pairs={{0,6},{1,7},{2,0},{3,1},{4,2},{5,3},{6,4},{7,5},{8,14},{9,15},{10,... | collective-permute-start | bytes 49160 | tf_op jit(solution)/shard_map/ppermute | solution.py:265
  97.2 6.8 %collective-permute-start.4 = (bf16[64,128]{1,0:T(8,128)(2,1)}, bf16[64,128]{1,0:T(8,128)(2,1)S(1)}, u32[]{:S(2)}, u32[]{:S(2)}) collective-permute-start(bf16[64,128]{1,0:T(8,128)(2,1)} %sketch.1), channel_id=1, source_target_pairs={{0,5},{1,6},{2,7},{3,0},{4,1},{5,2},{6,3},{7,4},{8,13},{9,14},{10,... | collective-permute-start | bytes 49160 | tf_op jit(solution)/shard_map/ppermute | solution.py:265
  97.2 6.9 %collective-permute-start.3 = (bf16[64,128]{1,0:T(8,128)(2,1)}, bf16[64,128]{1,0:T(8,128)(2,1)S(1)}, u32[]{:S(2)}, u32[]{:S(2)}) collective-permute-start(bf16[64,128]{1,0:T(8,128)(2,1)} %sketch.1), channel_id=1, source_target_pairs={{0,4},{1,5},{2,6},{3,7},{4,0},{5,1},{6,2},{7,3},{8,12},{9,13},{10,... | collective-permute-start | bytes 49160 | tf_op jit(solution)/shard_map/ppermute | solution.py:265
  100.2 5.9 %collective-permute-start.2 = (bf16[64,128]{1,0:T(8,128)(2,1)}, bf16[64,128]{1,0:T(8,128)(2,1)S(1)}, u32[]{:S(2)}, u32[]{:S(2)}) collective-permute-start(bf16[64,128]{1,0:T(8,128)(2,1)} %sketch.1), channel_id=1, source_target_pairs={{0,3},{1,4},{2,5},{3,6},{4,7},{5,0},{6,1},{7,2},{8,11},{9,12},{10,... | collective-permute-start | bytes 49160 | tf_op jit(solution)/shard_map/ppermute | solution.py:265
  100.2 6.9 %collective-permute-start.1 = (bf16[64,128]{1,0:T(8,128)(2,1)}, bf16[64,128]{1,0:T(8,128)(2,1)S(1)}, u32[]{:S(2)}, u32[]{:S(2)}) collective-permute-start(bf16[64,128]{1,0:T(8,128)(2,1)} %sketch.1), channel_id=1, source_target_pairs={{0,2},{1,3},{2,4},{3,5},{4,6},{5,7},{6,0},{7,1},{8,10},{9,11},{10,... | collective-permute-start | bytes 49160 | tf_op jit(solution)/shard_map/ppermute | solution.py:265
  102.1 6.6 %collective-permute-start = (bf16[64,128]{1,0:T(8,128)(2,1)}, bf16[64,128]{1,0:T(8,128)(2,1)S(1)}, u32[]{:S(2)}, u32[]{:S(2)}) collective-permute-start(bf16[64,128]{1,0:T(8,128)(2,1)} %sketch.1), channel_id=1, source_target_pairs={{0,1},{1,2},{2,3},{3,4},{4,5},{5,6},{6,7},{7,0},{8,9},{9,10},{10,1... | collective-permute-start | bytes 49160 | tf_op jit(solution)/shard_map/ppermute | solution.py:265
  111.4 6.3 %collective-permute-start.13 = (f32[128]{0:T(128)S(1)}, f32[128]{0:T(128)S(1)}, u32[]{:S(2)}, u32[]{:S(2)}) collective-permute-start(f32[128]{0:T(128)S(1)} %get-tuple-element.5), channel_id=1, source_target_pairs={{0,1},{1,2},{2,3},{3,4},{4,5},{5,6},{6,7},{7,0},{8,9},{9,10},{10,1... | collective-permute-start | bytes 1544 | tf_op jit(solution)/shard_map/ppermute | solution.py:265
  111.4 8.5 %collective-permute-start.12 = (f32[128]{0:T(128)S(1)}, f32[128]{0:T(128)S(1)}, u32[]{:S(2)}, u32[]{:S(2)}) collective-permute-start(f32[128]{0:T(128)S(1)} %get-tuple-element.6), channel_id=1, source_target_pairs={{0,2},{1,3},{2,4},{3,5},{4,6},{5,7},{6,0},{7,1},{8,10},{9,11},{10,... | collective-permute-start | bytes 1544 | tf_op jit(solution)/shard_map/ppermute | solution.py:265
  111.9 10.9 %collective-permute-start.11 = (f32[128]{0:T(128)S(1)}, f32[128]{0:T(128)S(1)}, u32[]{:S(2)}, u32[]{:S(2)}) collective-permute-start(f32[128]{0:T(128)S(1)} %get-tuple-element.7), channel_id=1, source_target_pairs={{0,3},{1,4},{2,5},{3,6},{4,7},{5,0},{6,1},{7,2},{8,11},{9,12},{10,... | collective-permute-start | bytes 1544 | tf_op jit(solution)/shard_map/ppermute | solution.py:265
  114.6 8.2 %collective-permute-start.10 = (f32[128]{0:T(128)S(1)}, f32[128]{0:T(128)S(1)}, u32[]{:S(2)}, u32[]{:S(2)}) collective-permute-start(f32[128]{0:T(128)S(1)} %get-tuple-element.8), channel_id=1, source_target_pairs={{0,4},{1,5},{2,6},{3,7},{4,0},{5,1},{6,2},{7,3},{8,12},{9,13},{10,... | collective-permute-start | bytes 1544 | tf_op jit(solution)/shard_map/ppermute | solution.py:265
  116.7 6.1 %collective-permute-start.9 = (f32[128]{0:T(128)S(1)}, f32[128]{0:T(128)S(1)}, u32[]{:S(2)}, u32[]{:S(2)}) collective-permute-start(f32[128]{0:T(128)S(1)} %get-tuple-element.9), channel_id=1, source_target_pairs={{0,5},{1,6},{2,7},{3,0},{4,1},{5,2},{6,3},{7,4},{8,13},{9,14},{10,... | collective-permute-start | bytes 1544 | tf_op jit(solution)/shard_map/ppermute | solution.py:265
  117.6 5.2 %collective-permute-start.8 = (f32[128]{0:T(128)S(1)}, f32[128]{0:T(128)S(1)}, u32[]{:S(2)}, u32[]{:S(2)}) collective-permute-start(f32[128]{0:T(128)S(1)} %get-tuple-element.10), channel_id=1, source_target_pairs={{0,6},{1,7},{2,0},{3,1},{4,2},{5,3},{6,4},{7,5},{8,14},{9,15},{10,... | collective-permute-start | bytes 1544 | tf_op jit(solution)/shard_map/ppermute | solution.py:265
  119.9 4.2 %collective-permute-start.7 = (f32[128]{0:T(128)S(1)}, f32[128]{0:T(128)S(1)}, u32[]{:S(2)}, u32[]{:S(2)}) collective-permute-start(f32[128]{0:T(128)S(1)} %get-tuple-element.11), channel_id=1, source_target_pairs={{0,7},{1,0},{2,1},{3,2},{4,3},{5,4},{6,5},{7,6},{8,15},{9,8},{10,9... | collective-permute-start | bytes 1544 | tf_op jit(solution)/shard_map/ppermute | solution.py:265
  124.1 1.8 %collective-permute-start.16 = (f32[8,128]{1,0:T(8,128)S(1)}, f32[8,128]{1,0:T(8,128)S(1)}, u32[]{:S(2)}, u32[]{:S(2)}) collective-permute-start(f32[8,128]{1,0:T(8,128)S(1)} %stack.67), channel_id=1, source_target_pairs={{0,24},{8,0},{16,8},{24,16},{1,25},{9,1},{17,9},{25,17},{2,26},{10... | collective-permute-start | bytes 12296 | tf_op jit(solution)/shard_map/ppermute | solution.py:265
  124.2 3.7 %collective-permute-start.15 = (f32[8,128]{1,0:T(8,128)S(1)}, f32[8,128]{1,0:T(8,128)S(1)}, u32[]{:S(2)}, u32[]{:S(2)}) collective-permute-start(f32[8,128]{1,0:T(8,128)S(1)} %stack.67), channel_id=1, source_target_pairs={{0,16},{8,24},{16,0},{24,8},{1,17},{9,25},{17,1},{25,9},{2,18},{10... | collective-permute-start | bytes 12296 | tf_op jit(solution)/shard_map/ppermute | solution.py:265
  125.7 3.0 %collective-permute-start.14 = (f32[8,128]{1,0:T(8,128)S(1)}, f32[8,128]{1,0:T(8,128)S(1)}, u32[]{:S(2)}, u32[]{:S(2)}) collective-permute-start(f32[8,128]{1,0:T(8,128)S(1)} %stack.67), channel_id=1, source_target_pairs={{0,8},{8,16},{16,24},{24,0},{1,9},{9,17},{17,25},{25,1},{2,10},{10... | collective-permute-start | bytes 12296 | tf_op jit(solution)/shard_map/ppermute | solution.py:265

commit v3 on v2

v3 whole, which is shorter than its diff:
```python
import functools

import jax
import jax.numpy as jnp
from jax import lax
from jax.experimental import pallas as pl
from jax.experimental.pallas import tpu as pltpu
from jax.sharding import PartitionSpec as P

NMID = 256
NLOW = 256
TOP = 8
GROUP = 8
STEP = 4
SLOTS = 2
ROWS = 2 * STEP
HALVED = TOP // 2
LANES = 128
PACK = 16


def odd_common_bits(left, right):
    return jnp.bitwise_and(lax.population_count(jnp.bitwise_and(left, right)), 1) == 1


def iota(shape, axis):
    return lax.broadcasted_iota(jnp.int32, shape, axis)


def sketch_kernel(
    place_ref, grads, words, sub_ref, out_ref,
    xbuf, wbuf, wpair, table, ybuf, tbuf, entries, weights, signs, acc, found_rows, sems, wsem,
    *, high_dev, scale,
):
    high_parts = out_ref.shape[0] * LANES // TOP // high_dev
    rest = NMID // TOP
    chunks = rest // GROUP
    steps = rest // STEP
    groups = high_dev // PACK
    points = entries.shape[2]
    pairs = HALVED * groups
    rounds = GROUP * TOP
    highs = high_dev // (STEP * TOP)
    half = LANES // 16
    stride = high_dev + 1

    def grad_copies(step, then):
        slot = lax.rem(step, SLOTS)
        for top in range(TOP):
            copy = pltpu.make_async_copy(
                grads.at[:, top, step],
                xbuf.at[slot, :, :, top * ROWS * LANES : (top + 1) * ROWS * LANES],
                sems.at[slot, top],
            )
            then(copy)

    word_copy = pltpu.make_async_copy(words, wbuf, wsem)
    word_copy.start()
    for step in range(SLOTS):
        grad_copies(step, lambda copy: copy.start())

    table[...] = jnp.where(
        odd_common_bits(iota(table.shape, 0), iota(table.shape, 1)), -1.0, 1.0
    ).astype(jnp.bfloat16)
    acc[...] = jnp.zeros_like(acc)
    lane = iota((groups, LANES), 1)
    for j in range(HALVED):
        spot = (lane // 2 % PACK) * TOP + 2 * j + lane % 2
        for part in range(points // LANES):
            line = jnp.zeros((groups, LANES), jnp.int32)
            for n in range(LANES // (2 * PACK)):
                hi = part * (LANES // (2 * PACK)) + n
                rows = sub_ref[hi * groups : (hi + 1) * groups, :]
                taken = jnp.take_along_axis(rows, spot, axis=1, mode="promise_in_bounds")
                line = jnp.where(lane // (2 * PACK) == n, taken, line)
            entries[j, :, part * LANES : (part + 1) * LANES] = line

    @pl.loop(0, pairs)
    def _(e):
        entry = entries[e // groups, pl.ds(e % groups, 1), :]
        row = iota((24, points), 0)
        mask = jnp.where(
            row < 2 * GROUP,
            jnp.bitwise_or(jnp.left_shift(row % GROUP, 8), jnp.left_shift(row // GROUP, 13)),
            jnp.left_shift(row - 2 * GROUP, 11),
        )
        signs[e] = jnp.where(odd_common_bits(entry, mask), -1.0, 1.0)
        weights[e] = jnp.where(
            odd_common_bits(entry, iota((NLOW, points), 0)), -1.0, 1.0
        ).astype(jnp.bfloat16)

    word_copy.wait()
    per_high = NMID * NLOW // 16 // LANES

    @pl.loop(0, high_dev // 8)
    def _(n):
        for c in range(chunks):
            for pair in range(TOP // 2):
                one = wbuf[pl.ds(n * 8 * per_high + (2 * pair) * chunks + c, 8, per_high), :]
                two = wbuf[pl.ds(n * 8 * per_high + (2 * pair + 1) * chunks + c, 8, per_high), :]
                wpair[c, pair, pl.ds(pl.multiple_of(n * 8, 8), 8), :] = jnp.bitwise_or(
                    one, jnp.left_shift(two, 16)
                )

    def prepare(step, u):
        slot = lax.rem(step, SLOTS)
        chunk = step * STEP // GROUP
        lane8 = iota((ROWS, LANES), 1)
        bits = [jnp.left_shift(1, lane8 % 16), jnp.left_shift(1, lane8 % 16 + 16)]
        spot = lax.rem(step, GROUP // STEP) * (16 * STEP) + iota((ROWS, LANES), 0) * half + lane8 // 16
        for n in range(highs):
            h = u * highs + n
            values = []
            for pair in range(TOP // 2):
                word = jnp.broadcast_to(wpair[chunk, pair, pl.ds(h, 1), :], (ROWS, LANES))
                word = jnp.take_along_axis(word, spot, axis=1, mode="promise_in_bounds")
                two = xbuf[slot, h, :, 2 * pair * ROWS * LANES : 2 * (pair + 1) * ROWS * LANES]
                two = two.reshape(2 * ROWS, LANES).astype(jnp.float32)
                for which in range(2):
                    value = two[which * ROWS : (which + 1) * ROWS]
                    values.append(jnp.where(jnp.bitwise_and(word, bits[which]) != 0, value, -value))
            for reach in (2, 4):
                nxt = list(values)
                for at in range(TOP):
                    if not at & reach:
                        nxt[at] = values[at] + values[at + reach]
                        nxt[at + reach] = values[at] - values[at + reach]
                values = nxt
            for top in range(TOP):
                ybuf[lax.rem(step, 2), top, pl.ds(h, ROWS, stride), :] = values[top]

    def transform_high(step, u):
        top, i = u % TOP, u // TOP
        columns = [
            ybuf[lax.rem(step, 2), top, pl.ds((2 * i + l_hi) * stride, high_dev), :].astype(jnp.bfloat16)
            for l_hi in range(2)
        ]
        result = jnp.dot(
            table[...], jnp.concatenate(columns, axis=1), preferred_element_type=jnp.float32
        )
        chunk = step * STEP // GROUP
        row = (top % 2) * GROUP + lax.rem(step, GROUP // STEP) * STEP + i
        tbuf[lax.rem(chunk, 2), top // 2, row] = result.astype(jnp.bfloat16)

    def evaluate(chunk, e):
        j, g = e // groups, e % groups
        block = tbuf[chunk % 2, j, :, pl.ds(pl.multiple_of(g * PACK, PACK), PACK), :]
        found = jnp.dot(
            block.reshape(2 * GROUP * PACK, NLOW), weights[e], preferred_element_type=jnp.float32
        )
        total = found[:PACK] * signs[e, 0:1, :]
        for n in range(1, 2 * GROUP):
            total += found[n * PACK : (n + 1) * PACK] * signs[e, n : n + 1, :]
        acc[e] += total * signs[e, 2 * GROUP + chunk : 2 * GROUP + chunk + 1, :]

    def evaluate_round(chunk, n):
        if pairs >= rounds:
            for m in range(pairs // rounds):
                evaluate(chunk, n * (pairs // rounds) + m)
        else:
            pl.when(n < pairs)(lambda: evaluate(chunk, n))

    turns = STEP * TOP
    per_chunk = GROUP // STEP

    grad_copies(0, lambda copy: copy.wait())

    @pl.loop(0, turns)
    def _(u):
        prepare(0, u)

    for step in range(steps):
        if step + SLOTS < steps:
            grad_copies(step + SLOTS, lambda copy: copy.start())
        if step + 1 < steps:
            grad_copies(step + 1, lambda copy: copy.wait())

        @pl.loop(0, turns)
        def _(u):
            if step >= per_chunk:
                evaluate_round(step // per_chunk - 1, step % per_chunk * turns + u)
            transform_high(step, u)
            if step + 1 < steps:
                prepare(step + 1, u)

    @pl.loop(0, pairs)
    def _(e):
        evaluate(chunks - 1, e)
        own = iota((PACK, points), 1) // 2 % PACK == iota((PACK, points), 0)
        found_rows[e // groups, pl.ds(e % groups, 1), :] = jnp.sum(
            jnp.where(own, acc[e], 0.0), axis=0, keepdims=True
        )

    place = place_ref[0]
    shares = []
    for hi in range(high_parts):
        common = jnp.bitwise_and(place, hi)
        odd = jnp.bitwise_and(common ^ (common >> 1) ^ (common >> 2) ^ (common >> 3), 1)
        sign = jnp.where(odd == 1, -scale, scale)
        part, first = divmod(hi * 2 * PACK, LANES)
        spot = first + lane // TOP * 2 + lane % 2
        line = jnp.zeros((groups, LANES), jnp.float32)
        for j in range(HALVED):
            rows = found_rows[j, :, part * LANES : (part + 1) * LANES]
            taken = jnp.take_along_axis(rows, spot, axis=1, mode="promise_in_bounds")
            line = jnp.where(lane % TOP // 2 == j, taken, line)
        shares.append(line * sign)
    out_ref[...] = jnp.concatenate(shares, axis=0).astype(out_ref.dtype)


def partial_sketch(gradients, sign_words, sub_index, place, high_dev, scale):
    kept = sub_index.shape[0]
    rest = NMID // TOP
    groups = high_dev // PACK
    points = kept // (HALVED * groups)
    grads = gradients.reshape(high_dev, TOP, rest // STEP, 1, ROWS * LANES)
    words = sign_words.reshape(-1, LANES)
    return pl.pallas_call(
        functools.partial(sketch_kernel, high_dev=high_dev, scale=scale),
        out_shape=jax.ShapeDtypeStruct((kept // LANES, LANES), jnp.bfloat16),
        in_specs=[
            pl.BlockSpec(memory_space=pltpu.SMEM),
            pl.BlockSpec(memory_space=pl.ANY),
            pl.BlockSpec(memory_space=pl.ANY),
            pl.BlockSpec(memory_space=pltpu.VMEM),
        ],
        out_specs=pl.BlockSpec(memory_space=pltpu.VMEM),
        scratch_shapes=[
            pltpu.VMEM((SLOTS, high_dev, 1, TOP * ROWS * LANES), jnp.bfloat16),
            pltpu.VMEM(words.shape, jnp.int32),
            pltpu.VMEM((rest // GROUP, TOP // 2, high_dev, LANES), jnp.int32),
            pltpu.VMEM((high_dev, high_dev), jnp.bfloat16),
            pltpu.VMEM((2, TOP, ROWS * (high_dev + 1), LANES), jnp.float32),
            pltpu.VMEM((2, HALVED, 2 * GROUP, high_dev, NLOW), jnp.bfloat16),
            pltpu.VMEM((HALVED, groups, points), jnp.int32),
            pltpu.VMEM((HALVED * groups, NLOW, points), jnp.bfloat16),
            pltpu.VMEM((HALVED * groups, 24, points), jnp.float32),
            pltpu.VMEM((HALVED * groups, PACK, points), jnp.float32),
            pltpu.VMEM((HALVED, groups, points), jnp.float32),
            pltpu.SemaphoreType.DMA((SLOTS, TOP)),
            pltpu.SemaphoreType.DMA,
        ],
        compiler_params=pltpu.CompilerParams(vmem_limit_bytes=62 * 1024 * 1024),
        name="sketch",
    )(place, grads, words, sub_index.reshape(kept // LANES, LANES))


def swapped(value, axis, size, bit):
    return lax.ppermute(value, axis, [(i, i ^ bit) for i in range(size)])


def on_device(gradients, sign_words, sub_index, test_sketch, *, feat_size, ex_size):
    local_features = gradients.shape[1]
    kept = sub_index.shape[0]
    tests = test_sketch.shape[0]
    high_dev = local_features // (NMID * NLOW)
    feature_scale = float(local_features * feat_size) ** (-0.5)
    score_scale = float(kept) ** (-0.5)
    ex_bits = [1 << b for b in range(ex_size.bit_length() - 1)]
    place = lax.axis_index("feat").astype(jnp.int32).reshape(1)
    shares = partial_sketch(gradients, sign_words, sub_index, place, high_dev, feature_scale)
    for bit in ex_bits:
        shares = jnp.concatenate([shares, swapped(shares, "ex", ex_size, bit)], axis=0)
    shares = shares.reshape(ex_size, kept)
    scores = jnp.einsum("ek,tk->et", shares, test_sketch, preferred_element_type=jnp.float32)
    for bit in ex_bits:
        split = scores.reshape(-1, 2, bit, tests)
        scores = jnp.stack([split[:, 0], swapped(split[:, 1], "ex", ex_size, bit)], axis=1)
    scores = scores.reshape(ex_size, tests)
    for b in range(feat_size.bit_length() - 1):
        scores = scores + swapped(scores, "feat", feat_size, 1 << b)
    scores = scores * score_scale
    own = lax.axis_index("ex")
    for bit in ex_bits:
        split = scores.reshape(-1, 2, bit, tests)
        scores = jnp.where(jnp.bitwise_and(own, bit) != 0, split[:, ::-1], split)
    return scores.reshape(1, ex_size * tests)


def solution(mesh):
    return jax.shard_map(
        functools.partial(on_device, feat_size=mesh.shape["feat"], ex_size=mesh.shape["ex"]),
        mesh=mesh,
        in_specs=(P("ex", "feat"), P("feat"), P(), P("ex", None)),
        out_specs=P("ex", None),
        check_vma=False,
    )
```

time: 130 us -> 121 us (0.931)
  starting transfers between devices: 25.5 us -> 16.8 us
  Pallas kernels: 90.7 us -> 84.3 us
  waiting for transfers between devices: 8.81 us -> 14.1 us
  other arithmetic: 0.61 us -> 2.81 us
    ppermute x17 -> x8, starting transfers between devices: 25.5 us -> 16.8 us  [swapped(): return lax.ppermute(value, axis, [(i, i ^ bit) for i in range(size)])]
    pallas_call x1, Pallas kernels: 90.7 us -> 84.3 us  [partial_sketch(): pl.pallas_call(functools.partial(sketch_kernel, high_dev=high_dev, scale=...]
    ppermute x17 -> x8, waiting for transfers between devices: 8.81 us -> 14.1 us  [swapped(): return lax.ppermute(value, axis, [(i, i ^ bit) for i in range(size)])]
    concatenate x1 -> x3, other arithmetic: 0.6 us -> 2.17 us  [on_device(): jnp.concatenate([shares, swapped(shares, 'ex', ex_size, bit)], axis=0)]
  transfers between devices with their start and end apart: 17 -> 8, of which waited for: 7 -> 8; matrix products, arithmetic and copies ran while one was open for 1% -> 0% of each run, Pallas kernels for 0% -> 0%
where the time goes in v3:
time: 121 us; the launch traced here: 120 us
  Pallas kernels  84.3 us (70%)
  starting transfers between devices  16.8 us (14%)
  waiting for transfers between devices  14.1 us (12%)
  other arithmetic  2.81 us (2%)
  matrix products  2.29 us (2%)
    pallas_call x1, Pallas kernels, partial_sketch(): pl.pallas_call(functools.partial(sketch_kernel, high_dev=high_dev, scale=...  84.3 us
    ppermute x8, starting transfers between devices, swapped(): return lax.ppermute(value, axis, [(i, i ^ bit) for i in range(size)])  16.8 us
    ppermute x8, waiting for transfers between devices, swapped(): return lax.ppermute(value, axis, [(i, i ^ bit) for i in range(size)])  14.1 us
  transfers between devices with their start and end apart: 8, of which 8 were waited for; matrix products, arithmetic and copies ran while one was open for 0% of the time, Pallas kernels for 0%

profile of v3, /device:TPU:0, one launch (start us, length us, event | category | flops | bytes accessed | tf_op | source)
XLA Modules:
  0.0 120.5 jit_solution(8873308240937201401)
XLA Ops:
  0.0 84.3 %sketch.1 = bf16[64,128]{1,0:T(8,128)(2,1)} custom-call(s32[1]{0:T(128)} %bitcast.place_ref, bf16[256,8,8,1,1024]{4,3,2,1,0:T(2,128)(2,1)} %bitcast.1.grads, s32[8192,128]{1,0:T(8,128)} %bitcast.30, s32[64,128]{1,0:T(8,128)} %bitcast.33), custom_call_target="tpu_custom_call" | custom-call | tf_op jit(solution)/shard_map/sketch/pallas_call | solution.py:218
  84.3 3.0 %collective-permute-start = (bf16[64,128]{1,0:T(8,128)(2,1)}, bf16[64,128]{1,0:T(8,128)(2,1)S(1)}, u32[]{:S(2)}, u32[]{:S(2)}) collective-permute-start(bf16[64,128]{1,0:T(8,128)(2,1)} %sketch.1), channel_id=1, source_target_pairs={{0,1},{1,0},{2,3},{3,2},{4,5},{5,4},{6,7},{7,6},{8,9},{9,8},{10,11... | collective-permute-start | bytes 49160 | tf_op jit(solution)/shard_map/ppermute | solution.py:249
  87.4 1.9 %collective-permute-done = bf16[64,128]{1,0:T(8,128)(2,1)S(1)} collective-permute-done((bf16[64,128]{1,0:T(8,128)(2,1)}, bf16[64,128]{1,0:T(8,128)(2,1)S(1)}, u32[]{:S(2)}, u32[]{:S(2)}) %collective-permute-start) | collective-permute-done | bytes 16416 | tf_op jit(solution)/shard_map/ppermute | solution.py:249
  89.3 0.7 pad_maximum_fusion.2
  90.0 2.1 %collective-permute-start.1 = (bf16[128,128]{1,0:T(8,128)(2,1)S(1)}, bf16[128,128]{1,0:T(8,128)(2,1)S(1)}, u32[]{:S(2)}, u32[]{:S(2)}) collective-permute-start(bf16[128,128]{1,0:T(8,128)(2,1)S(1)} %pad_maximum_fusion.2), channel_id=1, source_target_pairs={{0,2},{1,3},{2,0},{3,1},{4,6},{5,7},{6,4},{7,5},{8,10},{9,11},{10,... | collective-permute-start | bytes 98312 | tf_op jit(solution)/shard_map/ppermute | solution.py:249
  92.1 1.9 %collective-permute-done.1 = bf16[128,128]{1,0:T(8,128)(2,1)S(1)} collective-permute-done((bf16[128,128]{1,0:T(8,128)(2,1)S(1)}, bf16[128,128]{1,0:T(8,128)(2,1)S(1)}, u32[]{:S(2)}, u32[]{:S(2)}) %collective-permute-start.1) | collective-permute-done | bytes 32800 | tf_op jit(solution)/shard_map/ppermute | solution.py:249
  94.0 0.7 pad_maximum_fusion.1
  94.7 3.0 %collective-permute-start.2 = (bf16[256,128]{1,0:T(8,128)(2,1)S(1)}, bf16[256,128]{1,0:T(8,128)(2,1)S(1)}, u32[]{:S(2)}, u32[]{:S(2)}) collective-permute-start(bf16[256,128]{1,0:T(8,128)(2,1)S(1)} %pad_maximum_fusion.1), channel_id=1, source_target_pairs={{0,4},{1,5},{2,6},{3,7},{4,0},{5,1},{6,2},{7,3},{8,12},{9,13},{10,... | collective-permute-start | bytes 196616 | tf_op jit(solution)/shard_map/ppermute | solution.py:249
  97.8 2.2 %collective-permute-done.2 = bf16[256,128]{1,0:T(8,128)(2,1)S(1)} collective-permute-done((bf16[256,128]{1,0:T(8,128)(2,1)S(1)}, bf16[256,128]{1,0:T(8,128)(2,1)S(1)}, u32[]{:S(2)}, u32[]{:S(2)}) %collective-permute-start.2) | collective-permute-done | bytes 65568 | tf_op jit(solution)/shard_map/ppermute | solution.py:249
  100.0 0.7 pad_maximum_fusion
  100.8 2.3 %fusion = f32[4,2,128]{2,1,0:T(2,128)S(1)} fusion(bf16[4,2,8192]{2,1,0:T(2,128)(2,1)S(1)} %dot_general.7, bf16[128,8192]{1,0:T(8,128)(2,1)} %param.7), kind=kOutput, calls=%fused_computation | convolution fusion | flops 16777216 | bytes 2232320 | tf_op jit(solution)/shard_map/ek,tk->et/dot_general | solution.py:265
  103.1 1.9 %collective-permute-start.3 = (f32[4,1,128]{2,0,1:T(4,128)S(1)}, f32[4,1,128]{2,0,1:T(4,128)S(1)}, u32[]{:S(2)}, u32[]{:S(2)}) collective-permute-start(f32[4,1,128]{2,0,1:T(4,128)S(1)} %get-tuple-element.10), channel_id=1, source_target_pairs={{0,1},{1,0},{2,3},{3,2},{4,5},{5,4},{6,7},{7,6},{8,9},{9,8},{10,11... | collective-permute-start | bytes 6152 | tf_op jit(solution)/shard_map/ppermute | solution.py:249
  105.0 1.8 %collective-permute-done.3 = f32[4,1,128]{2,0,1:T(4,128)S(1)} collective-permute-done((f32[4,1,128]{2,0,1:T(4,128)S(1)}, f32[4,1,128]{2,0,1:T(4,128)S(1)}, u32[]{:S(2)}, u32[]{:S(2)}) %collective-permute-start.3) | collective-permute-done | bytes 2080 | tf_op jit(solution)/shard_map/ppermute | solution.py:249
  106.7 1.9 %collective-permute-start.4 = (f32[2,2,128]{2,0,1:T(2,128)S(1)}, f32[2,2,128]{2,0,1:T(2,128)S(1)}, u32[]{:S(2)}, u32[]{:S(2)}) collective-permute-start(f32[2,2,128]{2,0,1:T(2,128)S(1)} %bitcast.45), channel_id=1, source_target_pairs={{0,2},{1,3},{2,0},{3,1},{4,6},{5,7},{6,4},{7,5},{8,10},{9,11},{10,... | collective-permute-start | bytes 6152 | tf_op jit(solution)/shard_map/ppermute | solution.py:249
  108.7 1.7 %collective-permute-done.4 = f32[2,2,128]{2,0,1:T(2,128)S(1)} collective-permute-done((f32[2,2,128]{2,0,1:T(2,128)S(1)}, f32[2,2,128]{2,0,1:T(2,128)S(1)}, u32[]{:S(2)}, u32[]{:S(2)}) %collective-permute-start.4) | collective-permute-done | bytes 2080 | tf_op jit(solution)/shard_map/ppermute | solution.py:249
  110.3 3.1 %collective-permute-start.5 = (f32[1,4,128]{2,1,0:T(4,128)S(1)}, f32[1,4,128]{2,1,0:T(4,128)S(1)}, u32[]{:S(2)}, u32[]{:S(2)}) collective-permute-start(f32[1,4,128]{2,1,0:T(4,128)S(1)} %bitcast.47), channel_id=1, source_target_pairs={{0,4},{1,5},{2,6},{3,7},{4,0},{5,1},{6,2},{7,3},{8,12},{9,13},{10,... | collective-permute-start | bytes 6152 | tf_op jit(solution)/shard_map/ppermute | solution.py:249
  113.5 1.6 %collective-permute-done.5 = f32[1,4,128]{2,1,0:T(4,128)S(1)} collective-permute-done((f32[1,4,128]{2,1,0:T(4,128)S(1)}, f32[1,4,128]{2,1,0:T(4,128)S(1)}, u32[]{:S(2)}, u32[]{:S(2)}) %collective-permute-start.5) | collective-permute-done | bytes 2080 | tf_op jit(solution)/shard_map/ppermute | solution.py:249
  115.0 0.0 collective-permute-start.6
  115.0 1.2 collective-permute-done.6
  116.2 1.7 %collective-permute-start.7 = (f32[8,128]{1,0:T(8,128)S(1)}, f32[8,128]{1,0:T(8,128)S(1)}, u32[]{:S(2)}, u32[]{:S(2)}) collective-permute-start(f32[8,128]{1,0:T(8,128)S(1)} %add.6), channel_id=1, source_target_pairs={{0,16},{8,24},{16,0},{24,8},{1,17},{9,25},{17,1},{25,9},{2,18},{10... | collective-permute-start | bytes 12296 | tf_op jit(solution)/shard_map/ppermute | solution.py:249
  117.9 1.9 %collective-permute-done.7 = f32[8,128]{1,0:T(8,128)S(1)} collective-permute-done((f32[8,128]{1,0:T(8,128)S(1)}, f32[8,128]{1,0:T(8,128)S(1)}, u32[]{:S(2)}, u32[]{:S(2)}) %collective-permute-start.7) | collective-permute-done | bytes 4128 | tf_op jit(solution)/shard_map/ppermute | solution.py:249
  119.9 0.6 reverse_select_fusion
  (12 shorter events, 0.1 us)
Async XLA Ops:
  84.3 4.9 %collective-permute-start = (bf16[64,128]{1,0:T(8,128)(2,1)}, bf16[64,128]{1,0:T(8,128)(2,1)S(1)}, u32[]{:S(2)}, u32[]{:S(2)}) collective-permute-start(bf16[64,128]{1,0:T(8,128)(2,1)} %sketch.1), channel_id=1, source_target_pairs={{0,1},{1,0},{2,3},{3,2},{4,5},{5,4},{6,7},{7,6},{8,9},{9,8},{10,11... | collective-permute-start | bytes 49160 | tf_op jit(solution)/shard_map/ppermute | solution.py:249
  90.0 4.0 %collective-permute-start.1 = (bf16[128,128]{1,0:T(8,128)(2,1)S(1)}, bf16[128,128]{1,0:T(8,128)(2,1)S(1)}, u32[]{:S(2)}, u32[]{:S(2)}) collective-permute-start(bf16[128,128]{1,0:T(8,128)(2,1)S(1)} %pad_maximum_fusion.2), channel_id=1, source_target_pairs={{0,2},{1,3},{2,0},{3,1},{4,6},{5,7},{6,4},{7,5},{8,10},{9,11},{10,... | collective-permute-start | bytes 98312 | tf_op jit(solution)/shard_map/ppermute | solution.py:249
  94.7 5.3 %collective-permute-start.2 = (bf16[256,128]{1,0:T(8,128)(2,1)S(1)}, bf16[256,128]{1,0:T(8,128)(2,1)S(1)}, u32[]{:S(2)}, u32[]{:S(2)}) collective-permute-start(bf16[256,128]{1,0:T(8,128)(2,1)S(1)} %pad_maximum_fusion.1), channel_id=1, source_target_pairs={{0,4},{1,5},{2,6},{3,7},{4,0},{5,1},{6,2},{7,3},{8,12},{9,13},{10,... | collective-permute-start | bytes 196616 | tf_op jit(solution)/shard_map/ppermute | solution.py:249
  103.1 3.7 %collective-permute-start.3 = (f32[4,1,128]{2,0,1:T(4,128)S(1)}, f32[4,1,128]{2,0,1:T(4,128)S(1)}, u32[]{:S(2)}, u32[]{:S(2)}) collective-permute-start(f32[4,1,128]{2,0,1:T(4,128)S(1)} %get-tuple-element.10), channel_id=1, source_target_pairs={{0,1},{1,0},{2,3},{3,2},{4,5},{5,4},{6,7},{7,6},{8,9},{9,8},{10,11... | collective-permute-start | bytes 6152 | tf_op jit(solution)/shard_map/ppermute | solution.py:249
  106.7 3.6 %collective-permute-start.4 = (f32[2,2,128]{2,0,1:T(2,128)S(1)}, f32[2,2,128]{2,0,1:T(2,128)S(1)}, u32[]{:S(2)}, u32[]{:S(2)}) collective-permute-start(f32[2,2,128]{2,0,1:T(2,128)S(1)} %bitcast.45), channel_id=1, source_target_pairs={{0,2},{1,3},{2,0},{3,1},{4,6},{5,7},{6,4},{7,5},{8,10},{9,11},{10,... | collective-permute-start | bytes 6152 | tf_op jit(solution)/shard_map/ppermute | solution.py:249
  110.3 4.7 %collective-permute-start.5 = (f32[1,4,128]{2,1,0:T(4,128)S(1)}, f32[1,4,128]{2,1,0:T(4,128)S(1)}, u32[]{:S(2)}, u32[]{:S(2)}) collective-permute-start(f32[1,4,128]{2,1,0:T(4,128)S(1)} %bitcast.47), channel_id=1, source_target_pairs={{0,4},{1,5},{2,6},{3,7},{4,0},{5,1},{6,2},{7,3},{8,12},{9,13},{10,... | collective-permute-start | bytes 6152 | tf_op jit(solution)/shard_map/ppermute | solution.py:249
  115.0 1.2 collective-permute-start.6
  116.2 3.6 %collective-permute-start.7 = (f32[8,128]{1,0:T(8,128)S(1)}, f32[8,128]{1,0:T(8,128)S(1)}, u32[]{:S(2)}, u32[]{:S(2)}) collective-permute-start(f32[8,128]{1,0:T(8,128)S(1)} %add.6), channel_id=1, source_target_pairs={{0,16},{8,24},{16,0},{24,8},{1,17},{9,25},{17,1},{25,9},{2,18},{10... | collective-permute-start | bytes 12296 | tf_op jit(solution)/shard_map/ppermute | solution.py:249

commit v4 on v3

--- a/solution.py
+++ b/solution.py
@@ -17,6 +17,7 @@
 HALVED = TOP // 2
 LANES = 128
 PACK = 16
+PAIR = 2
 
 
 def odd_common_bits(left, right):
@@ -29,7 +30,7 @@
 
 def sketch_kernel(
     place_ref, grads, words, sub_ref, out_ref,
-    xbuf, wbuf, wpair, table, ybuf, tbuf, entries, weights, signs, acc, found_rows, sems, wsem,
+    xbuf, wbuf, wpair, table, ybuf0, ybuf1, tbuf0, tbuf1, entries, weights, signs, acc, found_rows, sems, wsem,
     *, high_dev, scale,
 ):
     high_parts = out_ref.shape[0] * LANES // TOP // high_dev
@@ -39,13 +40,15 @@
     groups = high_dev // PACK
     points = entries.shape[2]
     pairs = HALVED * groups
-    rounds = GROUP * TOP
-    highs = high_dev // (STEP * TOP)
+    rounds = GROUP * TOP // PAIR
+    highs = high_dev * PAIR // (STEP * TOP)
     half = LANES // 16
     stride = high_dev + 1
+    ybuf = (ybuf0, ybuf1)
+    tbuf = (tbuf0, tbuf1)
 
     def grad_copies(step, then):
-        slot = lax.rem(step, SLOTS)
+        slot = step % SLOTS
         for top in range(TOP):
             copy = pltpu.make_async_copy(
                 grads.at[:, top, step],
@@ -103,11 +106,11 @@
                 )
 
     def prepare(step, u):
-        slot = lax.rem(step, SLOTS)
+        slot = step % SLOTS
         chunk = step * STEP // GROUP
         lane8 = iota((ROWS, LANES), 1)
         bits = [jnp.left_shift(1, lane8 % 16), jnp.left_shift(1, lane8 % 16 + 16)]
-        spot = lax.rem(step, GROUP // STEP) * (16 * STEP) + iota((ROWS, LANES), 0) * half + lane8 // 16
+        spot = step % (GROUP // STEP) * (16 * STEP) + iota((ROWS, LANES), 0) * half + lane8 // 16
         for n in range(highs):
             h = u * highs + n
             values = []
@@ -127,24 +130,27 @@
                         nxt[at + reach] = values[at] - values[at + reach]
                 values = nxt
             for top in range(TOP):
-                ybuf[lax.rem(step, 2), top, pl.ds(h, ROWS, stride), :] = values[top]
+                ybuf[step % 2][top, pl.ds(h, ROWS, stride), :] = values[top]
 
     def transform_high(step, u):
-        top, i = u % TOP, u // TOP
+        first, i = u * PAIR % TOP, u * PAIR // TOP
         columns = [
-            ybuf[lax.rem(step, 2), top, pl.ds((2 * i + l_hi) * stride, high_dev), :].astype(jnp.bfloat16)
+            ybuf[step % 2][first + n, pl.ds((2 * i + l_hi) * stride, high_dev), :].astype(jnp.bfloat16)
+            for n in range(PAIR)
             for l_hi in range(2)
         ]
         result = jnp.dot(
             table[...], jnp.concatenate(columns, axis=1), preferred_element_type=jnp.float32
-        )
+        ).astype(jnp.bfloat16)
         chunk = step * STEP // GROUP
-        row = (top % 2) * GROUP + lax.rem(step, GROUP // STEP) * STEP + i
-        tbuf[lax.rem(chunk, 2), top // 2, row] = result.astype(jnp.bfloat16)
+        row = step % (GROUP // STEP) * STEP + i
+        for n in range(PAIR):
+            top = first + n
+            tbuf[chunk % 2][top // 2, n % 2 * GROUP + row] = result[:, n * NLOW : (n + 1) * NLOW]
 
     def evaluate(chunk, e):
         j, g = e // groups, e % groups
-        block = tbuf[chunk % 2, j, :, pl.ds(pl.multiple_of(g * PACK, PACK), PACK), :]
+        block = tbuf[chunk % 2][j, :, pl.ds(pl.multiple_of(g * PACK, PACK), PACK), :]
         found = jnp.dot(
             block.reshape(2 * GROUP * PACK, NLOW), weights[e], preferred_element_type=jnp.float32
         )
@@ -160,7 +166,7 @@
         else:
             pl.when(n < pairs)(lambda: evaluate(chunk, n))
 
-    turns = STEP * TOP
+    turns = STEP * TOP // PAIR
     per_chunk = GROUP // STEP
 
     grad_copies(0, lambda copy: copy.wait())
@@ -230,8 +236,10 @@
             pltpu.VMEM(words.shape, jnp.int32),
             pltpu.VMEM((rest // GROUP, TOP // 2, high_dev, LANES), jnp.int32),
             pltpu.VMEM((high_dev, high_dev), jnp.bfloat16),
-            pltpu.VMEM((2, TOP, ROWS * (high_dev + 1), LANES), jnp.float32),
-            pltpu.VMEM((2, HALVED, 2 * GROUP, high_dev, NLOW), jnp.bfloat16),
+            pltpu.VMEM((TOP, ROWS * (high_dev + 1), LANES), jnp.float32),
+            pltpu.VMEM((TOP, ROWS * (high_dev + 1), LANES), jnp.float32),
+            pltpu.VMEM((HALVED, 2 * GROUP, high_dev, NLOW), jnp.bfloat16),
+            pltpu.VMEM((HALVED, 2 * GROUP, high_dev, NLOW), jnp.bfloat16),
             pltpu.VMEM((HALVED, groups, points), jnp.int32),
             pltpu.VMEM((HALVED * groups, NLOW, points), jnp.bfloat16),
             pltpu.VMEM((HALVED * groups, 24, points), jnp.float32),

time: 121 us -> 102 us (0.84)
  Pallas kernels: 84.3 us -> 65.6 us
    pallas_call x1, Pallas kernels: 84.3 us -> 65.6 us  [partial_sketch(): pl.pallas_call(functools.partial(sketch_kernel, high_dev=high_dev, scale=...]
where the time goes in v4:
time: 102 us
  Pallas kernels  65.6 us (64%)
  starting transfers between devices  16.8 us (16%)
  waiting for transfers between devices  14.1 us (14%)
  other arithmetic  2.81 us (3%)
  matrix products  2.29 us (2%)
    pallas_call x1, Pallas kernels, partial_sketch(): pl.pallas_call(functools.partial(sketch_kernel, high_dev=high_dev, scale=...  65.6 us
    ppermute x8, starting transfers between devices, swapped(): return lax.ppermute(value, axis, [(i, i ^ bit) for i in range(size)])  16.8 us
    ppermute x8, waiting for transfers between devices, swapped(): return lax.ppermute(value, axis, [(i, i ^ bit) for i in range(size)])  14.1 us
    dot_general x1, matrix products, on_device(): jnp.einsum('ek,tk->et', shares, test_sketch, preferred_element_type=jnp.f...  2.29 us
    concatenate x3, other arithmetic, on_device(): jnp.concatenate([shares, swapped(shares, 'ex', ex_size, bit)], axis=0)  2.17 us
  transfers between devices with their start and end apart: 8, of which 8 were waited for; matrix products, arithmetic and copies ran while one was open for 0% of the time, Pallas kernels for 0%

profile of v4, /device:TPU:0, one launch (start us, length us, event | category | flops | bytes accessed | tf_op | source)
XLA Modules:
  0.0 101.8 jit_solution(6993668713203779883)
XLA Ops:
  0.0 65.6 %sketch.1 = bf16[64,128]{1,0:T(8,128)(2,1)} custom-call(s32[1]{0:T(128)} %bitcast.place_ref, bf16[256,8,8,1,1024]{4,3,2,1,0:T(2,128)(2,1)} %bitcast.1.grads, s32[8192,128]{1,0:T(8,128)} %bitcast.30, s32[64,128]{1,0:T(8,128)} %bitcast.33), custom_call_target="tpu_custom_call" | custom-call | tf_op jit(solution)/shard_map/sketch/pallas_call | solution.py:224
  65.6 3.0 %collective-permute-start = (bf16[64,128]{1,0:T(8,128)(2,1)}, bf16[64,128]{1,0:T(8,128)(2,1)S(1)}, u32[]{:S(2)}, u32[]{:S(2)}) collective-permute-start(bf16[64,128]{1,0:T(8,128)(2,1)} %sketch.1), channel_id=1, source_target_pairs={{0,1},{1,0},{2,3},{3,2},{4,5},{5,4},{6,7},{7,6},{8,9},{9,8},{10,11... | collective-permute-start | bytes 49160 | tf_op jit(solution)/shard_map/ppermute | solution.py:257
  68.6 1.9 %collective-permute-done = bf16[64,128]{1,0:T(8,128)(2,1)S(1)} collective-permute-done((bf16[64,128]{1,0:T(8,128)(2,1)}, bf16[64,128]{1,0:T(8,128)(2,1)S(1)}, u32[]{:S(2)}, u32[]{:S(2)}) %collective-permute-start) | collective-permute-done | bytes 16416 | tf_op jit(solution)/shard_map/ppermute | solution.py:257
  70.6 0.7 pad_maximum_fusion.2
  71.3 2.1 %collective-permute-start.1 = (bf16[128,128]{1,0:T(8,128)(2,1)S(1)}, bf16[128,128]{1,0:T(8,128)(2,1)S(1)}, u32[]{:S(2)}, u32[]{:S(2)}) collective-permute-start(bf16[128,128]{1,0:T(8,128)(2,1)S(1)} %pad_maximum_fusion.2), channel_id=1, source_target_pairs={{0,2},{1,3},{2,0},{3,1},{4,6},{5,7},{6,4},{7,5},{8,10},{9,11},{10,... | collective-permute-start | bytes 98312 | tf_op jit(solution)/shard_map/ppermute | solution.py:257
  73.4 1.9 %collective-permute-done.1 = bf16[128,128]{1,0:T(8,128)(2,1)S(1)} collective-permute-done((bf16[128,128]{1,0:T(8,128)(2,1)S(1)}, bf16[128,128]{1,0:T(8,128)(2,1)S(1)}, u32[]{:S(2)}, u32[]{:S(2)}) %collective-permute-start.1) | collective-permute-done | bytes 32800 | tf_op jit(solution)/shard_map/ppermute | solution.py:257
  75.3 0.7 pad_maximum_fusion.1
  76.0 3.0 %collective-permute-start.2 = (bf16[256,128]{1,0:T(8,128)(2,1)S(1)}, bf16[256,128]{1,0:T(8,128)(2,1)S(1)}, u32[]{:S(2)}, u32[]{:S(2)}) collective-permute-start(bf16[256,128]{1,0:T(8,128)(2,1)S(1)} %pad_maximum_fusion.1), channel_id=1, source_target_pairs={{0,4},{1,5},{2,6},{3,7},{4,0},{5,1},{6,2},{7,3},{8,12},{9,13},{10,... | collective-permute-start | bytes 196616 | tf_op jit(solution)/shard_map/ppermute | solution.py:257
  79.0 2.2 %collective-permute-done.2 = bf16[256,128]{1,0:T(8,128)(2,1)S(1)} collective-permute-done((bf16[256,128]{1,0:T(8,128)(2,1)S(1)}, bf16[256,128]{1,0:T(8,128)(2,1)S(1)}, u32[]{:S(2)}, u32[]{:S(2)}) %collective-permute-start.2) | collective-permute-done | bytes 65568 | tf_op jit(solution)/shard_map/ppermute | solution.py:257
  81.3 0.7 pad_maximum_fusion
  82.0 2.3 %fusion = f32[4,2,128]{2,1,0:T(2,128)S(1)} fusion(bf16[4,2,8192]{2,1,0:T(2,128)(2,1)S(1)} %dot_general.7, bf16[128,8192]{1,0:T(8,128)(2,1)} %param.7), kind=kOutput, calls=%fused_computation | convolution fusion | flops 16777216 | bytes 2232320 | tf_op jit(solution)/shard_map/ek,tk->et/dot_general | solution.py:273
  84.4 1.9 %collective-permute-start.3 = (f32[4,1,128]{2,0,1:T(4,128)S(1)}, f32[4,1,128]{2,0,1:T(4,128)S(1)}, u32[]{:S(2)}, u32[]{:S(2)}) collective-permute-start(f32[4,1,128]{2,0,1:T(4,128)S(1)} %get-tuple-element.10), channel_id=1, source_target_pairs={{0,1},{1,0},{2,3},{3,2},{4,5},{5,4},{6,7},{7,6},{8,9},{9,8},{10,11... | collective-permute-start | bytes 6152 | tf_op jit(solution)/shard_map/ppermute | solution.py:257
  86.3 1.8 %collective-permute-done.3 = f32[4,1,128]{2,0,1:T(4,128)S(1)} collective-permute-done((f32[4,1,128]{2,0,1:T(4,128)S(1)}, f32[4,1,128]{2,0,1:T(4,128)S(1)}, u32[]{:S(2)}, u32[]{:S(2)}) %collective-permute-start.3) | collective-permute-done | bytes 2080 | tf_op jit(solution)/shard_map/ppermute | solution.py:257
  88.0 1.9 %collective-permute-start.4 = (f32[2,2,128]{2,0,1:T(2,128)S(1)}, f32[2,2,128]{2,0,1:T(2,128)S(1)}, u32[]{:S(2)}, u32[]{:S(2)}) collective-permute-start(f32[2,2,128]{2,0,1:T(2,128)S(1)} %bitcast.45), channel_id=1, source_target_pairs={{0,2},{1,3},{2,0},{3,1},{4,6},{5,7},{6,4},{7,5},{8,10},{9,11},{10,... | collective-permute-start | bytes 6152 | tf_op jit(solution)/shard_map/ppermute | solution.py:257
  89.9 1.7 %collective-permute-done.4 = f32[2,2,128]{2,0,1:T(2,128)S(1)} collective-permute-done((f32[2,2,128]{2,0,1:T(2,128)S(1)}, f32[2,2,128]{2,0,1:T(2,128)S(1)}, u32[]{:S(2)}, u32[]{:S(2)}) %collective-permute-start.4) | collective-permute-done | bytes 2080 | tf_op jit(solution)/shard_map/ppermute | solution.py:257
  91.6 3.1 %collective-permute-start.5 = (f32[1,4,128]{2,1,0:T(4,128)S(1)}, f32[1,4,128]{2,1,0:T(4,128)S(1)}, u32[]{:S(2)}, u32[]{:S(2)}) collective-permute-start(f32[1,4,128]{2,1,0:T(4,128)S(1)} %bitcast.47), channel_id=1, source_target_pairs={{0,4},{1,5},{2,6},{3,7},{4,0},{5,1},{6,2},{7,3},{8,12},{9,13},{10,... | collective-permute-start | bytes 6152 | tf_op jit(solution)/shard_map/ppermute | solution.py:257
  94.7 1.6 %collective-permute-done.5 = f32[1,4,128]{2,1,0:T(4,128)S(1)} collective-permute-done((f32[1,4,128]{2,1,0:T(4,128)S(1)}, f32[1,4,128]{2,1,0:T(4,128)S(1)}, u32[]{:S(2)}, u32[]{:S(2)}) %collective-permute-start.5) | collective-permute-done | bytes 2080 | tf_op jit(solution)/shard_map/ppermute | solution.py:257
  96.3 0.0 collective-permute-start.6
  96.3 1.2 %collective-permute-done.6 = f32[8,128]{1,0:T(8,128)S(1)} collective-permute-done((f32[8,128]{1,0:T(8,128)S(1)}, f32[8,128]{1,0:T(8,128)S(1)}, u32[]{:S(2)}, u32[]{:S(2)}) %collective-permute-start.6) | collective-permute-done | bytes 4128 | tf_op jit(solution)/shard_map/ppermute | solution.py:257
  97.5 1.7 %collective-permute-start.7 = (f32[8,128]{1,0:T(8,128)S(1)}, f32[8,128]{1,0:T(8,128)S(1)}, u32[]{:S(2)}, u32[]{:S(2)}) collective-permute-start(f32[8,128]{1,0:T(8,128)S(1)} %add.6), channel_id=1, source_target_pairs={{0,16},{8,24},{16,0},{24,8},{1,17},{9,25},{17,1},{25,9},{2,18},{10... | collective-permute-start | bytes 12296 | tf_op jit(solution)/shard_map/ppermute | solution.py:257
  99.2 1.9 %collective-permute-done.7 = f32[8,128]{1,0:T(8,128)S(1)} collective-permute-done((f32[8,128]{1,0:T(8,128)S(1)}, f32[8,128]{1,0:T(8,128)S(1)}, u32[]{:S(2)}, u32[]{:S(2)}) %collective-permute-start.7) | collective-permute-done | bytes 4128 | tf_op jit(solution)/shard_map/ppermute | solution.py:257
  101.2 0.6 reverse_select_fusion
  (12 shorter events, 0.1 us)
Async XLA Ops:
  65.6 4.9 %collective-permute-start = (bf16[64,128]{1,0:T(8,128)(2,1)}, bf16[64,128]{1,0:T(8,128)(2,1)S(1)}, u32[]{:S(2)}, u32[]{:S(2)}) collective-permute-start(bf16[64,128]{1,0:T(8,128)(2,1)} %sketch.1), channel_id=1, source_target_pairs={{0,1},{1,0},{2,3},{3,2},{4,5},{5,4},{6,7},{7,6},{8,9},{9,8},{10,11... | collective-permute-start | bytes 49160 | tf_op jit(solution)/shard_map/ppermute | solution.py:257
  71.3 4.0 %collective-permute-start.1 = (bf16[128,128]{1,0:T(8,128)(2,1)S(1)}, bf16[128,128]{1,0:T(8,128)(2,1)S(1)}, u32[]{:S(2)}, u32[]{:S(2)}) collective-permute-start(bf16[128,128]{1,0:T(8,128)(2,1)S(1)} %pad_maximum_fusion.2), channel_id=1, source_target_pairs={{0,2},{1,3},{2,0},{3,1},{4,6},{5,7},{6,4},{7,5},{8,10},{9,11},{10,... | collective-permute-start | bytes 98312 | tf_op jit(solution)/shard_map/ppermute | solution.py:257
  76.0 5.3 %collective-permute-start.2 = (bf16[256,128]{1,0:T(8,128)(2,1)S(1)}, bf16[256,128]{1,0:T(8,128)(2,1)S(1)}, u32[]{:S(2)}, u32[]{:S(2)}) collective-permute-start(bf16[256,128]{1,0:T(8,128)(2,1)S(1)} %pad_maximum_fusion.1), channel_id=1, source_target_pairs={{0,4},{1,5},{2,6},{3,7},{4,0},{5,1},{6,2},{7,3},{8,12},{9,13},{10,... | collective-permute-start | bytes 196616 | tf_op jit(solution)/shard_map/ppermute | solution.py:257
  84.4 3.7 %collective-permute-start.3 = (f32[4,1,128]{2,0,1:T(4,128)S(1)}, f32[4,1,128]{2,0,1:T(4,128)S(1)}, u32[]{:S(2)}, u32[]{:S(2)}) collective-permute-start(f32[4,1,128]{2,0,1:T(4,128)S(1)} %get-tuple-element.10), channel_id=1, source_target_pairs={{0,1},{1,0},{2,3},{3,2},{4,5},{5,4},{6,7},{7,6},{8,9},{9,8},{10,11... | collective-permute-start | bytes 6152 | tf_op jit(solution)/shard_map/ppermute | solution.py:257
  88.0 3.6 %collective-permute-start.4 = (f32[2,2,128]{2,0,1:T(2,128)S(1)}, f32[2,2,128]{2,0,1:T(2,128)S(1)}, u32[]{:S(2)}, u32[]{:S(2)}) collective-permute-start(f32[2,2,128]{2,0,1:T(2,128)S(1)} %bitcast.45), channel_id=1, source_target_pairs={{0,2},{1,3},{2,0},{3,1},{4,6},{5,7},{6,4},{7,5},{8,10},{9,11},{10,... | collective-permute-start | bytes 6152 | tf_op jit(solution)/shard_map/ppermute | solution.py:257
  91.6 4.7 %collective-permute-start.5 = (f32[1,4,128]{2,1,0:T(4,128)S(1)}, f32[1,4,128]{2,1,0:T(4,128)S(1)}, u32[]{:S(2)}, u32[]{:S(2)}) collective-permute-start(f32[1,4,128]{2,1,0:T(4,128)S(1)} %bitcast.47), channel_id=1, source_target_pairs={{0,4},{1,5},{2,6},{3,7},{4,0},{5,1},{6,2},{7,3},{8,12},{9,13},{10,... | collective-permute-start | bytes 6152 | tf_op jit(solution)/shard_map/ppermute | solution.py:257
  96.3 1.2 %collective-permute-start.6 = (f32[8,128]{1,0:T(8,128)S(1)}, f32[8,128]{1,0:T(8,128)S(1)}, u32[]{:S(2)}, u32[]{:S(2)}) collective-permute-start(f32[8,128]{1,0:T(8,128)S(1)} %bitcast.34), channel_id=1, source_target_pairs={{0,8},{8,0},{16,24},{24,16},{1,9},{9,1},{17,25},{25,17},{2,10},{10... | collective-permute-start | bytes 12296 | tf_op jit(solution)/shard_map/ppermute | solution.py:257
  97.5 3.6 %collective-permute-start.7 = (f32[8,128]{1,0:T(8,128)S(1)}, f32[8,128]{1,0:T(8,128)S(1)}, u32[]{:S(2)}, u32[]{:S(2)}) collective-permute-start(f32[8,128]{1,0:T(8,128)S(1)} %add.6), channel_id=1, source_target_pairs={{0,16},{8,24},{16,0},{24,8},{1,17},{9,25},{17,1},{25,9},{2,18},{10... | collective-permute-start | bytes 12296 | tf_op jit(solution)/shard_map/ppermute | solution.py:257

commit v5 on v4

--- a/solution.py
+++ b/solution.py
@@ -5,7 +5,7 @@
 from jax import lax
 from jax.experimental import pallas as pl
 from jax.experimental.pallas import tpu as pltpu
-from jax.sharding import PartitionSpec as P
+from jax.sharding import Mesh, PartitionSpec as P
 
 NMID = 256
 NLOW = 256
@@ -17,7 +17,7 @@
 HALVED = TOP // 2
 LANES = 128
 PACK = 16
-PAIR = 2
+PAIR = 4
 
 
 def odd_common_bits(left, right):
@@ -33,7 +33,7 @@
     xbuf, wbuf, wpair, table, ybuf0, ybuf1, tbuf0, tbuf1, entries, weights, signs, acc, found_rows, sems, wsem,
     *, high_dev, scale,
 ):
-    high_parts = out_ref.shape[0] * LANES // TOP // high_dev
+    high_parts = out_ref.shape[0]
     rest = NMID // TOP
     chunks = rest // GROUP
     steps = rest // STEP
@@ -78,8 +78,7 @@
                 line = jnp.where(lane // (2 * PACK) == n, taken, line)
             entries[j, :, part * LANES : (part + 1) * LANES] = line
 
-    @pl.loop(0, pairs)
-    def _(e):
+    def build(e):
         entry = entries[e // groups, pl.ds(e % groups, 1), :]
         row = iota((24, points), 0)
         mask = jnp.where(
@@ -159,12 +158,12 @@
             total += found[n * PACK : (n + 1) * PACK] * signs[e, n : n + 1, :]
         acc[e] += total * signs[e, 2 * GROUP + chunk : 2 * GROUP + chunk + 1, :]
 
-    def evaluate_round(chunk, n):
+    def some_pairs(n, do):
         if pairs >= rounds:
             for m in range(pairs // rounds):
-                evaluate(chunk, n * (pairs // rounds) + m)
+                do(n * (pairs // rounds) + m)
         else:
-            pl.when(n < pairs)(lambda: evaluate(chunk, n))
+            pl.when(n < pairs)(lambda: do(n))
 
     turns = STEP * TOP // PAIR
     per_chunk = GROUP // STEP
@@ -184,7 +183,9 @@
         @pl.loop(0, turns)
         def _(u):
             if step >= per_chunk:
-                evaluate_round(step // per_chunk - 1, step % per_chunk * turns + u)
+                some_pairs(step % per_chunk * turns + u, functools.partial(evaluate, step // per_chunk - 1))
+            else:
+                some_pairs(step * turns + u, build)
             transform_high(step, u)
             if step + 1 < steps:
                 prepare(step + 1, u)
@@ -198,7 +199,6 @@
         )
 
     place = place_ref[0]
-    shares = []
     for hi in range(high_parts):
         common = jnp.bitwise_and(place, hi)
         odd = jnp.bitwise_and(common ^ (common >> 1) ^ (common >> 2) ^ (common >> 3), 1)
@@ -210,8 +210,7 @@
             rows = found_rows[j, :, part * LANES : (part + 1) * LANES]
             taken = jnp.take_along_axis(rows, spot, axis=1, mode="promise_in_bounds")
             line = jnp.where(lane % TOP // 2 == j, taken, line)
-        shares.append(line * sign)
-    out_ref[...] = jnp.concatenate(shares, axis=0).astype(out_ref.dtype)
+        out_ref[jnp.bitwise_xor(hi, place)] = line * sign
 
 
 def partial_sketch(gradients, sign_words, sub_index, place, high_dev, scale):
@@ -223,7 +222,7 @@
     words = sign_words.reshape(-1, LANES)
     return pl.pallas_call(
         functools.partial(sketch_kernel, high_dev=high_dev, scale=scale),
-        out_shape=jax.ShapeDtypeStruct((kept // LANES, LANES), jnp.bfloat16),
+        out_shape=jax.ShapeDtypeStruct((kept // TOP // high_dev, groups, LANES), jnp.float32),
         in_specs=[
             pl.BlockSpec(memory_space=pltpu.SMEM),
             pl.BlockSpec(memory_space=pl.ANY),
@@ -253,43 +252,55 @@
     )(place, grads, words, sub_index.reshape(kept // LANES, LANES))
 
 
-def swapped(value, axis, size, bit):
-    return lax.ppermute(value, axis, [(i, i ^ bit) for i in range(size)])
-
-
-def on_device(gradients, sign_words, sub_index, test_sketch, *, feat_size, ex_size):
+def swapped(value, axis, size, bits):
+    return lax.ppermute(value, axis, [(i, i ^ bits) for i in range(size)])
+
+
+def on_device(gradients, sign_words, sub_index, test_sketch, *, mesh):
+    feat_size, far_size, near_size = (mesh.shape[axis] for axis in ("feat", "far", "near"))
     local_features = gradients.shape[1]
     kept = sub_index.shape[0]
     tests = test_sketch.shape[0]
     high_dev = local_features // (NMID * NLOW)
     feature_scale = float(local_features * feat_size) ** (-0.5)
     score_scale = float(kept) ** (-0.5)
-    ex_bits = [1 << b for b in range(ex_size.bit_length() - 1)]
-    place = lax.axis_index("feat").astype(jnp.int32).reshape(1)
-    shares = partial_sketch(gradients, sign_words, sub_index, place, high_dev, feature_scale)
-    for bit in ex_bits:
-        shares = jnp.concatenate([shares, swapped(shares, "ex", ex_size, bit)], axis=0)
-    shares = shares.reshape(ex_size, kept)
-    scores = jnp.einsum("ek,tk->et", shares, test_sketch, preferred_element_type=jnp.float32)
-    for bit in ex_bits:
-        split = scores.reshape(-1, 2, bit, tests)
-        scores = jnp.stack([split[:, 0], swapped(split[:, 1], "ex", ex_size, bit)], axis=1)
-    scores = scores.reshape(ex_size, tests)
-    for b in range(feat_size.bit_length() - 1):
-        scores = scores + swapped(scores, "feat", feat_size, 1 << b)
-    scores = scores * score_scale
-    own = lax.axis_index("ex")
-    for bit in ex_bits:
-        split = scores.reshape(-1, 2, bit, tests)
-        scores = jnp.where(jnp.bitwise_and(own, bit) != 0, split[:, ::-1], split)
-    return scores.reshape(1, ex_size * tests)
+    place = lax.axis_index("feat").astype(jnp.int32)
+    own_kept = kept // feat_size
+    own_tests = lax.dynamic_slice_in_dim(test_sketch, place * own_kept, own_kept, axis=1)
+    own_tests = lax.all_gather(own_tests, "far", axis=0, tiled=True)
+    shares = partial_sketch(gradients, sign_words, sub_index, place.reshape(1), high_dev, feature_scale)
+    sketch = shares[0]
+    for s in range(1, feat_size):
+        sketch = sketch + swapped(shares[s], "feat", feat_size, s)
+    sketch = sketch.astype(jnp.bfloat16).reshape(1, own_kept)
+    sketches = [sketch] + [swapped(sketch, "near", near_size, s) for s in range(1, near_size)]
+    scores = jnp.einsum(
+        "ek,tk->et", jnp.concatenate(sketches, axis=0), own_tests, preferred_element_type=jnp.float32
+    )
+    scores = jnp.stack(
+        [scores[0]] + [swapped(scores[s], "near", near_size, s) for s in range(1, near_size)]
+    )
+    total = scores
+    for s in range(1, feat_size):
+        total = total + swapped(scores, "feat", feat_size, s)
+    total = (total * score_scale).reshape(near_size, far_size, tests)
+    own = lax.axis_index("near")
+    for b in range(near_size.bit_length() - 1):
+        split = total.reshape(-1, 2, 1 << b, far_size, tests)
+        total = jnp.where(jnp.bitwise_and(own, 1 << b) != 0, split[:, ::-1], split)
+    total = total.reshape(near_size, far_size, tests)
+    return jnp.swapaxes(total, 0, 1).reshape(1, -1)
 
 
 def solution(mesh):
+    feat_size, ex_size = mesh.shape["feat"], mesh.shape["ex"]
+    far_size = min(4, ex_size)
+    mesh = Mesh(mesh.devices.reshape(feat_size, far_size, ex_size // far_size), ("feat", "far", "near"))
+    ex = ("far", "near")
     return jax.shard_map(
-        functools.partial(on_device, feat_size=mesh.shape["feat"], ex_size=mesh.shape["ex"]),
+        functools.partial(on_device, mesh=mesh),
         mesh=mesh,
-        in_specs=(P("ex", "feat"), P("feat"), P(), P("ex", None)),
-        out_specs=P("ex", None),
+        in_specs=(P(ex, "feat"), P("feat"), P(), P(ex, None)),
+        out_specs=P(ex, None),
         check_vma=False,
     )

time: 102 us -> 98.4 us (0.965)
  between operations: 0.05 us -> 13.4 us
  starting transfers between devices: 16.8 us -> 8.09 us
  waiting for transfers between devices: 14.1 us -> 9.05 us
  Pallas kernels: 65.6 us -> 61.3 us
  local copies, waits for them, and re-layouts: 0.08 us -> 3.26 us
  other arithmetic: 2.81 us -> 0.73 us
    ppermute x8, starting transfers between devices: 16.8 us -> 8.09 us  [swapped(): return lax.ppermute(value, axis, [(i, i ^ bits) for i in range(size)])]
    ppermute x8, waiting for transfers between devices: 14.1 us -> 9.03 us  [swapped(): return lax.ppermute(value, axis, [(i, i ^ bits) for i in range(size)])]
    pallas_call x1, Pallas kernels: 65.6 us -> 61.3 us  [partial_sketch(): pl.pallas_call(functools.partial(sketch_kernel, high_dev=high_dev, scale=...]
    concatenate x3 -> x0, other arithmetic: 2.17 us -> none  [on_device(): jnp.concatenate([shares, swapped(shares, 'ex', ex_size, bit)], axis=0)]
    dynamic_slice x0 -> x1, local copies, waits for them, and re-layouts: none -> 1.9 us  [on_device(): lax.dynamic_slice_in_dim(test_sketch, place * own_kept, own_kept, axis=1)]
  transfers between devices with their start and end apart: 8 -> 9, of which waited for: 8 -> 6; matrix products, arithmetic and copies ran while one was open for 0% -> 1% of each run, Pallas kernels for 0% -> 62%
where the time goes in v5:
time: 98.4 us; the launch traced here: 98.1 us
  Pallas kernels  61.3 us (62%)
  between operations  13.4 us (14%)
  waiting for transfers between devices  9.05 us (9%)
  starting transfers between devices  8.09 us (8%)
  local copies, waits for them, and re-layouts  3.26 us (3%)
  matrix products  2.23 us (2%)
    pallas_call x1, Pallas kernels, partial_sketch(): pl.pallas_call(functools.partial(sketch_kernel, high_dev=high_dev, scale=...  61.3 us
    ppermute x8, waiting for transfers between devices, swapped(): return lax.ppermute(value, axis, [(i, i ^ bits) for i in range(size)])  9.03 us
    ppermute x8, starting transfers between devices, swapped(): return lax.ppermute(value, axis, [(i, i ^ bits) for i in range(size)])  8.09 us
    dot_general x1, matrix products, on_device(): jnp.einsum('ek,tk->et', jnp.concatenate(sketches, axis=0), own_tests, pre...  2.23 us
  transfers between devices with their start and end apart: 9, of which 6 were waited for; matrix products, arithmetic and copies ran while one was open for 1% of the time, Pallas kernels for 62%

profile of v5, /device:TPU:0, one launch (start us, length us, event | category | flops | bytes accessed | tf_op | source)
XLA Modules:
  0.0 98.1 jit_solution(2882846045006564170)
XLA Ops:
  6.5 0.0 all-gather.2.cloned.1.call-start
  6.5 1.9 %constant_dynamic-slice_fusion = bf16[128,2048]{1,0:T(8,128)(2,1)} fusion(bf16[128,8192]{1,0:T(8,128)(2,1)} %param.7, s32[]{:T(128)S(6)} %select_n.12), kind=kLoop, calls=%fused_computation.18 | loop fusion | bytes 1048580 | tf_op jit(solution)/shard_map/dynamic_slice | solution.py:269
  8.4 0.0 all-gather.2.cloned.1.call-update
  8.5 61.3 %sketch.1 = f32[4,16,128]{2,1,0:T(8,128)} custom-call(s32[1]{0:T(128)} %bitcast.place_ref, bf16[256,8,8,1,1024]{4,3,2,1,0:T(2,128)(2,1)} %bitcast.1.grads, s32[8192,128]{1,0:T(8,128)} %bitcast.36, s32[64,128]{1,0:T(8,128)} %bitcast.37), custom_call_target="tpu_custom_call" | custom-call | tf_op jit(solution)/shard_map/sketch/pallas_call | solution.py:223
  69.7 0.7 slice_bitcast_fusion.2
  70.5 2.4 %collective-permute-start.2 = (f32[16,128]{1,0:T(8,128)S(1)}, f32[16,128]{1,0:T(8,128)S(1)}, u32[]{:S(2)}, u32[]{:S(2)}) collective-permute-start(f32[16,128]{1,0:T(8,128)S(1)} %get-tuple-element.6), channel_id=1, source_target_pairs={{0,24},{8,16},{16,8},{24,0},{1,25},{9,17},{17,9},{25,1},{2,26},{10... | collective-permute-start | bytes 24584 | tf_op jit(solution)/shard_map/ppermute | solution.py:256
  72.9 0.6 collective-permute-start.1
  73.5 0.1 collective-permute-start
  73.6 0.7 collective-permute-done.2
  74.2 2.3 %collective-permute-done.1 = f32[16,128]{1,0:T(8,128)S(1)} collective-permute-done((f32[16,128]{1,0:T(8,128)S(1)}, f32[16,128]{1,0:T(8,128)S(1)}, u32[]{:S(2)}, u32[]{:S(2)}) %collective-permute-start.1) | collective-permute-done | bytes 8224 | tf_op jit(solution)/shard_map/ppermute | solution.py:256
  76.5 0.0 collective-permute-done
  76.5 0.7 fusion.9
  77.2 1.6 %collective-permute-start.3 = (bf16[1,2048]{1,0:T(2,128)(2,1)S(1)}, bf16[1,2048]{1,0:T(2,128)(2,1)S(1)}, u32[]{:S(2)}, u32[]{:S(2)}) collective-permute-start(bf16[1,2048]{1,0:T(2,128)(2,1)S(1)} %bitcast.38), channel_id=1, source_target_pairs={{0,1},{1,0},{2,3},{3,2},{4,5},{5,4},{6,7},{7,6},{8,9},{9,8},{10,11... | collective-permute-start | bytes 12296 | tf_op jit(solution)/shard_map/ppermute | solution.py:256
  78.8 2.2 %collective-permute-done.3 = bf16[1,2048]{1,0:T(2,128)(2,1)S(1)} collective-permute-done((bf16[1,2048]{1,0:T(2,128)(2,1)S(1)}, bf16[1,2048]{1,0:T(2,128)(2,1)S(1)}, u32[]{:S(2)}, u32[]{:S(2)}) %collective-permute-start.3) | collective-permute-done | bytes 4128 | tf_op jit(solution)/shard_map/ppermute | solution.py:256
  81.0 0.0 all-gather.2.cloned.1.call-done
  81.0 2.2 %fusion.4 = f32[2,512]{1,0:T(2,128)S(1)} fusion(bf16[512,2048]{1,0:T(8,128)(2,1)} %all-gather.2.cloned.1.call-done, bf16[1,2048]{1,0:T(2,128)(2,1)S(1)} %collective-permute-done.3, bf16[1,2048]{1,0:T(2,128)(2,1)S(1)} %bitcast.39), kind=kOutput, calls=%fused_computation.9 | convolution fusion | flops 4210688 | bytes 2109440 | tf_op jit(solution)/shard_map/ek,tk->et/dot_general | solution.py:277
  83.2 1.5 %collective-permute-start.4 = (f32[512]{0:T(512)S(1)}, f32[512]{0:T(512)S(1)}, u32[]{:S(2)}, u32[]{:S(2)}) collective-permute-start(f32[512]{0:T(512)S(1)} %bitcast.42), channel_id=1, source_target_pairs={{0,1},{1,0},{2,3},{3,2},{4,5},{5,4},{6,7},{7,6},{8,9},{9,8},{10,11... | collective-permute-start | bytes 6152 | tf_op jit(solution)/shard_map/ppermute | solution.py:256
  84.7 2.1 %collective-permute-done.4 = f32[512]{0:T(512)S(1)} collective-permute-done((f32[512]{0:T(512)S(1)}, f32[512]{0:T(512)S(1)}, u32[]{:S(2)}, u32[]{:S(2)}) %collective-permute-start.4) | collective-permute-done | bytes 2080 | tf_op jit(solution)/shard_map/ppermute | solution.py:256
  86.8 0.1 collective-permute-start.7
  86.9 0.7 collective-permute-start.6
  87.6 1.2 %collective-permute-start.5 = (f32[2,512]{1,0:T(2,128)S(1)}, f32[2,512]{1,0:T(2,128)S(1)}, u32[]{:S(2)}, u32[]{:S(2)}) collective-permute-start(f32[2,512]{1,0:T(2,128)S(1)} %pad_maximum_fusion), channel_id=1, source_target_pairs={{0,8},{8,0},{16,24},{24,16},{1,9},{9,1},{17,25},{25,17},{2,10},{10... | collective-permute-start | bytes 12296 | tf_op jit(solution)/shard_map/ppermute | solution.py:256
  88.7 1.2 %collective-permute-done.7 = f32[2,512]{1,0:T(2,128)S(1)} collective-permute-done((f32[2,512]{1,0:T(2,128)S(1)}, f32[2,512]{1,0:T(2,128)S(1)}, u32[]{:S(2)}, u32[]{:S(2)}) %collective-permute-start.7) | collective-permute-done | bytes 4128 | tf_op jit(solution)/shard_map/ppermute | solution.py:256
  89.9 0.7 collective-permute-done.6
  90.6 0.0 collective-permute-done.5
  90.6 0.6 copy.5
  (6 shorter events, 0.1 us)
Async XLA Ops:
  6.5 74.4 %all-gather.2.cloned.1.call-start = ((), (), s32[]{:S(2)}) async-start(), calls=%async_computation | async-start | bytes 2621440 | tf_op jit(solution)/shard_map/all_gather | solution.py:270
  70.5 3.8 %collective-permute-start.2 = (f32[16,128]{1,0:T(8,128)S(1)}, f32[16,128]{1,0:T(8,128)S(1)}, u32[]{:S(2)}, u32[]{:S(2)}) collective-permute-start(f32[16,128]{1,0:T(8,128)S(1)} %get-tuple-element.6), channel_id=1, source_target_pairs={{0,24},{8,16},{16,8},{24,0},{1,25},{9,17},{17,9},{25,1},{2,26},{10... | collective-permute-start | bytes 24584 | tf_op jit(solution)/shard_map/ppermute | solution.py:256
  72.9 3.7 %collective-permute-start.1 = (f32[16,128]{1,0:T(8,128)S(1)}, f32[16,128]{1,0:T(8,128)S(1)}, u32[]{:S(2)}, u32[]{:S(2)}) collective-permute-start(f32[16,128]{1,0:T(8,128)S(1)} %get-tuple-element.7), channel_id=1, source_target_pairs={{0,16},{8,24},{16,0},{24,8},{1,17},{9,25},{17,1},{25,9},{2,18},{10... | collective-permute-start | bytes 24584 | tf_op jit(solution)/shard_map/ppermute | solution.py:256
  73.5 3.1 %collective-permute-start = (f32[16,128]{1,0:T(8,128)S(1)}, f32[16,128]{1,0:T(8,128)S(1)}, u32[]{:S(2)}, u32[]{:S(2)}) collective-permute-start(f32[16,128]{1,0:T(8,128)S(1)} %get-tuple-element.5), channel_id=1, source_target_pairs={{0,8},{8,0},{16,24},{24,16},{1,9},{9,1},{17,25},{25,17},{2,10},{10... | collective-permute-start | bytes 24584 | tf_op jit(solution)/shard_map/ppermute | solution.py:256
  77.2 3.7 %collective-permute-start.3 = (bf16[1,2048]{1,0:T(2,128)(2,1)S(1)}, bf16[1,2048]{1,0:T(2,128)(2,1)S(1)}, u32[]{:S(2)}, u32[]{:S(2)}) collective-permute-start(bf16[1,2048]{1,0:T(2,128)(2,1)S(1)} %bitcast.38), channel_id=1, source_target_pairs={{0,1},{1,0},{2,3},{3,2},{4,5},{5,4},{6,7},{7,6},{8,9},{9,8},{10,11... | collective-permute-start | bytes 12296 | tf_op jit(solution)/shard_map/ppermute | solution.py:256
  83.2 3.6 %collective-permute-start.4 = (f32[512]{0:T(512)S(1)}, f32[512]{0:T(512)S(1)}, u32[]{:S(2)}, u32[]{:S(2)}) collective-permute-start(f32[512]{0:T(512)S(1)} %bitcast.42), channel_id=1, source_target_pairs={{0,1},{1,0},{2,3},{3,2},{4,5},{5,4},{6,7},{7,6},{8,9},{9,8},{10,11... | collective-permute-start | bytes 6152 | tf_op jit(solution)/shard_map/ppermute | solution.py:256
  86.8 3.1 %collective-permute-start.7 = (f32[2,512]{1,0:T(2,128)S(1)}, f32[2,512]{1,0:T(2,128)S(1)}, u32[]{:S(2)}, u32[]{:S(2)}) collective-permute-start(f32[2,512]{1,0:T(2,128)S(1)} %pad_maximum_fusion), channel_id=1, source_target_pairs={{0,24},{8,16},{16,8},{24,0},{1,25},{9,17},{17,9},{25,1},{2,26},{10... | collective-permute-start | bytes 12296 | tf_op jit(solution)/shard_map/ppermute | solution.py:256
  86.9 3.7 %collective-permute-start.6 = (f32[2,512]{1,0:T(2,128)S(1)}, f32[2,512]{1,0:T(2,128)S(1)}, u32[]{:S(2)}, u32[]{:S(2)}) collective-permute-start(f32[2,512]{1,0:T(2,128)S(1)} %pad_maximum_fusion), channel_id=1, source_target_pairs={{0,16},{8,24},{16,0},{24,8},{1,17},{9,25},{17,1},{25,9},{2,18},{10... | collective-permute-start | bytes 12296 | tf_op jit(solution)/shard_map/ppermute | solution.py:256
  87.6 3.0 %collective-permute-start.5 = (f32[2,512]{1,0:T(2,128)S(1)}, f32[2,512]{1,0:T(2,128)S(1)}, u32[]{:S(2)}, u32[]{:S(2)}) collective-permute-start(f32[2,512]{1,0:T(2,128)S(1)} %pad_maximum_fusion), channel_id=1, source_target_pairs={{0,8},{8,0},{16,24},{24,16},{1,9},{9,1},{17,25},{25,17},{2,10},{10... | collective-permute-start | bytes 12296 | tf_op jit(solution)/shard_map/ppermute | solution.py:256
Sparse Core Ops, SparseCore 0:
  8.9 48.6 all-gather.1

commit v6 on v5

--- a/solution.py
+++ b/solution.py
@@ -12,7 +12,7 @@
 TOP = 8
 GROUP = 8
 STEP = 4
-SLOTS = 2
+SLOTS = 3
 ROWS = 2 * STEP
 HALVED = TOP // 2
 LANES = 128
@@ -33,7 +33,7 @@
     xbuf, wbuf, wpair, table, ybuf0, ybuf1, tbuf0, tbuf1, entries, weights, signs, acc, found_rows, sems, wsem,
     *, high_dev, scale,
 ):
-    high_parts = out_ref.shape[0]
+    high_parts = out_ref.shape[0] * LANES // TOP // high_dev
     rest = NMID // TOP
     chunks = rest // GROUP
     steps = rest // STEP
@@ -41,26 +41,34 @@
     points = entries.shape[2]
     pairs = HALVED * groups
     rounds = GROUP * TOP // PAIR
-    highs = high_dev * PAIR // (STEP * TOP)
+    turns = STEP * TOP // PAIR
+    per_chunk = GROUP // STEP
+    blocks = STEP * high_dev // PACK // turns
     half = LANES // 16
-    stride = high_dev + 1
     ybuf = (ybuf0, ybuf1)
     tbuf = (tbuf0, tbuf1)
 
-    def grad_copies(step, then):
+    def grad_copy(step, h):
+        return pltpu.make_async_copy(
+            grads.at[h, :, pl.ds(step * ROWS, ROWS)],
+            xbuf.at[step % SLOTS, :, :, :, pl.ds(pl.multiple_of(h * LANES, LANES), LANES)],
+            sems.at[step % SLOTS],
+        )
+
+    def start_copies(step):
+        @pl.loop(0, high_dev // 8)
+        def _(n):
+            for i in range(8):
+                grad_copy(step, n * 8 + i).start()
+
+    def wait_copies(step):
         slot = step % SLOTS
-        for top in range(TOP):
-            copy = pltpu.make_async_copy(
-                grads.at[:, top, step],
-                xbuf.at[slot, :, :, top * ROWS * LANES : (top + 1) * ROWS * LANES],
-                sems.at[slot, top],
-            )
-            then(copy)
+        pltpu.make_async_copy(xbuf.at[slot], xbuf.at[slot], sems.at[slot]).wait()
 
     word_copy = pltpu.make_async_copy(words, wbuf, wsem)
     word_copy.start()
-    for step in range(SLOTS):
-        grad_copies(step, lambda copy: copy.start())
+    start_copies(0)
+    start_copies(1)
 
     table[...] = jnp.where(
         odd_common_bits(iota(table.shape, 0), iota(table.shape, 1)), -1.0, 1.0
@@ -107,37 +115,38 @@
     def prepare(step, u):
         slot = step % SLOTS
         chunk = step * STEP // GROUP
-        lane8 = iota((ROWS, LANES), 1)
-        bits = [jnp.left_shift(1, lane8 % 16), jnp.left_shift(1, lane8 % 16 + 16)]
-        spot = step % (GROUP // STEP) * (16 * STEP) + iota((ROWS, LANES), 0) * half + lane8 // 16
-        for n in range(highs):
-            h = u * highs + n
-            values = []
-            for pair in range(TOP // 2):
-                word = jnp.broadcast_to(wpair[chunk, pair, pl.ds(h, 1), :], (ROWS, LANES))
-                word = jnp.take_along_axis(word, spot, axis=1, mode="promise_in_bounds")
-                two = xbuf[slot, h, :, 2 * pair * ROWS * LANES : 2 * (pair + 1) * ROWS * LANES]
-                two = two.reshape(2 * ROWS, LANES).astype(jnp.float32)
-                for which in range(2):
-                    value = two[which * ROWS : (which + 1) * ROWS]
-                    values.append(jnp.where(jnp.bitwise_and(word, bits[which]) != 0, value, -value))
-            for reach in (2, 4):
-                nxt = list(values)
-                for at in range(TOP):
-                    if not at & reach:
-                        nxt[at] = values[at] + values[at + reach]
-                        nxt[at + reach] = values[at] - values[at + reach]
-                values = nxt
-            for top in range(TOP):
-                ybuf[step % 2][top, pl.ds(h, ROWS, stride), :] = values[top]
+        lane16 = iota((PACK, LANES), 1)
+        bits = [jnp.left_shift(1, lane16 % 16), jnp.left_shift(1, lane16 % 16 + 16)]
+        i = u * STEP // turns
+        for n in range(blocks):
+            block = (u * blocks + n) % (high_dev // PACK)
+            rows = pl.ds(pl.multiple_of(block * PACK, PACK), PACK)
+            columns = pl.ds(pl.multiple_of(block * (PACK * LANES), PACK * LANES), PACK * LANES)
+            packed = [wpair[chunk, pair, rows, :] for pair in range(TOP // 2)]
+            for l_hi in range(2):
+                spot = (step % (GROUP // STEP) * STEP + i) * 16 + l_hi * half + lane16 // 16
+                values = []
+                for pair in range(TOP // 2):
+                    word = jnp.take_along_axis(packed[pair], spot, axis=1, mode="promise_in_bounds")
+                    for which in range(2):
+                        value = xbuf[slot, 2 * pair + which, 2 * i + l_hi, :, columns]
+                        value = value.reshape(PACK, LANES).astype(jnp.float32)
+                        values.append(jnp.where(jnp.bitwise_and(word, bits[which]) != 0, value, -value))
+                for reach in (2, 4):
+                    nxt = list(values)
+                    for at in range(TOP):
+                        if not at & reach:
+                            nxt[at] = values[at] + values[at + reach]
+                            nxt[at + reach] = values[at] - values[at + reach]
+                    values = nxt
+                for top in range(TOP):
+                    ybuf[step % 2][top, i, rows, l_hi * LANES : (l_hi + 1) * LANES] = values[top].astype(
+                        jnp.bfloat16
+                    )
 
     def transform_high(step, u):
         first, i = u * PAIR % TOP, u * PAIR // TOP
-        columns = [
-            ybuf[step % 2][first + n, pl.ds((2 * i + l_hi) * stride, high_dev), :].astype(jnp.bfloat16)
-            for n in range(PAIR)
-            for l_hi in range(2)
-        ]
+        columns = [ybuf[step % 2][first + n, i] for n in range(PAIR)]
         result = jnp.dot(
             table[...], jnp.concatenate(columns, axis=1), preferred_element_type=jnp.float32
         ).astype(jnp.bfloat16)
@@ -165,23 +174,23 @@
         else:
             pl.when(n < pairs)(lambda: do(n))
 
-    turns = STEP * TOP // PAIR
-    per_chunk = GROUP // STEP
-
-    grad_copies(0, lambda copy: copy.wait())
+
+    wait_copies(0)
+    start_copies(2)
 
     @pl.loop(0, turns)
     def _(u):
         prepare(0, u)
 
     for step in range(steps):
-        if step + SLOTS < steps:
-            grad_copies(step + SLOTS, lambda copy: copy.start())
         if step + 1 < steps:
-            grad_copies(step + 1, lambda copy: copy.wait())
+            wait_copies(step + 1)
 
         @pl.loop(0, turns)
         def _(u):
+            if step + SLOTS < steps:
+                for n in range(high_dev // turns):
+                    grad_copy(step + SLOTS, u * (high_dev // turns) + n).start()
             if step >= per_chunk:
                 some_pairs(step % per_chunk * turns + u, functools.partial(evaluate, step // per_chunk - 1))
             else:
@@ -210,7 +219,7 @@
             rows = found_rows[j, :, part * LANES : (part + 1) * LANES]
             taken = jnp.take_along_axis(rows, spot, axis=1, mode="promise_in_bounds")
             line = jnp.where(lane % TOP // 2 == j, taken, line)
-        out_ref[jnp.bitwise_xor(hi, place)] = line * sign
+        out_ref[hi * groups : (hi + 1) * groups, :] = line * sign
 
 
 def partial_sketch(gradients, sign_words, sub_index, place, high_dev, scale):
@@ -218,11 +227,11 @@
     rest = NMID // TOP
     groups = high_dev // PACK
     points = kept // (HALVED * groups)
-    grads = gradients.reshape(high_dev, TOP, rest // STEP, 1, ROWS * LANES)
+    grads = gradients.reshape(high_dev, TOP, 2 * rest, 1, LANES)
     words = sign_words.reshape(-1, LANES)
     return pl.pallas_call(
         functools.partial(sketch_kernel, high_dev=high_dev, scale=scale),
-        out_shape=jax.ShapeDtypeStruct((kept // TOP // high_dev, groups, LANES), jnp.float32),
+        out_shape=jax.ShapeDtypeStruct((kept // LANES, LANES), jnp.float32),
         in_specs=[
             pl.BlockSpec(memory_space=pltpu.SMEM),
             pl.BlockSpec(memory_space=pl.ANY),
@@ -231,12 +240,12 @@
         ],
         out_specs=pl.BlockSpec(memory_space=pltpu.VMEM),
         scratch_shapes=[
-            pltpu.VMEM((SLOTS, high_dev, 1, TOP * ROWS * LANES), jnp.bfloat16),
+            pltpu.VMEM((SLOTS, TOP, ROWS, 1, high_dev * LANES), jnp.bfloat16),
             pltpu.VMEM(words.shape, jnp.int32),
             pltpu.VMEM((rest // GROUP, TOP // 2, high_dev, LANES), jnp.int32),
             pltpu.VMEM((high_dev, high_dev), jnp.bfloat16),
-            pltpu.VMEM((TOP, ROWS * (high_dev + 1), LANES), jnp.float32),
-            pltpu.VMEM((TOP, ROWS * (high_dev + 1), LANES), jnp.float32),
+            pltpu.VMEM((TOP, STEP, high_dev, NLOW), jnp.bfloat16),
+            pltpu.VMEM((TOP, STEP, high_dev, NLOW), jnp.bfloat16),
             pltpu.VMEM((HALVED, 2 * GROUP, high_dev, NLOW), jnp.bfloat16),
             pltpu.VMEM((HALVED, 2 * GROUP, high_dev, NLOW), jnp.bfloat16),
             pltpu.VMEM((HALVED, groups, points), jnp.int32),
@@ -244,16 +253,46 @@
             pltpu.VMEM((HALVED * groups, 24, points), jnp.float32),
             pltpu.VMEM((HALVED * groups, PACK, points), jnp.float32),
             pltpu.VMEM((HALVED, groups, points), jnp.float32),
-            pltpu.SemaphoreType.DMA((SLOTS, TOP)),
+            pltpu.SemaphoreType.DMA((SLOTS,)),
             pltpu.SemaphoreType.DMA,
         ],
         compiler_params=pltpu.CompilerParams(vmem_limit_bytes=62 * 1024 * 1024),
+        cost_estimate=pl.CostEstimate(
+            flops=4 * NLOW * high_dev * NMID * NLOW, bytes_accessed=4 * gradients.size, transcendentals=0
+        ),
         name="sketch",
     )(place, grads, words, sub_index.reshape(kept // LANES, LANES))
 
 
 def swapped(value, axis, size, bits):
     return lax.ppermute(value, axis, [(i, i ^ bits) for i in range(size)])
+
+
+def score_kernel(*refs, scale):
+    *sketches, own_tests, near_tests, out_ref, lines = refs
+    for n, sketch in enumerate(sketches):
+        whole = sketch[...].astype(jnp.float32)
+        for row in range(whole.shape[0]):
+            lines[n : n + 1, row * LANES : (row + 1) * LANES] = whole[row : row + 1, :]
+    left = lines[...].astype(jnp.bfloat16)
+    for n, tests in enumerate([own_tests] + [near_tests.at[s] for s in range(near_tests.shape[0])]):
+        found = lax.dot_general(
+            left, tests[...], (((1,), (1,)), ((), ())), preferred_element_type=jnp.float32
+        )
+        found = found[: len(sketches)] * scale
+        out_ref[:, n * tests.shape[0] : (n + 1) * tests.shape[0]] = found
+
+
+def scores_of(sketches, own_tests, near_tests, scale):
+    tests, kept = own_tests.shape
+    count = len(sketches)
+    return pl.pallas_call(
+        functools.partial(score_kernel, scale=scale),
+        out_shape=jax.ShapeDtypeStruct((count, tests * (1 + near_tests.shape[0])), jnp.float32),
+        scratch_shapes=[pltpu.VMEM((16, kept), jnp.float32)],
+        compiler_params=pltpu.CompilerParams(vmem_limit_bytes=32 * 1024 * 1024),
+        name="scores",
+    )(*sketches, own_tests, near_tests)
 
 
 def on_device(gradients, sign_words, sub_index, test_sketch, *, mesh):
@@ -264,32 +303,27 @@
     high_dev = local_features // (NMID * NLOW)
     feature_scale = float(local_features * feat_size) ** (-0.5)
     score_scale = float(kept) ** (-0.5)
-    place = lax.axis_index("feat").astype(jnp.int32)
-    own_kept = kept // feat_size
-    own_tests = lax.dynamic_slice_in_dim(test_sketch, place * own_kept, own_kept, axis=1)
-    own_tests = lax.all_gather(own_tests, "far", axis=0, tiled=True)
-    shares = partial_sketch(gradients, sign_words, sub_index, place.reshape(1), high_dev, feature_scale)
-    sketch = shares[0]
+    place = lax.axis_index("feat").astype(jnp.int32).reshape(1)
+    near_tests = jnp.stack([swapped(test_sketch, "near", near_size, s) for s in range(1, near_size)])
+    shares = partial_sketch(gradients, sign_words, sub_index, place, high_dev, feature_scale)
+    sketch = shares
     for s in range(1, feat_size):
-        sketch = sketch + swapped(shares[s], "feat", feat_size, s)
-    sketch = sketch.astype(jnp.bfloat16).reshape(1, own_kept)
-    sketches = [sketch] + [swapped(sketch, "near", near_size, s) for s in range(1, near_size)]
-    scores = jnp.einsum(
-        "ek,tk->et", jnp.concatenate(sketches, axis=0), own_tests, preferred_element_type=jnp.float32
+        sketch = sketch + swapped(shares, "feat", feat_size, s)
+    sketch = sketch.astype(jnp.bfloat16)
+    sketches = [sketch] + [swapped(sketch, "far", far_size, s) for s in range(1, far_size)]
+    scores = scores_of(sketches, test_sketch, near_tests, score_scale)
+    scores = jnp.stack(
+        [scores[:1]] + [swapped(scores[s : s + 1], "far", far_size, s) for s in range(1, far_size)]
     )
-    scores = jnp.stack(
-        [scores[0]] + [swapped(scores[s], "near", near_size, s) for s in range(1, near_size)]
-    )
-    total = scores
-    for s in range(1, feat_size):
-        total = total + swapped(scores, "feat", feat_size, s)
-    total = (total * score_scale).reshape(near_size, far_size, tests)
-    own = lax.axis_index("near")
+    scores = scores.reshape(far_size, near_size, tests)
+    far, near = lax.axis_index("far"), lax.axis_index("near")
     for b in range(near_size.bit_length() - 1):
-        split = total.reshape(-1, 2, 1 << b, far_size, tests)
-        total = jnp.where(jnp.bitwise_and(own, 1 << b) != 0, split[:, ::-1], split)
-    total = total.reshape(near_size, far_size, tests)
-    return jnp.swapaxes(total, 0, 1).reshape(1, -1)
+        split = scores.reshape(far_size, -1, 2, 1 << b, tests)
+        scores = jnp.where(jnp.bitwise_and(near, 1 << b) != 0, split[:, :, ::-1], split)
+    for b in range(far_size.bit_length() - 1):
+        split = scores.reshape(-1, 2, 1 << b, near_size, tests)
+        scores = jnp.where(jnp.bitwise_and(far, 1 << b) != 0, split[:, ::-1], split)
+    return scores.reshape(1, -1)
 
 
 def solution(mesh):

time: 98.4 us -> 96 us (0.976)
  between operations: 13.4 us -> 0.05 us
  Pallas kernels: 61.3 us -> 68.5 us
  starting transfers between devices: 8.09 us -> 13.7 us
  matrix products: 2.23 us -> 0 us
  local copies, waits for them, and re-layouts: 3.26 us -> 1.63 us
  waiting for transfers between devices: 9.05 us -> 10.4 us
    ppermute x8 -> x10, starting transfers between devices: 8.09 us -> 13.7 us  [swapped(): return lax.ppermute(value, axis, [(i, i ^ bits) for i in range(size)])]
    pallas_call x1, Pallas kernels: 61.3 us -> 65.7 us  [partial_sketch(): pl.pallas_call(functools.partial(sketch_kernel, high_dev=high_dev, scale=...]
    pallas_call x0 -> x1, Pallas kernels: none -> 2.78 us  [scores_of(): pl.pallas_call(functools.partial(score_kernel, scale=scale), out_shape=ja...]
    dot_general x1 -> x0, matrix products: 2.23 us -> none  [on_device(): jnp.einsum('ek,tk->et', jnp.concatenate(sketches, axis=0), own_tests, pre...]
    dynamic_slice x1 -> x0, local copies, waits for them, and re-layouts: 1.9 us -> none  [on_device(): lax.dynamic_slice_in_dim(test_sketch, place * own_kept, own_kept, axis=1)]
    unnamed x1 -> x2, local copies, waits for them, and re-layouts: 0.01 us -> 1.59 us
    ppermute x8 -> x10, waiting for transfers between devices: 9.03 us -> 10.4 us  [swapped(): return lax.ppermute(value, axis, [(i, i ^ bits) for i in range(size)])]
  transfers between devices with their start and end apart: 9 -> 10, of which waited for: 6 -> 6; matrix products, arithmetic and copies ran while one was open for 1% -> 1% of each run, Pallas kernels for 62% -> 69%
where the time goes in v6:
time: 96 us; the launch traced here: 95.7 us
  Pallas kernels  68.5 us (71%)
  starting transfers between devices  13.7 us (14%)
  waiting for transfers between devices  10.4 us (11%)
  local copies, waits for them, and re-layouts  1.63 us (2%)
  other arithmetic  1.39 us (1%)
    pallas_call x1, Pallas kernels, partial_sketch(): pl.pallas_call(functools.partial(sketch_kernel, high_dev=high_dev, scale=...  65.7 us
    ppermute x10, starting transfers between devices, swapped(): return lax.ppermute(value, axis, [(i, i ^ bits) for i in range(size)])  13.7 us
    ppermute x10, waiting for transfers between devices, swapped(): return lax.ppermute(value, axis, [(i, i ^ bits) for i in range(size)])  10.4 us
    pallas_call x1, Pallas kernels, scores_of(): pl.pallas_call(functools.partial(score_kernel, scale=scale), out_shape=ja...  2.78 us
  transfers between devices with their start and end apart: 10, of which 6 were waited for; matrix products, arithmetic and copies ran while one was open for 1% of the time, Pallas kernels for 69%

profile of v6, /device:TPU:0, one launch (start us, length us, event | category | flops | bytes accessed | tf_op | source)
XLA Modules:
  0.0 95.7 jit_solution(13981511454228064828)
XLA Ops:
  0.0 2.9 %collective-permute-start.6 = (bf16[128,8192]{1,0:T(8,128)(2,1)}, bf16[128,8192]{1,0:T(8,128)(2,1)}, u32[]{:S(2)}, u32[]{:S(2)}) collective-permute-start(bf16[128,8192]{1,0:T(8,128)(2,1)} %refs_4_.1), channel_id=1, source_target_pairs={{0,1},{1,0},{2,3},{3,2},{4,5},{5,4},{6,7},{7,6},{8,9},{9,8},{10,11... | collective-permute-start | bytes 6291464 | tf_op jit(solution)/shard_map/ppermute | solution.py:268
  2.9 65.7 %sketch.1 = f32[64,128]{1,0:T(8,128)} custom-call(s32[1]{0:T(128)} %bitcast.place_ref, bf16[256,8,64,1,128]{4,3,2,1,0:T(2,128)(2,1)} %bitcast.1.grads, s32[8192,128]{1,0:T(8,128)} %bitcast.13, s32[64,128]{1,0:T(8,128)} %bitcast.14), custom_call_target="tpu_custom_call" | custom-call | flops 17179869184 | bytes 67108864 | tf_op jit(solution)/shard_map/sketch/pallas_call | solution.py:232
  68.6 0.1 collective-permute-start
  68.7 1.6 %collective-permute-start.1 = (f32[64,128]{1,0:T(8,128)}, f32[64,128]{1,0:T(8,128)S(1)}, u32[]{:S(2)}, u32[]{:S(2)}) collective-permute-start(f32[64,128]{1,0:T(8,128)} %sketch.1), channel_id=1, source_target_pairs={{0,16},{8,24},{16,0},{24,8},{1,17},{9,25},{17,1},{25,9},{2,18},{10... | collective-permute-start | bytes 98312 | tf_op jit(solution)/shard_map/ppermute | solution.py:268
  70.3 0.3 collective-permute-start.2
  70.6 0.0 collective-permute-done
  70.6 2.3 %collective-permute-done.1 = f32[64,128]{1,0:T(8,128)S(1)} collective-permute-done((f32[64,128]{1,0:T(8,128)}, f32[64,128]{1,0:T(8,128)S(1)}, u32[]{:S(2)}, u32[]{:S(2)}) %collective-permute-start.1) | collective-permute-done | bytes 32800 | tf_op jit(solution)/shard_map/ppermute | solution.py:268
  72.9 1.0 collective-permute-done.2
  73.9 0.8 add_convert_fusion.refs_0_
  74.6 1.6 %collective-permute-start.3 = (bf16[64,128]{1,0:T(8,128)(2,1)S(1)}, bf16[64,128]{1,0:T(8,128)(2,1)S(1)}, u32[]{:S(2)}, u32[]{:S(2)}) collective-permute-start(bf16[64,128]{1,0:T(8,128)(2,1)S(1)} %add_convert_fusion.refs_0_), channel_id=1, source_target_pairs={{0,2},{2,0},{4,6},{6,4},{1,3},{3,1},{5,7},{7,5},{8,10},{10,8},{12,... | collective-permute-start | bytes 49160 | tf_op jit(solution)/shard_map/ppermute | solution.py:268
  76.3 2.6 %collective-permute-start.4 = (bf16[64,128]{1,0:T(8,128)(2,1)S(1)}, bf16[64,128]{1,0:T(8,128)(2,1)S(1)}, u32[]{:S(2)}, u32[]{:S(2)}) collective-permute-start(bf16[64,128]{1,0:T(8,128)(2,1)S(1)} %add_convert_fusion.refs_0_), channel_id=1, source_target_pairs={{0,4},{2,6},{4,0},{6,2},{1,5},{3,7},{5,1},{7,3},{8,12},{10,14},{12... | collective-permute-start | bytes 49160 | tf_op jit(solution)/shard_map/ppermute | solution.py:268
  78.9 0.2 collective-permute-start.5
  79.1 0.0 collective-permute-done.3.refs_1_
  79.1 1.9 %collective-permute-done.4.refs_2_ = bf16[64,128]{1,0:T(8,128)(2,1)S(1)} collective-permute-done((bf16[64,128]{1,0:T(8,128)(2,1)S(1)}, bf16[64,128]{1,0:T(8,128)(2,1)S(1)}, u32[]{:S(2)}, u32[]{:S(2)}) %collective-permute-start.4) | collective-permute-done | bytes 16416 | tf_op jit(solution)/shard_map/ppermute | solution.py:268
  81.0 3.4 %collective-permute-done.5.refs_3_ = bf16[64,128]{1,0:T(8,128)(2,1)S(1)} collective-permute-done((bf16[64,128]{1,0:T(8,128)(2,1)S(1)}, bf16[64,128]{1,0:T(8,128)(2,1)S(1)}, u32[]{:S(2)}, u32[]{:S(2)}) %collective-permute-start.5) | collective-permute-done | bytes 16416 | tf_op jit(solution)/shard_map/ppermute | solution.py:268
  84.4 0.0 collective-permute-done.6
  84.4 0.0 copy-start
  84.4 1.6 %copy-done = bf16[128,8192]{1,0:T(8,128)(2,1)S(1)} copy-done((bf16[128,8192]{1,0:T(8,128)(2,1)S(1)}, bf16[128,8192]{1,0:T(8,128)(2,1)}, u32[]{:S(2)}) %copy-start) | copy-done | bytes 2097176
  86.0 2.8 %scores.1 = f32[4,256]{1,0:T(4,128)S(1)} custom-call(bf16[64,128]{1,0:T(8,128)(2,1)S(1)} %add_convert_fusion.refs_0_, bf16[64,128]{1,0:T(8,128)(2,1)S(1)} %collective-permute-done.3.refs_1_, bf16[64,128]{1,0:T(8,128)(2,1)S(1)} %collective-permute-done.4.refs_2_, bf16[64,128]{1,0:T(8,128)(2,1)S(1)} %collective-permute-done.5.refs_3_, ...), custom_call_target="tpu_custom_call" | custom-call | tf_op jit(solution)/shard_map/scores/pallas_call | solution.py:289
  88.8 0.1 collective-permute-start.7
  88.8 0.8 collective-permute-start.8
  89.6 3.6 %collective-permute-start.9 = (f32[1,256]{1,0:T(1,128)S(1)}, f32[1,256]{1,0:T(1,128)S(1)}, u32[]{:S(2)}, u32[]{:S(2)}) collective-permute-start(f32[1,256]{1,0:T(1,128)S(1)} %get-tuple-element.6), channel_id=1, source_target_pairs={{0,6},{2,4},{4,2},{6,0},{1,7},{3,5},{5,3},{7,1},{8,14},{10,12},{12... | collective-permute-start | bytes 3080 | tf_op jit(solution)/shard_map/ppermute | solution.py:268
  93.2 0.0 collective-permute-done.7
  93.2 0.2 collective-permute-done.8
  93.4 1.6 %collective-permute-done.9 = f32[1,256]{1,0:T(1,128)S(1)} collective-permute-done((f32[1,256]{1,0:T(1,128)S(1)}, f32[1,256]{1,0:T(1,128)S(1)}, u32[]{:S(2)}, u32[]{:S(2)}) %collective-permute-start.9) | collective-permute-done | bytes 1056 | tf_op jit(solution)/shard_map/ppermute | solution.py:268
  95.0 0.6 reverse_select_fusion
  (5 shorter events, 0.1 us)
Async XLA Ops:
  0.0 84.4 %collective-permute-start.6 = (bf16[128,8192]{1,0:T(8,128)(2,1)}, bf16[128,8192]{1,0:T(8,128)(2,1)}, u32[]{:S(2)}, u32[]{:S(2)}) collective-permute-start(bf16[128,8192]{1,0:T(8,128)(2,1)} %refs_4_.1), channel_id=1, source_target_pairs={{0,1},{1,0},{2,3},{3,2},{4,5},{5,4},{6,7},{7,6},{8,9},{9,8},{10,11... | collective-permute-start | bytes 6291464 | tf_op jit(solution)/shard_map/ppermute | solution.py:268
  68.6 1.9 %collective-permute-start = (f32[64,128]{1,0:T(8,128)}, f32[64,128]{1,0:T(8,128)S(1)}, u32[]{:S(2)}, u32[]{:S(2)}) collective-permute-start(f32[64,128]{1,0:T(8,128)} %sketch.1), channel_id=1, source_target_pairs={{0,8},{8,0},{16,24},{24,16},{1,9},{9,1},{17,25},{25,17},{2,10},{10... | collective-permute-start | bytes 98312 | tf_op jit(solution)/shard_map/ppermute | solution.py:268
  68.7 4.2 %collective-permute-start.1 = (f32[64,128]{1,0:T(8,128)}, f32[64,128]{1,0:T(8,128)S(1)}, u32[]{:S(2)}, u32[]{:S(2)}) collective-permute-start(f32[64,128]{1,0:T(8,128)} %sketch.1), channel_id=1, source_target_pairs={{0,16},{8,24},{16,0},{24,8},{1,17},{9,25},{17,1},{25,9},{2,18},{10... | collective-permute-start | bytes 98312 | tf_op jit(solution)/shard_map/ppermute | solution.py:268
  70.3 3.6 %collective-permute-start.2 = (f32[64,128]{1,0:T(8,128)}, f32[64,128]{1,0:T(8,128)S(1)}, u32[]{:S(2)}, u32[]{:S(2)}) collective-permute-start(f32[64,128]{1,0:T(8,128)} %sketch.1), channel_id=1, source_target_pairs={{0,24},{8,16},{16,8},{24,0},{1,25},{9,17},{17,9},{25,1},{2,26},{10... | collective-permute-start | bytes 98312 | tf_op jit(solution)/shard_map/ppermute | solution.py:268
  74.6 4.5 %collective-permute-start.3 = (bf16[64,128]{1,0:T(8,128)(2,1)S(1)}, bf16[64,128]{1,0:T(8,128)(2,1)S(1)}, u32[]{:S(2)}, u32[]{:S(2)}) collective-permute-start(bf16[64,128]{1,0:T(8,128)(2,1)S(1)} %add_convert_fusion.refs_0_), channel_id=1, source_target_pairs={{0,2},{2,0},{4,6},{6,4},{1,3},{3,1},{5,7},{7,5},{8,10},{10,8},{12,... | collective-permute-start | bytes 49160 | tf_op jit(solution)/shard_map/ppermute | solution.py:268
  76.3 4.7 %collective-permute-start.4 = (bf16[64,128]{1,0:T(8,128)(2,1)S(1)}, bf16[64,128]{1,0:T(8,128)(2,1)S(1)}, u32[]{:S(2)}, u32[]{:S(2)}) collective-permute-start(bf16[64,128]{1,0:T(8,128)(2,1)S(1)} %add_convert_fusion.refs_0_), channel_id=1, source_target_pairs={{0,4},{2,6},{4,0},{6,2},{1,5},{3,7},{5,1},{7,3},{8,12},{10,14},{12... | collective-permute-start | bytes 49160 | tf_op jit(solution)/shard_map/ppermute | solution.py:268
  78.9 5.5 %collective-permute-start.5 = (bf16[64,128]{1,0:T(8,128)(2,1)S(1)}, bf16[64,128]{1,0:T(8,128)(2,1)S(1)}, u32[]{:S(2)}, u32[]{:S(2)}) collective-permute-start(bf16[64,128]{1,0:T(8,128)(2,1)S(1)} %add_convert_fusion.refs_0_), channel_id=1, source_target_pairs={{0,6},{2,4},{4,2},{6,0},{1,7},{3,5},{5,3},{7,1},{8,14},{10,12},{12... | collective-permute-start | bytes 49160 | tf_op jit(solution)/shard_map/ppermute | solution.py:268
  84.4 1.6 %copy-start = (bf16[128,8192]{1,0:T(8,128)(2,1)S(1)}, bf16[128,8192]{1,0:T(8,128)(2,1)}, u32[]{:S(2)}) copy-start(bf16[128,8192]{1,0:T(8,128)(2,1)} %refs_4_.1) | copy-start | bytes 6291460
  88.8 4.4 %collective-permute-start.7 = (f32[1,256]{1,0:T(1,128)S(1)}, f32[1,256]{1,0:T(1,128)S(1)}, u32[]{:S(2)}, u32[]{:S(2)}) collective-permute-start(f32[1,256]{1,0:T(1,128)S(1)} %get-tuple-element.8), channel_id=1, source_target_pairs={{0,2},{2,0},{4,6},{6,4},{1,3},{3,1},{5,7},{7,5},{8,10},{10,8},{12,... | collective-permute-start | bytes 3080 | tf_op jit(solution)/shard_map/ppermute | solution.py:268
  88.8 4.5 %collective-permute-start.8 = (f32[1,256]{1,0:T(1,128)S(1)}, f32[1,256]{1,0:T(1,128)S(1)}, u32[]{:S(2)}, u32[]{:S(2)}) collective-permute-start(f32[1,256]{1,0:T(1,128)S(1)} %get-tuple-element.7), channel_id=1, source_target_pairs={{0,4},{2,6},{4,0},{6,2},{1,5},{3,7},{5,1},{7,3},{8,12},{10,14},{12... | collective-permute-start | bytes 3080 | tf_op jit(solution)/shard_map/ppermute | solution.py:268
  89.6 5.4 %collective-permute-start.9 = (f32[1,256]{1,0:T(1,128)S(1)}, f32[1,256]{1,0:T(1,128)S(1)}, u32[]{:S(2)}, u32[]{:S(2)}) collective-permute-start(f32[1,256]{1,0:T(1,128)S(1)} %get-tuple-element.6), channel_id=1, source_target_pairs={{0,6},{2,4},{4,2},{6,0},{1,7},{3,5},{5,3},{7,1},{8,14},{10,12},{12... | collective-permute-start | bytes 3080 | tf_op jit(solution)/shard_map/ppermute | solution.py:268

commit v7 on v6

--- a/solution.py
+++ b/solution.py
@@ -59,13 +59,14 @@
         @pl.loop(0, high_dev // 8)
         def _(n):
             for i in range(8):
-                grad_copy(step, n * 8 + i).start()
+                grad_copy(step, n * 8 + i).start(priority=i % 2)
 
     def wait_copies(step):
         slot = step % SLOTS
         pltpu.make_async_copy(xbuf.at[slot], xbuf.at[slot], sems.at[slot]).wait()
 
-    word_copy = pltpu.make_async_copy(words, wbuf, wsem)
+    per_high = NMID * NLOW // 16 // LANES
+    word_copy = pltpu.make_async_copy(words, wbuf.at[:, :per_high], wsem)
     word_copy.start()
     start_copies(0)
     start_copies(1)
@@ -100,14 +101,18 @@
         ).astype(jnp.bfloat16)
 
     word_copy.wait()
-    per_high = NMID * NLOW // 16 // LANES
+    lines = wbuf.reshape(high_dev * (per_high + 1), 1, LANES)
 
     @pl.loop(0, high_dev // 8)
     def _(n):
         for c in range(chunks):
             for pair in range(TOP // 2):
-                one = wbuf[pl.ds(n * 8 * per_high + (2 * pair) * chunks + c, 8, per_high), :]
-                two = wbuf[pl.ds(n * 8 * per_high + (2 * pair + 1) * chunks + c, 8, per_high), :]
+                one, two = (
+                    lines[
+                        pl.ds(n * 8 * (per_high + 1) + (2 * pair + which) * chunks + c, 8, per_high + 1), 0, :
+                    ]
+                    for which in range(2)
+                )
                 wpair[c, pair, pl.ds(pl.multiple_of(n * 8, 8), 8), :] = jnp.bitwise_or(
                     one, jnp.left_shift(two, 16)
                 )
@@ -190,7 +195,7 @@
         def _(u):
             if step + SLOTS < steps:
                 for n in range(high_dev // turns):
-                    grad_copy(step + SLOTS, u * (high_dev // turns) + n).start()
+                    grad_copy(step + SLOTS, u * (high_dev // turns) + n).start(priority=n % 2)
             if step >= per_chunk:
                 some_pairs(step % per_chunk * turns + u, functools.partial(evaluate, step // per_chunk - 1))
             else:
@@ -228,7 +233,7 @@
     groups = high_dev // PACK
     points = kept // (HALVED * groups)
     grads = gradients.reshape(high_dev, TOP, 2 * rest, 1, LANES)
-    words = sign_words.reshape(-1, LANES)
+    words = sign_words.reshape(high_dev, -1, 1, LANES)
     return pl.pallas_call(
         functools.partial(sketch_kernel, high_dev=high_dev, scale=scale),
         out_shape=jax.ShapeDtypeStruct((kept // LANES, LANES), jnp.float32),
@@ -241,7 +246,7 @@
         out_specs=pl.BlockSpec(memory_space=pltpu.VMEM),
         scratch_shapes=[
             pltpu.VMEM((SLOTS, TOP, ROWS, 1, high_dev * LANES), jnp.bfloat16),
-            pltpu.VMEM(words.shape, jnp.int32),
+            pltpu.VMEM((high_dev, words.shape[1] + 1, 1, LANES), jnp.int32),
             pltpu.VMEM((rest // GROUP, TOP // 2, high_dev, LANES), jnp.int32),
             pltpu.VMEM((high_dev, high_dev), jnp.bfloat16),
             pltpu.VMEM((TOP, STEP, high_dev, NLOW), jnp.bfloat16),
@@ -270,6 +275,11 @@
 
 def score_kernel(*refs, scale):
     *sketches, own_tests, near_tests, out_ref, lines = refs
+
+    @pl.when(pl.program_id(0) == 0)
+    def _():
+        out_ref[...] = jnp.zeros_like(out_ref)
+
     for n, sketch in enumerate(sketches):
         whole = sketch[...].astype(jnp.float32)
         for row in range(whole.shape[0]):
@@ -279,18 +289,25 @@
         found = lax.dot_general(
             left, tests[...], (((1,), (1,)), ((), ())), preferred_element_type=jnp.float32
         )
-        found = found[: len(sketches)] * scale
-        out_ref[:, n * tests.shape[0] : (n + 1) * tests.shape[0]] = found
+        out_ref[:, n * tests.shape[0] : (n + 1) * tests.shape[0]] += found[: len(sketches)] * scale
 
 
 def scores_of(sketches, own_tests, near_tests, scale):
     tests, kept = own_tests.shape
-    count = len(sketches)
+    count, near = len(sketches), near_tests.shape[0]
+    step = PACK * LANES
     return pl.pallas_call(
         functools.partial(score_kernel, scale=scale),
-        out_shape=jax.ShapeDtypeStruct((count, tests * (1 + near_tests.shape[0])), jnp.float32),
-        scratch_shapes=[pltpu.VMEM((16, kept), jnp.float32)],
-        compiler_params=pltpu.CompilerParams(vmem_limit_bytes=32 * 1024 * 1024),
+        grid=(kept // step,),
+        out_shape=jax.ShapeDtypeStruct((count, tests * (1 + near)), jnp.float32),
+        in_specs=[pl.BlockSpec((PACK, LANES), lambda n: (n, 0))] * count
+        + [
+            pl.BlockSpec((tests, step), lambda n: (0, n)),
+            pl.BlockSpec((near, tests, step), lambda n: (0, 0, n)),
+        ],
+        out_specs=pl.BlockSpec((count, tests * (1 + near)), lambda n: (0, 0)),
+        scratch_shapes=[pltpu.VMEM((16, step), jnp.float32)],
+        compiler_params=pltpu.CompilerParams(vmem_limit_bytes=62 * 1024 * 1024),
         name="scores",
     )(*sketches, own_tests, near_tests)
 

time: 96 us -> 97.2 us (1.012)
  Pallas kernels: 68.5 us -> 69.9 us
    pallas_call x1, Pallas kernels: 2.78 us -> 4.29 us  [scores_of(): pl.pallas_call(functools.partial(score_kernel, scale=scale), grid=(kept /...]
    unnamed x2 -> x8, local copies, waits for them, and re-layouts: 1.59 us -> 0.58 us
  transfers between devices with their start and end apart: 10 -> 10, of which waited for: 6 -> 6; matrix products, arithmetic and copies ran while one was open for 1% -> 1% of each run, Pallas kernels for 69% -> 68%
where the time goes in v7:
time: 97.2 us; the launch traced here: 96.8 us
  Pallas kernels  69.9 us (72%)
  starting transfers between devices  13.7 us (14%)
  waiting for transfers between devices  10.3 us (11%)
  local copies, waits for them, and re-layouts  1.45 us (1%)
  other arithmetic  1.39 us (1%)
    pallas_call x1, Pallas kernels, partial_sketch(): pl.pallas_call(functools.partial(sketch_kernel, high_dev=high_dev, scale=...  65.6 us
    ppermute x10, starting transfers between devices, swapped(): return lax.ppermute(value, axis, [(i, i ^ bits) for i in range(size)])  13.7 us
    ppermute x10, waiting for transfers between devices, swapped(): return lax.ppermute(value, axis, [(i, i ^ bits) for i in range(size)])  10.3 us
    pallas_call x1, Pallas kernels, scores_of(): pl.pallas_call(functools.partial(score_kernel, scale=scale), grid=(kept /...  4.29 us
  transfers between devices with their start and end apart: 10, of which 6 were waited for; matrix products, arithmetic and copies ran while one was open for 1% of the time, Pallas kernels for 68%

profile of v7, /device:TPU:0, one launch (start us, length us, event | category | flops | bytes accessed | tf_op | source)
XLA Modules:
  0.0 96.8 jit_solution(17010635448753909329)
XLA Ops:
  0.0 2.9 %collective-permute-start.6 = (bf16[128,8192]{1,0:T(8,128)(2,1)}, bf16[128,8192]{1,0:T(8,128)(2,1)}, u32[]{:S(2)}, u32[]{:S(2)}) collective-permute-start(bf16[128,8192]{1,0:T(8,128)(2,1)} %refs_4_.1), channel_id=1, source_target_pairs={{0,1},{1,0},{2,3},{3,2},{4,5},{5,4},{6,7},{7,6},{8,9},{9,8},{10,11... | collective-permute-start | bytes 6291464 | tf_op jit(solution)/shard_map/ppermute | solution.py:273
  2.9 65.6 %sketch.1 = f32[64,128]{1,0:T(8,128)} custom-call(s32[1]{0:T(128)} %bitcast.place_ref, bf16[256,8,64,1,128]{4,3,2,1,0:T(2,128)(2,1)} %bitcast.1.grads, s32[256,32,1,128]{3,2,1,0:T(1,128)} %bitcast.13, s32[64,128]{1,0:T(8,128)} %bitcast.14), custom_call_target="tpu_custom_call" | custom-call | flops 17179869184 | bytes 67108864 | tf_op jit(solution)/shard_map/sketch/pallas_call | solution.py:237
  68.5 0.1 collective-permute-start
  68.6 1.6 %collective-permute-start.1 = (f32[64,128]{1,0:T(8,128)}, f32[64,128]{1,0:T(8,128)S(1)}, u32[]{:S(2)}, u32[]{:S(2)}) collective-permute-start(f32[64,128]{1,0:T(8,128)} %sketch.1), channel_id=1, source_target_pairs={{0,16},{8,24},{16,0},{24,8},{1,17},{9,25},{17,1},{25,9},{2,18},{10... | collective-permute-start | bytes 98312 | tf_op jit(solution)/shard_map/ppermute | solution.py:273
  70.2 0.3 collective-permute-start.2
  70.5 0.0 collective-permute-done
  70.5 2.3 %collective-permute-done.1 = f32[64,128]{1,0:T(8,128)S(1)} collective-permute-done((f32[64,128]{1,0:T(8,128)}, f32[64,128]{1,0:T(8,128)S(1)}, u32[]{:S(2)}, u32[]{:S(2)}) %collective-permute-start.1) | collective-permute-done | bytes 32800 | tf_op jit(solution)/shard_map/ppermute | solution.py:273
  72.8 0.9 collective-permute-done.2
  73.7 0.8 add_convert_fusion.refs_0_
  74.5 0.0 copy-start
  74.5 1.7 %collective-permute-start.3 = (bf16[64,128]{1,0:T(8,128)(2,1)S(1)}, bf16[64,128]{1,0:T(8,128)(2,1)S(1)}, u32[]{:S(2)}, u32[]{:S(2)}) collective-permute-start(bf16[64,128]{1,0:T(8,128)(2,1)S(1)} %add_convert_fusion.refs_0_), channel_id=1, source_target_pairs={{0,2},{2,0},{4,6},{6,4},{1,3},{3,1},{5,7},{7,5},{8,10},{10,8},{12,... | collective-permute-start | bytes 49160 | tf_op jit(solution)/shard_map/ppermute | solution.py:273
  76.2 2.6 %collective-permute-start.4 = (bf16[64,128]{1,0:T(8,128)(2,1)S(1)}, bf16[64,128]{1,0:T(8,128)(2,1)S(1)}, u32[]{:S(2)}, u32[]{:S(2)}) collective-permute-start(bf16[64,128]{1,0:T(8,128)(2,1)S(1)} %add_convert_fusion.refs_0_), channel_id=1, source_target_pairs={{0,4},{2,6},{4,0},{6,2},{1,5},{3,7},{5,1},{7,3},{8,12},{10,14},{12... | collective-permute-start | bytes 49160 | tf_op jit(solution)/shard_map/ppermute | solution.py:273
  78.8 0.2 collective-permute-start.5
  79.0 0.0 collective-permute-done.3.refs_1_
  79.0 0.0 copy-start.1
  79.0 1.9 %collective-permute-done.4.refs_2_ = bf16[64,128]{1,0:T(8,128)(2,1)S(1)} collective-permute-done((bf16[64,128]{1,0:T(8,128)(2,1)S(1)}, bf16[64,128]{1,0:T(8,128)(2,1)S(1)}, u32[]{:S(2)}, u32[]{:S(2)}) %collective-permute-start.4) | collective-permute-done | bytes 16416 | tf_op jit(solution)/shard_map/ppermute | solution.py:273
  80.9 0.0 copy-start.2
  80.9 3.5 %collective-permute-done.5.refs_3_ = bf16[64,128]{1,0:T(8,128)(2,1)S(1)} collective-permute-done((bf16[64,128]{1,0:T(8,128)(2,1)S(1)}, bf16[64,128]{1,0:T(8,128)(2,1)S(1)}, u32[]{:S(2)}, u32[]{:S(2)}) %collective-permute-start.5) | collective-permute-done | bytes 16416 | tf_op jit(solution)/shard_map/ppermute | solution.py:273
  84.3 0.0 copy-start.3
  84.3 0.0 collective-permute-done.6
  84.3 0.0 copy-done
  84.3 0.0 copy-done.1
  84.3 0.0 copy-done.2
  84.3 0.6 copy-done.3
  84.9 4.3 %scores.1 = f32[4,256]{1,0:T(4,128)} custom-call(bf16[64,128]{1,0:T(8,128)(2,1)} %copy-done, bf16[64,128]{1,0:T(8,128)(2,1)} %copy-done.1, bf16[64,128]{1,0:T(8,128)(2,1)} %copy-done.2, bf16[64,128]{1,0:T(8,128)(2,1)} %copy-done.3, bf16[128,8192]{1,0:T(8,128)(2,1)} %refs_4_.1, bf16[1,128,8192]{2,1,0:T(8,128)(2,1)} %bitcast.4.refs_5_), custom_call_target="tpu_custom_call" | custom-call | tf_op jit(solution)/shard_map/scores/pallas_call | solution.py:299
  89.2 0.8 fusion.1
  90.0 0.0 collective-permute-start.7
  90.1 0.7 collective-permute-start.8
  90.8 3.6 %collective-permute-start.9 = (f32[1,256]{1,0:T(1,128)S(1)}, f32[1,256]{1,0:T(1,128)S(1)}, u32[]{:S(2)}, u32[]{:S(2)}) collective-permute-start(f32[1,256]{1,0:T(1,128)S(1)} %get-tuple-element.6), channel_id=1, source_target_pairs={{0,6},{2,4},{4,2},{6,0},{1,7},{3,5},{5,3},{7,1},{8,14},{10,12},{12... | collective-permute-start | bytes 3080 | tf_op jit(solution)/shard_map/ppermute | solution.py:273
  94.4 0.0 collective-permute-done.7
  94.4 0.2 collective-permute-done.8
  94.6 1.6 %collective-permute-done.9 = f32[1,256]{1,0:T(1,128)S(1)} collective-permute-done((f32[1,256]{1,0:T(1,128)S(1)}, f32[1,256]{1,0:T(1,128)S(1)}, u32[]{:S(2)}, u32[]{:S(2)}) %collective-permute-start.9) | collective-permute-done | bytes 1056 | tf_op jit(solution)/shard_map/ppermute | solution.py:273
  96.2 0.6 reverse_select_fusion
  (4 shorter events, 0.1 us)
Async XLA Ops:
  0.0 84.3 %collective-permute-start.6 = (bf16[128,8192]{1,0:T(8,128)(2,1)}, bf16[128,8192]{1,0:T(8,128)(2,1)}, u32[]{:S(2)}, u32[]{:S(2)}) collective-permute-start(bf16[128,8192]{1,0:T(8,128)(2,1)} %refs_4_.1), channel_id=1, source_target_pairs={{0,1},{1,0},{2,3},{3,2},{4,5},{5,4},{6,7},{7,6},{8,9},{9,8},{10,11... | collective-permute-start | bytes 6291464 | tf_op jit(solution)/shard_map/ppermute | solution.py:273
  68.5 1.9 %collective-permute-start = (f32[64,128]{1,0:T(8,128)}, f32[64,128]{1,0:T(8,128)S(1)}, u32[]{:S(2)}, u32[]{:S(2)}) collective-permute-start(f32[64,128]{1,0:T(8,128)} %sketch.1), channel_id=1, source_target_pairs={{0,8},{8,0},{16,24},{24,16},{1,9},{9,1},{17,25},{25,17},{2,10},{10... | collective-permute-start | bytes 98312 | tf_op jit(solution)/shard_map/ppermute | solution.py:273
  68.6 4.2 %collective-permute-start.1 = (f32[64,128]{1,0:T(8,128)}, f32[64,128]{1,0:T(8,128)S(1)}, u32[]{:S(2)}, u32[]{:S(2)}) collective-permute-start(f32[64,128]{1,0:T(8,128)} %sketch.1), channel_id=1, source_target_pairs={{0,16},{8,24},{16,0},{24,8},{1,17},{9,25},{17,1},{25,9},{2,18},{10... | collective-permute-start | bytes 98312 | tf_op jit(solution)/shard_map/ppermute | solution.py:273
  70.2 3.6 %collective-permute-start.2 = (f32[64,128]{1,0:T(8,128)}, f32[64,128]{1,0:T(8,128)S(1)}, u32[]{:S(2)}, u32[]{:S(2)}) collective-permute-start(f32[64,128]{1,0:T(8,128)} %sketch.1), channel_id=1, source_target_pairs={{0,24},{8,16},{16,8},{24,0},{1,25},{9,17},{17,9},{25,1},{2,26},{10... | collective-permute-start | bytes 98312 | tf_op jit(solution)/shard_map/ppermute | solution.py:273
  74.5 9.8 %copy-start = (bf16[64,128]{1,0:T(8,128)(2,1)}, bf16[64,128]{1,0:T(8,128)(2,1)S(1)}, u32[]{:S(2)}) copy-start(bf16[64,128]{1,0:T(8,128)(2,1)S(1)} %add_convert_fusion.refs_0_) | copy-start | bytes 49156
  74.5 4.5 %collective-permute-start.3 = (bf16[64,128]{1,0:T(8,128)(2,1)S(1)}, bf16[64,128]{1,0:T(8,128)(2,1)S(1)}, u32[]{:S(2)}, u32[]{:S(2)}) collective-permute-start(bf16[64,128]{1,0:T(8,128)(2,1)S(1)} %add_convert_fusion.refs_0_), channel_id=1, source_target_pairs={{0,2},{2,0},{4,6},{6,4},{1,3},{3,1},{5,7},{7,5},{8,10},{10,8},{12,... | collective-permute-start | bytes 49160 | tf_op jit(solution)/shard_map/ppermute | solution.py:273
  76.2 4.7 %collective-permute-start.4 = (bf16[64,128]{1,0:T(8,128)(2,1)S(1)}, bf16[64,128]{1,0:T(8,128)(2,1)S(1)}, u32[]{:S(2)}, u32[]{:S(2)}) collective-permute-start(bf16[64,128]{1,0:T(8,128)(2,1)S(1)} %add_convert_fusion.refs_0_), channel_id=1, source_target_pairs={{0,4},{2,6},{4,0},{6,2},{1,5},{3,7},{5,1},{7,3},{8,12},{10,14},{12... | collective-permute-start | bytes 49160 | tf_op jit(solution)/shard_map/ppermute | solution.py:273
  78.8 5.5 %collective-permute-start.5 = (bf16[64,128]{1,0:T(8,128)(2,1)S(1)}, bf16[64,128]{1,0:T(8,128)(2,1)S(1)}, u32[]{:S(2)}, u32[]{:S(2)}) collective-permute-start(bf16[64,128]{1,0:T(8,128)(2,1)S(1)} %add_convert_fusion.refs_0_), channel_id=1, source_target_pairs={{0,6},{2,4},{4,2},{6,0},{1,7},{3,5},{5,3},{7,1},{8,14},{10,12},{12... | collective-permute-start | bytes 49160 | tf_op jit(solution)/shard_map/ppermute | solution.py:273
  79.0 5.4 %copy-start.1 = (bf16[64,128]{1,0:T(8,128)(2,1)}, bf16[64,128]{1,0:T(8,128)(2,1)S(1)}, u32[]{:S(2)}) copy-start(bf16[64,128]{1,0:T(8,128)(2,1)S(1)} %collective-permute-done.3.refs_1_) | copy-start | bytes 49156
  80.9 3.5 %copy-start.2 = (bf16[64,128]{1,0:T(8,128)(2,1)}, bf16[64,128]{1,0:T(8,128)(2,1)S(1)}, u32[]{:S(2)}) copy-start(bf16[64,128]{1,0:T(8,128)(2,1)S(1)} %collective-permute-done.4.refs_2_) | copy-start | bytes 49156
  84.3 0.6 copy-start.3
  90.0 4.4 %collective-permute-start.7 = (f32[1,256]{1,0:T(1,128)S(1)}, f32[1,256]{1,0:T(1,128)S(1)}, u32[]{:S(2)}, u32[]{:S(2)}) collective-permute-start(f32[1,256]{1,0:T(1,128)S(1)} %get-tuple-element.8), channel_id=1, source_target_pairs={{0,2},{2,0},{4,6},{6,4},{1,3},{3,1},{5,7},{7,5},{8,10},{10,8},{12,... | collective-permute-start | bytes 3080 | tf_op jit(solution)/shard_map/ppermute | solution.py:273
  90.1 4.5 %collective-permute-start.8 = (f32[1,256]{1,0:T(1,128)S(1)}, f32[1,256]{1,0:T(1,128)S(1)}, u32[]{:S(2)}, u32[]{:S(2)}) collective-permute-start(f32[1,256]{1,0:T(1,128)S(1)} %get-tuple-element.7), channel_id=1, source_target_pairs={{0,4},{2,6},{4,0},{6,2},{1,5},{3,7},{5,1},{7,3},{8,12},{10,14},{12... | collective-permute-start | bytes 3080 | tf_op jit(solution)/shard_map/ppermute | solution.py:273
  90.8 5.4 %collective-permute-start.9 = (f32[1,256]{1,0:T(1,128)S(1)}, f32[1,256]{1,0:T(1,128)S(1)}, u32[]{:S(2)}, u32[]{:S(2)}) collective-permute-start(f32[1,256]{1,0:T(1,128)S(1)} %get-tuple-element.6), channel_id=1, source_target_pairs={{0,6},{2,4},{4,2},{6,0},{1,7},{3,5},{5,3},{7,1},{8,14},{10,12},{12... | collective-permute-start | bytes 3080 | tf_op jit(solution)/shard_map/ppermute | solution.py:273

commit v8 on v6

--- a/solution.py
+++ b/solution.py
@@ -13,7 +13,6 @@
 GROUP = 8
 STEP = 4
 SLOTS = 3
-ROWS = 2 * STEP
 HALVED = TOP // 2
 LANES = 128
 PACK = 16
@@ -50,8 +49,8 @@
 
     def grad_copy(step, h):
         return pltpu.make_async_copy(
-            grads.at[h, :, pl.ds(step * ROWS, ROWS)],
-            xbuf.at[step % SLOTS, :, :, :, pl.ds(pl.multiple_of(h * LANES, LANES), LANES)],
+            grads.at[h, :, pl.ds(step * STEP, STEP)],
+            xbuf.at[step % SLOTS, :, :, :, pl.ds(pl.multiple_of(h * NLOW, NLOW), NLOW)],
             sems.at[step % SLOTS],
         )
 
@@ -65,13 +64,17 @@
         slot = step % SLOTS
         pltpu.make_async_copy(xbuf.at[slot], xbuf.at[slot], sems.at[slot]).wait()
 
-    word_copy = pltpu.make_async_copy(words, wbuf, wsem)
+    per_high = NMID * NLOW // 16 // LANES
+    word_copy = pltpu.make_async_copy(words, wbuf.at[:, :per_high], wsem)
     word_copy.start()
     start_copies(0)
     start_copies(1)
 
+    out, given = iota(table.shape, 0), iota(table.shape, 1)
     table[...] = jnp.where(
-        odd_common_bits(iota(table.shape, 0), iota(table.shape, 1)), -1.0, 1.0
+        out // (high_dev // 2) == given % 2,
+        jnp.where(odd_common_bits(out % (high_dev // 2), given // 2), -1.0, 1.0),
+        0.0,
     ).astype(jnp.bfloat16)
     acc[...] = jnp.zeros_like(acc)
     lane = iota((groups, LANES), 1)
@@ -100,17 +103,21 @@
         ).astype(jnp.bfloat16)
 
     word_copy.wait()
-    per_high = NMID * NLOW // 16 // LANES
+    lines = wbuf.reshape(high_dev * (per_high + 1), 1, LANES)
 
     @pl.loop(0, high_dev // 8)
     def _(n):
         for c in range(chunks):
             for pair in range(TOP // 2):
-                one = wbuf[pl.ds(n * 8 * per_high + (2 * pair) * chunks + c, 8, per_high), :]
-                two = wbuf[pl.ds(n * 8 * per_high + (2 * pair + 1) * chunks + c, 8, per_high), :]
-                wpair[c, pair, pl.ds(pl.multiple_of(n * 8, 8), 8), :] = jnp.bitwise_or(
-                    one, jnp.left_shift(two, 16)
+                one, two = (
+                    lines[
+                        pl.ds(n * 8 * (per_high + 1) + (2 * pair + which) * chunks + c, 8, per_high + 1), 0, :
+                    ]
+                    for which in range(2)
                 )
+                both = jnp.bitwise_or(one, jnp.left_shift(two, 16))
+                for l_hi in range(2):
+                    wpair[c, pair, pl.ds(n * 16 + l_hi, 8, 2), :] = both
 
     def prepare(step, u):
         slot = step % SLOTS
@@ -118,29 +125,34 @@
         lane16 = iota((PACK, LANES), 1)
         bits = [jnp.left_shift(1, lane16 % 16), jnp.left_shift(1, lane16 % 16 + 16)]
         i = u * STEP // turns
+        spot = (step % (GROUP // STEP) * STEP + i) * 16 + iota((PACK, LANES), 0) % 2 * half + lane16 // 16
         for n in range(blocks):
             block = (u * blocks + n) % (high_dev // PACK)
+            values = [[None, None] for _ in range(TOP)]
+            for t in range(2):
+                row = pl.multiple_of(t * high_dev + block * PACK, PACK)
+                for pair in range(TOP // 2):
+                    word = wpair[chunk, pair, pl.ds(row, PACK), :]
+                    word = jnp.take_along_axis(word, spot, axis=1, mode="promise_in_bounds")
+                    for which in range(2):
+                        columns = pl.ds(pl.multiple_of(row * LANES, PACK * LANES), PACK * LANES)
+                        value = xbuf[slot, 2 * pair + which, i, :, columns]
+                        value = value.reshape(PACK, LANES).astype(jnp.float32)
+                        values[2 * pair + which][t] = jnp.where(
+                            jnp.bitwise_and(word, bits[which]) != 0, value, -value
+                        )
+            values = [[one + two, one - two] for one, two in values]
+            for reach in (2, 4):
+                nxt = list(values)
+                for at in range(TOP):
+                    if not at & reach:
+                        nxt[at] = [values[at][t] + values[at + reach][t] for t in range(2)]
+                        nxt[at + reach] = [values[at][t] - values[at + reach][t] for t in range(2)]
+                values = nxt
             rows = pl.ds(pl.multiple_of(block * PACK, PACK), PACK)
-            columns = pl.ds(pl.multiple_of(block * (PACK * LANES), PACK * LANES), PACK * LANES)
-            packed = [wpair[chunk, pair, rows, :] for pair in range(TOP // 2)]
-            for l_hi in range(2):
-                spot = (step % (GROUP // STEP) * STEP + i) * 16 + l_hi * half + lane16 // 16
-                values = []
-                for pair in range(TOP // 2):
-                    word = jnp.take_along_axis(packed[pair], spot, axis=1, mode="promise_in_bounds")
-                    for which in range(2):
-                        value = xbuf[slot, 2 * pair + which, 2 * i + l_hi, :, columns]
-                        value = value.reshape(PACK, LANES).astype(jnp.float32)
-                        values.append(jnp.where(jnp.bitwise_and(word, bits[which]) != 0, value, -value))
-                for reach in (2, 4):
-                    nxt = list(values)
-                    for at in range(TOP):
-                        if not at & reach:
-                            nxt[at] = values[at] + values[at + reach]
-                            nxt[at + reach] = values[at] - values[at + reach]
-                    values = nxt
-                for top in range(TOP):
-                    ybuf[step % 2][top, i, rows, l_hi * LANES : (l_hi + 1) * LANES] = values[top].astype(
+            for top in range(TOP):
+                for t in range(2):
+                    ybuf[step % 2][top, i, rows, t * LANES : (t + 1) * LANES] = values[top][t].astype(
                         jnp.bfloat16
                     )
 
@@ -152,9 +164,17 @@
         ).astype(jnp.bfloat16)
         chunk = step * STEP // GROUP
         row = step % (GROUP // STEP) * STEP + i
+        lower = high_dev // 2
         for n in range(PAIR):
             top = first + n
-            tbuf[chunk % 2][top // 2, n % 2 * GROUP + row] = result[:, n * NLOW : (n + 1) * NLOW]
+            for t in range(2):
+                for l_hi in range(2):
+                    tbuf[chunk % 2][
+                        top // 2,
+                        n % 2 * GROUP + row,
+                        t * lower : (t + 1) * lower,
+                        l_hi * LANES : (l_hi + 1) * LANES,
+                    ] = result[l_hi * lower : (l_hi + 1) * lower, (2 * n + t) * LANES : (2 * n + t + 1) * LANES]
 
     def evaluate(chunk, e):
         j, g = e // groups, e % groups
@@ -227,8 +247,8 @@
     rest = NMID // TOP
     groups = high_dev // PACK
     points = kept // (HALVED * groups)
-    grads = gradients.reshape(high_dev, TOP, 2 * rest, 1, LANES)
-    words = sign_words.reshape(-1, LANES)
+    grads = gradients.reshape(high_dev, TOP, rest, 1, NLOW)
+    words = sign_words.reshape(high_dev, -1, 1, LANES)
     return pl.pallas_call(
         functools.partial(sketch_kernel, high_dev=high_dev, scale=scale),
         out_shape=jax.ShapeDtypeStruct((kept // LANES, LANES), jnp.float32),
@@ -240,9 +260,9 @@
         ],
         out_specs=pl.BlockSpec(memory_space=pltpu.VMEM),
         scratch_shapes=[
-            pltpu.VMEM((SLOTS, TOP, ROWS, 1, high_dev * LANES), jnp.bfloat16),
-            pltpu.VMEM(words.shape, jnp.int32),
-            pltpu.VMEM((rest // GROUP, TOP // 2, high_dev, LANES), jnp.int32),
+            pltpu.VMEM((SLOTS, TOP, STEP, 1, high_dev * NLOW), jnp.bfloat16),
+            pltpu.VMEM((high_dev, words.shape[1] + 1, 1, LANES), jnp.int32),
+            pltpu.VMEM((rest // GROUP, TOP // 2, 2 * high_dev, LANES), jnp.int32),
             pltpu.VMEM((high_dev, high_dev), jnp.bfloat16),
             pltpu.VMEM((TOP, STEP, high_dev, NLOW), jnp.bfloat16),
             pltpu.VMEM((TOP, STEP, high_dev, NLOW), jnp.bfloat16),
@@ -256,7 +276,7 @@
             pltpu.SemaphoreType.DMA((SLOTS,)),
             pltpu.SemaphoreType.DMA,
         ],
-        compiler_params=pltpu.CompilerParams(vmem_limit_bytes=62 * 1024 * 1024),
+        compiler_params=pltpu.CompilerParams(vmem_limit_bytes=65000 * 1024),
         cost_estimate=pl.CostEstimate(
             flops=4 * NLOW * high_dev * NMID * NLOW, bytes_accessed=4 * gradients.size, transcendentals=0
         ),

time: 96 us -> 97.9 us (1.020)
  Pallas kernels: 68.5 us -> 70.4 us
    pallas_call x1, Pallas kernels: 65.7 us -> 67.7 us  [partial_sketch(): pl.pallas_call(functools.partial(sketch_kernel, high_dev=high_dev, scale=...]
where the time goes in v8:
time: 97.9 us; the launch traced here: 97.6 us
  Pallas kernels  70.4 us (72%)
  starting transfers between devices  13.7 us (14%)
  waiting for transfers between devices  10.4 us (11%)
  local copies, waits for them, and re-layouts  1.63 us (2%)
  other arithmetic  1.39 us (1%)
    pallas_call x1, Pallas kernels, partial_sketch(): pl.pallas_call(functools.partial(sketch_kernel, high_dev=high_dev, scale=...  67.7 us
    ppermute x10, starting transfers between devices, swapped(): return lax.ppermute(value, axis, [(i, i ^ bits) for i in range(size)])  13.7 us
    ppermute x10, waiting for transfers between devices, swapped(): return lax.ppermute(value, axis, [(i, i ^ bits) for i in range(size)])  10.4 us
    pallas_call x1, Pallas kernels, scores_of(): pl.pallas_call(functools.partial(score_kernel, scale=scale), out_shape=ja...  2.78 us
  transfers between devices with their start and end apart: 10, of which 6 were waited for; matrix products, arithmetic and copies ran while one was open for 1% of the time, Pallas kernels for 69%

profile of v8, /device:TPU:0, one launch (start us, length us, event | category | flops | bytes accessed | tf_op | source)
XLA Modules:
  0.0 97.6 jit_solution(7518117582538840946)
XLA Ops:
  0.0 2.9 %collective-permute-start.6 = (bf16[128,8192]{1,0:T(8,128)(2,1)}, bf16[128,8192]{1,0:T(8,128)(2,1)}, u32[]{:S(2)}, u32[]{:S(2)}) collective-permute-start(bf16[128,8192]{1,0:T(8,128)(2,1)} %refs_4_.1), channel_id=1, source_target_pairs={{0,1},{1,0},{2,3},{3,2},{4,5},{5,4},{6,7},{7,6},{8,9},{9,8},{10,11... | collective-permute-start | bytes 6291464 | tf_op jit(solution)/shard_map/ppermute | solution.py:288
  2.9 67.7 %sketch.1 = f32[64,128]{1,0:T(8,128)} custom-call(s32[1]{0:T(128)} %bitcast.place_ref, bf16[256,8,32,1,256]{4,3,2,1,0:T(2,128)(2,1)} %bitcast.1.grads, s32[256,32,1,128]{3,2,1,0:T(1,128)} %bitcast.13, s32[64,128]{1,0:T(8,128)} %bitcast.14), custom_call_target="tpu_custom_call" | custom-call | flops 17179869184 | bytes 67108864 | tf_op jit(solution)/shard_map/sketch/pallas_call | solution.py:252
  70.6 0.1 collective-permute-start
  70.7 1.6 %collective-permute-start.1 = (f32[64,128]{1,0:T(8,128)}, f32[64,128]{1,0:T(8,128)S(1)}, u32[]{:S(2)}, u32[]{:S(2)}) collective-permute-start(f32[64,128]{1,0:T(8,128)} %sketch.1), channel_id=1, source_target_pairs={{0,16},{8,24},{16,0},{24,8},{1,17},{9,25},{17,1},{25,9},{2,18},{10... | collective-permute-start | bytes 98312 | tf_op jit(solution)/shard_map/ppermute | solution.py:288
  72.3 0.3 collective-permute-start.2
  72.5 0.0 collective-permute-done
  72.5 2.3 %collective-permute-done.1 = f32[64,128]{1,0:T(8,128)S(1)} collective-permute-done((f32[64,128]{1,0:T(8,128)}, f32[64,128]{1,0:T(8,128)S(1)}, u32[]{:S(2)}, u32[]{:S(2)}) %collective-permute-start.1) | collective-permute-done | bytes 32800 | tf_op jit(solution)/shard_map/ppermute | solution.py:288
  74.9 0.9 collective-permute-done.2
  75.8 0.8 add_convert_fusion.refs_0_
  76.6 1.6 %collective-permute-start.3 = (bf16[64,128]{1,0:T(8,128)(2,1)S(1)}, bf16[64,128]{1,0:T(8,128)(2,1)S(1)}, u32[]{:S(2)}, u32[]{:S(2)}) collective-permute-start(bf16[64,128]{1,0:T(8,128)(2,1)S(1)} %add_convert_fusion.refs_0_), channel_id=1, source_target_pairs={{0,2},{2,0},{4,6},{6,4},{1,3},{3,1},{5,7},{7,5},{8,10},{10,8},{12,... | collective-permute-start | bytes 49160 | tf_op jit(solution)/shard_map/ppermute | solution.py:288
  78.2 2.6 %collective-permute-start.4 = (bf16[64,128]{1,0:T(8,128)(2,1)S(1)}, bf16[64,128]{1,0:T(8,128)(2,1)S(1)}, u32[]{:S(2)}, u32[]{:S(2)}) collective-permute-start(bf16[64,128]{1,0:T(8,128)(2,1)S(1)} %add_convert_fusion.refs_0_), channel_id=1, source_target_pairs={{0,4},{2,6},{4,0},{6,2},{1,5},{3,7},{5,1},{7,3},{8,12},{10,14},{12... | collective-permute-start | bytes 49160 | tf_op jit(solution)/shard_map/ppermute | solution.py:288
  80.8 0.2 collective-permute-start.5
  81.0 0.0 collective-permute-done.3.refs_1_
  81.0 1.9 %collective-permute-done.4.refs_2_ = bf16[64,128]{1,0:T(8,128)(2,1)S(1)} collective-permute-done((bf16[64,128]{1,0:T(8,128)(2,1)S(1)}, bf16[64,128]{1,0:T(8,128)(2,1)S(1)}, u32[]{:S(2)}, u32[]{:S(2)}) %collective-permute-start.4) | collective-permute-done | bytes 16416 | tf_op jit(solution)/shard_map/ppermute | solution.py:288
  82.9 3.4 %collective-permute-done.5.refs_3_ = bf16[64,128]{1,0:T(8,128)(2,1)S(1)} collective-permute-done((bf16[64,128]{1,0:T(8,128)(2,1)S(1)}, bf16[64,128]{1,0:T(8,128)(2,1)S(1)}, u32[]{:S(2)}, u32[]{:S(2)}) %collective-permute-start.5) | collective-permute-done | bytes 16416 | tf_op jit(solution)/shard_map/ppermute | solution.py:288
  86.3 0.0 collective-permute-done.6
  86.4 0.0 copy-start
  86.4 1.6 %copy-done = bf16[128,8192]{1,0:T(8,128)(2,1)S(1)} copy-done((bf16[128,8192]{1,0:T(8,128)(2,1)S(1)}, bf16[128,8192]{1,0:T(8,128)(2,1)}, u32[]{:S(2)}) %copy-start) | copy-done | bytes 2097176
  87.9 2.8 %scores.1 = f32[4,256]{1,0:T(4,128)S(1)} custom-call(bf16[64,128]{1,0:T(8,128)(2,1)S(1)} %add_convert_fusion.refs_0_, bf16[64,128]{1,0:T(8,128)(2,1)S(1)} %collective-permute-done.3.refs_1_, bf16[64,128]{1,0:T(8,128)(2,1)S(1)} %collective-permute-done.4.refs_2_, bf16[64,128]{1,0:T(8,128)(2,1)S(1)} %collective-permute-done.5.refs_3_, ...), custom_call_target="tpu_custom_call" | custom-call | tf_op jit(solution)/shard_map/scores/pallas_call | solution.py:309
  90.7 0.1 collective-permute-start.7
  90.8 0.8 collective-permute-start.8
  91.6 3.6 %collective-permute-start.9 = (f32[1,256]{1,0:T(1,128)S(1)}, f32[1,256]{1,0:T(1,128)S(1)}, u32[]{:S(2)}, u32[]{:S(2)}) collective-permute-start(f32[1,256]{1,0:T(1,128)S(1)} %get-tuple-element.6), channel_id=1, source_target_pairs={{0,6},{2,4},{4,2},{6,0},{1,7},{3,5},{5,3},{7,1},{8,14},{10,12},{12... | collective-permute-start | bytes 3080 | tf_op jit(solution)/shard_map/ppermute | solution.py:288
  95.2 0.0 collective-permute-done.7
  95.2 0.2 collective-permute-done.8
  95.3 1.6 %collective-permute-done.9 = f32[1,256]{1,0:T(1,128)S(1)} collective-permute-done((f32[1,256]{1,0:T(1,128)S(1)}, f32[1,256]{1,0:T(1,128)S(1)}, u32[]{:S(2)}, u32[]{:S(2)}) %collective-permute-start.9) | collective-permute-done | bytes 1056 | tf_op jit(solution)/shard_map/ppermute | solution.py:288
  97.0 0.6 reverse_select_fusion
  (5 shorter events, 0.1 us)
Async XLA Ops:
  0.0 86.4 %collective-permute-start.6 = (bf16[128,8192]{1,0:T(8,128)(2,1)}, bf16[128,8192]{1,0:T(8,128)(2,1)}, u32[]{:S(2)}, u32[]{:S(2)}) collective-permute-start(bf16[128,8192]{1,0:T(8,128)(2,1)} %refs_4_.1), channel_id=1, source_target_pairs={{0,1},{1,0},{2,3},{3,2},{4,5},{5,4},{6,7},{7,6},{8,9},{9,8},{10,11... | collective-permute-start | bytes 6291464 | tf_op jit(solution)/shard_map/ppermute | solution.py:288
  70.6 1.9 %collective-permute-start = (f32[64,128]{1,0:T(8,128)}, f32[64,128]{1,0:T(8,128)S(1)}, u32[]{:S(2)}, u32[]{:S(2)}) collective-permute-start(f32[64,128]{1,0:T(8,128)} %sketch.1), channel_id=1, source_target_pairs={{0,8},{8,0},{16,24},{24,16},{1,9},{9,1},{17,25},{25,17},{2,10},{10... | collective-permute-start | bytes 98312 | tf_op jit(solution)/shard_map/ppermute | solution.py:288
  70.7 4.2 %collective-permute-start.1 = (f32[64,128]{1,0:T(8,128)}, f32[64,128]{1,0:T(8,128)S(1)}, u32[]{:S(2)}, u32[]{:S(2)}) collective-permute-start(f32[64,128]{1,0:T(8,128)} %sketch.1), channel_id=1, source_target_pairs={{0,16},{8,24},{16,0},{24,8},{1,17},{9,25},{17,1},{25,9},{2,18},{10... | collective-permute-start | bytes 98312 | tf_op jit(solution)/shard_map/ppermute | solution.py:288
  72.3 3.6 %collective-permute-start.2 = (f32[64,128]{1,0:T(8,128)}, f32[64,128]{1,0:T(8,128)S(1)}, u32[]{:S(2)}, u32[]{:S(2)}) collective-permute-start(f32[64,128]{1,0:T(8,128)} %sketch.1), channel_id=1, source_target_pairs={{0,24},{8,16},{16,8},{24,0},{1,25},{9,17},{17,9},{25,1},{2,26},{10... | collective-permute-start | bytes 98312 | tf_op jit(solution)/shard_map/ppermute | solution.py:288
  76.6 4.5 %collective-permute-start.3 = (bf16[64,128]{1,0:T(8,128)(2,1)S(1)}, bf16[64,128]{1,0:T(8,128)(2,1)S(1)}, u32[]{:S(2)}, u32[]{:S(2)}) collective-permute-start(bf16[64,128]{1,0:T(8,128)(2,1)S(1)} %add_convert_fusion.refs_0_), channel_id=1, source_target_pairs={{0,2},{2,0},{4,6},{6,4},{1,3},{3,1},{5,7},{7,5},{8,10},{10,8},{12,... | collective-permute-start | bytes 49160 | tf_op jit(solution)/shard_map/ppermute | solution.py:288
  78.2 4.7 %collective-permute-start.4 = (bf16[64,128]{1,0:T(8,128)(2,1)S(1)}, bf16[64,128]{1,0:T(8,128)(2,1)S(1)}, u32[]{:S(2)}, u32[]{:S(2)}) collective-permute-start(bf16[64,128]{1,0:T(8,128)(2,1)S(1)} %add_convert_fusion.refs_0_), channel_id=1, source_target_pairs={{0,4},{2,6},{4,0},{6,2},{1,5},{3,7},{5,1},{7,3},{8,12},{10,14},{12... | collective-permute-start | bytes 49160 | tf_op jit(solution)/shard_map/ppermute | solution.py:288
  80.8 5.5 %collective-permute-start.5 = (bf16[64,128]{1,0:T(8,128)(2,1)S(1)}, bf16[64,128]{1,0:T(8,128)(2,1)S(1)}, u32[]{:S(2)}, u32[]{:S(2)}) collective-permute-start(bf16[64,128]{1,0:T(8,128)(2,1)S(1)} %add_convert_fusion.refs_0_), channel_id=1, source_target_pairs={{0,6},{2,4},{4,2},{6,0},{1,7},{3,5},{5,3},{7,1},{8,14},{10,12},{12... | collective-permute-start | bytes 49160 | tf_op jit(solution)/shard_map/ppermute | solution.py:288
  86.4 1.6 %copy-start = (bf16[128,8192]{1,0:T(8,128)(2,1)S(1)}, bf16[128,8192]{1,0:T(8,128)(2,1)}, u32[]{:S(2)}) copy-start(bf16[128,8192]{1,0:T(8,128)(2,1)} %refs_4_.1) | copy-start | bytes 6291460
  90.7 4.4 %collective-permute-start.7 = (f32[1,256]{1,0:T(1,128)S(1)}, f32[1,256]{1,0:T(1,128)S(1)}, u32[]{:S(2)}, u32[]{:S(2)}) collective-permute-start(f32[1,256]{1,0:T(1,128)S(1)} %get-tuple-element.8), channel_id=1, source_target_pairs={{0,2},{2,0},{4,6},{6,4},{1,3},{3,1},{5,7},{7,5},{8,10},{10,8},{12,... | collective-permute-start | bytes 3080 | tf_op jit(solution)/shard_map/ppermute | solution.py:288
  90.8 4.5 %collective-permute-start.8 = (f32[1,256]{1,0:T(1,128)S(1)}, f32[1,256]{1,0:T(1,128)S(1)}, u32[]{:S(2)}, u32[]{:S(2)}) collective-permute-start(f32[1,256]{1,0:T(1,128)S(1)} %get-tuple-element.7), channel_id=1, source_target_pairs={{0,4},{2,6},{4,0},{6,2},{1,5},{3,7},{5,1},{7,3},{8,12},{10,14},{12... | collective-permute-start | bytes 3080 | tf_op jit(solution)/shard_map/ppermute | solution.py:288
  91.6 5.4 %collective-permute-start.9 = (f32[1,256]{1,0:T(1,128)S(1)}, f32[1,256]{1,0:T(1,128)S(1)}, u32[]{:S(2)}, u32[]{:S(2)}) collective-permute-start(f32[1,256]{1,0:T(1,128)S(1)} %get-tuple-element.6), channel_id=1, source_target_pairs={{0,6},{2,4},{4,2},{6,0},{1,7},{3,5},{5,3},{7,1},{8,14},{10,12},{12... | collective-permute-start | bytes 3080 | tf_op jit(solution)/shard_map/ppermute | solution.py:288

commit v9 on v8

--- a/solution.py
+++ b/solution.py
@@ -119,14 +119,14 @@
                 for l_hi in range(2):
                     wpair[c, pair, pl.ds(n * 16 + l_hi, 8, 2), :] = both
 
-    def prepare(step, u):
+    def prepare(step, u, part, parts):
         slot = step % SLOTS
         chunk = step * STEP // GROUP
         lane16 = iota((PACK, LANES), 1)
         bits = [jnp.left_shift(1, lane16 % 16), jnp.left_shift(1, lane16 % 16 + 16)]
         i = u * STEP // turns
         spot = (step % (GROUP // STEP) * STEP + i) * 16 + iota((PACK, LANES), 0) % 2 * half + lane16 // 16
-        for n in range(blocks):
+        for n in range(part * blocks // parts, (part + 1) * blocks // parts):
             block = (u * blocks + n) % (high_dev // PACK)
             values = [[None, None] for _ in range(TOP)]
             for t in range(2):
@@ -156,25 +156,21 @@
                         jnp.bfloat16
                     )
 
-    def transform_high(step, u):
-        first, i = u * PAIR % TOP, u * PAIR // TOP
-        columns = [ybuf[step % 2][first + n, i] for n in range(PAIR)]
-        result = jnp.dot(
-            table[...], jnp.concatenate(columns, axis=1), preferred_element_type=jnp.float32
-        ).astype(jnp.bfloat16)
+    def transform_high(step, u, n):
+        top, i = u * PAIR % TOP + n, u * PAIR // TOP
+        result = jnp.dot(table[...], ybuf[step % 2][top, i], preferred_element_type=jnp.float32)
+        result = result.astype(jnp.bfloat16)
         chunk = step * STEP // GROUP
         row = step % (GROUP // STEP) * STEP + i
         lower = high_dev // 2
-        for n in range(PAIR):
-            top = first + n
-            for t in range(2):
-                for l_hi in range(2):
-                    tbuf[chunk % 2][
-                        top // 2,
-                        n % 2 * GROUP + row,
-                        t * lower : (t + 1) * lower,
-                        l_hi * LANES : (l_hi + 1) * LANES,
-                    ] = result[l_hi * lower : (l_hi + 1) * lower, (2 * n + t) * LANES : (2 * n + t + 1) * LANES]
+        for t in range(2):
+            for l_hi in range(2):
+                tbuf[chunk % 2][
+                    top // 2,
+                    n % 2 * GROUP + row,
+                    t * lower : (t + 1) * lower,
+                    l_hi * LANES : (l_hi + 1) * LANES,
+                ] = result[l_hi * lower : (l_hi + 1) * lower, t * LANES : (t + 1) * LANES]
 
     def evaluate(chunk, e):
         j, g = e // groups, e % groups
@@ -187,20 +183,19 @@
             total += found[n * PACK : (n + 1) * PACK] * signs[e, n : n + 1, :]
         acc[e] += total * signs[e, 2 * GROUP + chunk : 2 * GROUP + chunk + 1, :]
 
-    def some_pairs(n, do):
-        if pairs >= rounds:
-            for m in range(pairs // rounds):
-                do(n * (pairs // rounds) + m)
-        else:
-            pl.when(n < pairs)(lambda: do(n))
-
+    def some_pairs(n, part, do):
+        if pairs >= PAIR * rounds:
+            for m in range(pairs // (PAIR * rounds)):
+                do((n * PAIR + part) * (pairs // (PAIR * rounds)) + m)
+        elif part % (PAIR * rounds // pairs) == 0:
+            do((n * PAIR + part) // (PAIR * rounds // pairs))
 
     wait_copies(0)
     start_copies(2)
 
     @pl.loop(0, turns)
     def _(u):
-        prepare(0, u)
+        prepare(0, u, 0, 1)
 
     for step in range(steps):
         if step + 1 < steps:
@@ -211,13 +206,18 @@
             if step + SLOTS < steps:
                 for n in range(high_dev // turns):
                     grad_copy(step + SLOTS, u * (high_dev // turns) + n).start()
-            if step >= per_chunk:
-                some_pairs(step % per_chunk * turns + u, functools.partial(evaluate, step // per_chunk - 1))
-            else:
-                some_pairs(step * turns + u, build)
-            transform_high(step, u)
-            if step + 1 < steps:
-                prepare(step + 1, u)
+            for part in range(PAIR):
+                if step >= per_chunk:
+                    some_pairs(
+                        step % per_chunk * turns + u,
+                        part,
+                        functools.partial(evaluate, step // per_chunk - 1),
+                    )
+                else:
+                    some_pairs(step * turns + u, part, build)
+                transform_high(step, u, part)
+                if step + 1 < steps:
+                    prepare(step + 1, u, part, PAIR)
 
     @pl.loop(0, pairs)
     def _(e):
@@ -288,31 +288,63 @@
     return lax.ppermute(value, axis, [(i, i ^ bits) for i in range(size)])
 
 
-def score_kernel(*refs, scale):
-    *sketches, own_tests, near_tests, out_ref, lines = refs
+def score_kernel(*refs, scale, cuts):
+    *sketches, own_tests, near_tests, out_ref, lines, held, sems = refs
+    sources = [own_tests] + [near_tests.at[s] for s in range(near_tests.shape[0])]
+    tests, kept = own_tests.shape
+    wide = kept // cuts
+    copies = [
+        [
+            pltpu.make_async_copy(
+                source.at[:, cut * wide : (cut + 1) * wide],
+                held.at[n * tests : (n + 1) * tests, cut * wide : (cut + 1) * wide],
+                sems.at[n, cut],
+            )
+            for n, source in enumerate(sources)
+        ]
+        for cut in range(cuts)
+    ]
+    for cut in range(cuts):
+        for copy in copies[cut]:
+            copy.start()
     for n, sketch in enumerate(sketches):
         whole = sketch[...].astype(jnp.float32)
         for row in range(whole.shape[0]):
             lines[n : n + 1, row * LANES : (row + 1) * LANES] = whole[row : row + 1, :]
     left = lines[...].astype(jnp.bfloat16)
-    for n, tests in enumerate([own_tests] + [near_tests.at[s] for s in range(near_tests.shape[0])]):
-        found = lax.dot_general(
-            left, tests[...], (((1,), (1,)), ((), ())), preferred_element_type=jnp.float32
-        )
-        found = found[: len(sketches)] * scale
-        out_ref[:, n * tests.shape[0] : (n + 1) * tests.shape[0]] = found
+    total = jnp.zeros(out_ref.shape, jnp.float32)
+    for cut in range(cuts):
+        for copy in copies[cut]:
+            copy.wait()
+        columns = slice(cut * wide, (cut + 1) * wide)
+        total += lax.dot_general(
+            held[:, columns],
+            left[:, columns],
+            (((1,), (1,)), ((), ())),
+            preferred_element_type=jnp.float32,
+        )
+    out_ref[...] = total * scale
 
 
 def scores_of(sketches, own_tests, near_tests, scale):
     tests, kept = own_tests.shape
-    count = len(sketches)
-    return pl.pallas_call(
-        functools.partial(score_kernel, scale=scale),
-        out_shape=jax.ShapeDtypeStruct((count, tests * (1 + near_tests.shape[0])), jnp.float32),
-        scratch_shapes=[pltpu.VMEM((16, kept), jnp.float32)],
-        compiler_params=pltpu.CompilerParams(vmem_limit_bytes=32 * 1024 * 1024),
+    places = 1 + near_tests.shape[0]
+    cuts = 4
+    found = pl.pallas_call(
+        functools.partial(score_kernel, scale=scale, cuts=cuts),
+        out_shape=jax.ShapeDtypeStruct((places * tests, PACK), jnp.float32),
+        in_specs=[pl.BlockSpec(memory_space=pltpu.VMEM)] * len(sketches)
+        + [pl.BlockSpec(memory_space=pl.ANY)] * 2,
+        out_specs=pl.BlockSpec(memory_space=pltpu.VMEM),
+        scratch_shapes=[
+            pltpu.VMEM((PACK, kept), jnp.float32),
+            pltpu.VMEM((places * tests, kept), jnp.bfloat16),
+            pltpu.SemaphoreType.DMA((places, cuts)),
+        ],
+        compiler_params=pltpu.CompilerParams(vmem_limit_bytes=62 * 1024 * 1024),
         name="scores",
     )(*sketches, own_tests, near_tests)
+    return found.T[: len(sketches)]
 
 
 def on_device(gradients, sign_words, sub_index, test_sketch, *, mesh):

time: 97.9 us -> 104 us (1.062)
  waiting for transfers between devices: 10.4 us -> 16 us
    ppermute x10, waiting for transfers between devices: 10.4 us -> 16 us  [swapped(): return lax.ppermute(value, axis, [(i, i ^ bits) for i in range(size)])]
    pallas_call x1, Pallas kernels: 2.78 us -> 5.4 us  [scores_of(): pl.pallas_call(functools.partial(score_kernel, scale=scale, cuts=cuts), o...]
    pallas_call x1, Pallas kernels: 67.7 us -> 65.1 us  [partial_sketch(): pl.pallas_call(functools.partial(sketch_kernel, high_dev=high_dev, scale=...]
    slice x1, local copies, waits for them, and re-layouts: 0.01 us -> 1.41 us  [on_device(): scores[:1]]
  transfers between devices with their start and end apart: 10 -> 10, of which waited for: 6 -> 6; matrix products, arithmetic and copies ran while one was open for 1% -> 1% of each run, Pallas kernels for 69% -> 63%
where the time goes in v9:
time: 104 us
  Pallas kernels  70.5 us (68%)
  waiting for transfers between devices  16 us (15%)
  starting transfers between devices  13.8 us (13%)
  local copies, waits for them, and re-layouts  2.01 us (2%)
  other arithmetic  1.71 us (2%)
    pallas_call x1, Pallas kernels, partial_sketch(): pl.pallas_call(functools.partial(sketch_kernel, high_dev=high_dev, scale=...  65.1 us
    ppermute x10, waiting for transfers between devices, swapped(): return lax.ppermute(value, axis, [(i, i ^ bits) for i in range(size)])  16 us
    ppermute x10, starting transfers between devices, swapped(): return lax.ppermute(value, axis, [(i, i ^ bits) for i in range(size)])  13.8 us
    pallas_call x1, Pallas kernels, scores_of(): pl.pallas_call(functools.partial(score_kernel, scale=scale, cuts=cuts), o...  5.4 us
  transfers between devices with their start and end apart: 10, of which 6 were waited for; matrix products, arithmetic and copies ran while one was open for 1% of the time, Pallas kernels for 63%

profile of v9, /device:TPU:0, one launch (start us, length us, event | category | flops | bytes accessed | tf_op | source)
XLA Modules:
  0.0 104.1 jit_solution(5145337913595695259)
XLA Ops:
  0.0 2.9 %collective-permute-start.6 = (bf16[128,8192]{1,0:T(8,128)(2,1)}, bf16[128,8192]{1,0:T(8,128)(2,1)}, u32[]{:S(2)}, u32[]{:S(2)}) collective-permute-start(bf16[128,8192]{1,0:T(8,128)(2,1)} %refs_4_.1), channel_id=1, source_target_pairs={{0,1},{1,0},{2,3},{3,2},{4,5},{5,4},{6,7},{7,6},{8,9},{9,8},{10,11... | collective-permute-start | bytes 6291464 | tf_op jit(solution)/shard_map/ppermute | solution.py:288
  2.9 65.1 %sketch.1 = f32[64,128]{1,0:T(8,128)} custom-call(s32[1]{0:T(128)} %bitcast.place_ref, bf16[256,8,32,1,256]{4,3,2,1,0:T(2,128)(2,1)} %bitcast.1.grads, s32[256,32,1,128]{3,2,1,0:T(1,128)} %bitcast.14, s32[64,128]{1,0:T(8,128)} %bitcast.16), custom_call_target="tpu_custom_call" | custom-call | flops 17179869184 | bytes 67108864 | tf_op jit(solution)/shard_map/sketch/pallas_call | solution.py:252
  68.1 0.1 collective-permute-start
  68.2 1.6 %collective-permute-start.1 = (f32[64,128]{1,0:T(8,128)}, f32[64,128]{1,0:T(8,128)S(1)}, u32[]{:S(2)}, u32[]{:S(2)}) collective-permute-start(f32[64,128]{1,0:T(8,128)} %sketch.1), channel_id=1, source_target_pairs={{0,16},{8,24},{16,0},{24,8},{1,17},{9,25},{17,1},{25,9},{2,18},{10... | collective-permute-start | bytes 98312 | tf_op jit(solution)/shard_map/ppermute | solution.py:288
  69.7 0.3 collective-permute-start.2
  70.0 0.0 collective-permute-done
  70.0 2.3 %collective-permute-done.1 = f32[64,128]{1,0:T(8,128)S(1)} collective-permute-done((f32[64,128]{1,0:T(8,128)}, f32[64,128]{1,0:T(8,128)S(1)}, u32[]{:S(2)}, u32[]{:S(2)}) %collective-permute-start.1) | collective-permute-done | bytes 32800 | tf_op jit(solution)/shard_map/ppermute | solution.py:288
  72.3 0.9 collective-permute-done.2
  73.3 0.8 add_convert_fusion.refs_0_
  74.1 0.0 copy-start
  74.1 1.6 %collective-permute-start.3 = (bf16[64,128]{1,0:T(8,128)(2,1)S(1)}, bf16[64,128]{1,0:T(8,128)(2,1)S(1)}, u32[]{:S(2)}, u32[]{:S(2)}) collective-permute-start(bf16[64,128]{1,0:T(8,128)(2,1)S(1)} %add_convert_fusion.refs_0_), channel_id=1, source_target_pairs={{0,2},{2,0},{4,6},{6,4},{1,3},{3,1},{5,7},{7,5},{8,10},{10,8},{12,... | collective-permute-start | bytes 49160 | tf_op jit(solution)/shard_map/ppermute | solution.py:288
  75.7 2.6 %collective-permute-start.4 = (bf16[64,128]{1,0:T(8,128)(2,1)S(1)}, bf16[64,128]{1,0:T(8,128)(2,1)S(1)}, u32[]{:S(2)}, u32[]{:S(2)}) collective-permute-start(bf16[64,128]{1,0:T(8,128)(2,1)S(1)} %add_convert_fusion.refs_0_), channel_id=1, source_target_pairs={{0,4},{2,6},{4,0},{6,2},{1,5},{3,7},{5,1},{7,3},{8,12},{10,14},{12... | collective-permute-start | bytes 49160 | tf_op jit(solution)/shard_map/ppermute | solution.py:288
  78.3 0.2 collective-permute-start.5
  78.5 0.0 collective-permute-done.3.refs_1_
  78.5 0.0 copy-start.1
  78.5 1.9 %collective-permute-done.4.refs_2_ = bf16[64,128]{1,0:T(8,128)(2,1)S(1)} collective-permute-done((bf16[64,128]{1,0:T(8,128)(2,1)S(1)}, bf16[64,128]{1,0:T(8,128)(2,1)S(1)}, u32[]{:S(2)}, u32[]{:S(2)}) %collective-permute-start.4) | collective-permute-done | bytes 16416 | tf_op jit(solution)/shard_map/ppermute | solution.py:288
  80.4 0.0 copy-start.2
  80.4 3.4 %collective-permute-done.5.refs_3_ = bf16[64,128]{1,0:T(8,128)(2,1)S(1)} collective-permute-done((bf16[64,128]{1,0:T(8,128)(2,1)S(1)}, bf16[64,128]{1,0:T(8,128)(2,1)S(1)}, u32[]{:S(2)}, u32[]{:S(2)}) %collective-permute-start.5) | collective-permute-done | bytes 16416 | tf_op jit(solution)/shard_map/ppermute | solution.py:288
  83.8 0.0 copy-start.3
  83.8 0.0 collective-permute-done.6
  83.8 0.0 copy-done
  83.8 0.0 copy-done.1
  83.9 0.0 copy-done.2
  83.9 0.6 copy-done.3
  84.4 5.4 %scores.1 = f32[256,16]{1,0:T(8,128)} custom-call(bf16[64,128]{1,0:T(8,128)(2,1)} %copy-done, bf16[64,128]{1,0:T(8,128)(2,1)} %copy-done.1, bf16[64,128]{1,0:T(8,128)(2,1)} %copy-done.2, bf16[64,128]{1,0:T(8,128)(2,1)} %copy-done.3, bf16[128,8192]{1,0:T(8,128)(2,1)} %refs_4_.1, bf16[1,128,8192]{2,1,0:T(8,128)(2,1)} %bitcast.4.refs_5_), custom_call_target="tpu_custom_call" | custom-call | tf_op jit(solution)/shard_map/scores/pallas_call | solution.py:333
  89.8 1.4 %slice_reduce_fusion = (f32[256]{0:T(256)S(1)}, f32[1,256]{0,1:T(8,128)S(1)}, f32[1,256]{0,1:T(8,128)S(1)}, f32[1,256]{0,1:T(8,128)S(1)}) fusion(f32[16,256]{0,1:T(8,128)} %bitcast.15), kind=kLoop, calls=%fused_computation | loop fusion | bytes 8192 | tf_op jit(solution)/shard_map/slice | solution.py:368
  91.3 0.1 collective-permute-start.7
  91.3 0.8 collective-permute-start.8
  92.1 3.6 %collective-permute-start.9 = (f32[1,256]{0,1:T(8,128)S(1)}, f32[1,256]{0,1:T(8,128)S(1)}, u32[]{:S(2)}, u32[]{:S(2)}) collective-permute-start(f32[1,256]{0,1:T(8,128)S(1)} %get-tuple-element.6), channel_id=1, source_target_pairs={{0,6},{2,4},{4,2},{6,0},{1,7},{3,5},{5,3},{7,1},{8,14},{10,12},{12... | collective-permute-start | bytes 3080 | tf_op jit(solution)/shard_map/ppermute | solution.py:288
  95.7 2.1 %collective-permute-done.7 = f32[1,256]{0,1:T(8,128)S(1)} collective-permute-done((f32[1,256]{0,1:T(8,128)S(1)}, f32[1,256]{0,1:T(8,128)S(1)}, u32[]{:S(2)}, u32[]{:S(2)}) %collective-permute-start.7) | collective-permute-done | bytes 1056 | tf_op jit(solution)/shard_map/ppermute | solution.py:288
  97.8 0.1 reduce.1
  97.9 5.3 %collective-permute-done.8 = f32[1,256]{0,1:T(8,128)S(1)} collective-permute-done((f32[1,256]{0,1:T(8,128)S(1)}, f32[1,256]{0,1:T(8,128)S(1)}, u32[]{:S(2)}, u32[]{:S(2)}) %collective-permute-start.8) | collective-permute-done | bytes 1056 | tf_op jit(solution)/shard_map/ppermute | solution.py:288
  103.2 0.1 reduce.2
  103.3 0.0 collective-permute-done.9
  103.3 0.1 reduce.3
  103.5 0.6 reverse_select_fusion
  (4 shorter events, 0.1 us)
Async XLA Ops:
  0.0 83.8 %collective-permute-start.6 = (bf16[128,8192]{1,0:T(8,128)(2,1)}, bf16[128,8192]{1,0:T(8,128)(2,1)}, u32[]{:S(2)}, u32[]{:S(2)}) collective-permute-start(bf16[128,8192]{1,0:T(8,128)(2,1)} %refs_4_.1), channel_id=1, source_target_pairs={{0,1},{1,0},{2,3},{3,2},{4,5},{5,4},{6,7},{7,6},{8,9},{9,8},{10,11... | collective-permute-start | bytes 6291464 | tf_op jit(solution)/shard_map/ppermute | solution.py:288
  68.1 1.9 %collective-permute-start = (f32[64,128]{1,0:T(8,128)}, f32[64,128]{1,0:T(8,128)S(1)}, u32[]{:S(2)}, u32[]{:S(2)}) collective-permute-start(f32[64,128]{1,0:T(8,128)} %sketch.1), channel_id=1, source_target_pairs={{0,8},{8,0},{16,24},{24,16},{1,9},{9,1},{17,25},{25,17},{2,10},{10... | collective-permute-start | bytes 98312 | tf_op jit(solution)/shard_map/ppermute | solution.py:288
  68.2 4.2 %collective-permute-start.1 = (f32[64,128]{1,0:T(8,128)}, f32[64,128]{1,0:T(8,128)S(1)}, u32[]{:S(2)}, u32[]{:S(2)}) collective-permute-start(f32[64,128]{1,0:T(8,128)} %sketch.1), channel_id=1, source_target_pairs={{0,16},{8,24},{16,0},{24,8},{1,17},{9,25},{17,1},{25,9},{2,18},{10... | collective-permute-start | bytes 98312 | tf_op jit(solution)/shard_map/ppermute | solution.py:288
  69.7 3.6 %collective-permute-start.2 = (f32[64,128]{1,0:T(8,128)}, f32[64,128]{1,0:T(8,128)S(1)}, u32[]{:S(2)}, u32[]{:S(2)}) collective-permute-start(f32[64,128]{1,0:T(8,128)} %sketch.1), channel_id=1, source_target_pairs={{0,24},{8,16},{16,8},{24,0},{1,25},{9,17},{17,9},{25,1},{2,26},{10... | collective-permute-start | bytes 98312 | tf_op jit(solution)/shard_map/ppermute | solution.py:288
  74.1 9.8 %copy-start = (bf16[64,128]{1,0:T(8,128)(2,1)}, bf16[64,128]{1,0:T(8,128)(2,1)S(1)}, u32[]{:S(2)}) copy-start(bf16[64,128]{1,0:T(8,128)(2,1)S(1)} %add_convert_fusion.refs_0_) | copy-start | bytes 49156
  74.1 4.5 %collective-permute-start.3 = (bf16[64,128]{1,0:T(8,128)(2,1)S(1)}, bf16[64,128]{1,0:T(8,128)(2,1)S(1)}, u32[]{:S(2)}, u32[]{:S(2)}) collective-permute-start(bf16[64,128]{1,0:T(8,128)(2,1)S(1)} %add_convert_fusion.refs_0_), channel_id=1, source_target_pairs={{0,2},{2,0},{4,6},{6,4},{1,3},{3,1},{5,7},{7,5},{8,10},{10,8},{12,... | collective-permute-start | bytes 49160 | tf_op jit(solution)/shard_map/ppermute | solution.py:288
  75.7 4.7 %collective-permute-start.4 = (bf16[64,128]{1,0:T(8,128)(2,1)S(1)}, bf16[64,128]{1,0:T(8,128)(2,1)S(1)}, u32[]{:S(2)}, u32[]{:S(2)}) collective-permute-start(bf16[64,128]{1,0:T(8,128)(2,1)S(1)} %add_convert_fusion.refs_0_), channel_id=1, source_target_pairs={{0,4},{2,6},{4,0},{6,2},{1,5},{3,7},{5,1},{7,3},{8,12},{10,14},{12... | collective-permute-start | bytes 49160 | tf_op jit(solution)/shard_map/ppermute | solution.py:288
  78.3 5.5 %collective-permute-start.5 = (bf16[64,128]{1,0:T(8,128)(2,1)S(1)}, bf16[64,128]{1,0:T(8,128)(2,1)S(1)}, u32[]{:S(2)}, u32[]{:S(2)}) collective-permute-start(bf16[64,128]{1,0:T(8,128)(2,1)S(1)} %add_convert_fusion.refs_0_), channel_id=1, source_target_pairs={{0,6},{2,4},{4,2},{6,0},{1,7},{3,5},{5,3},{7,1},{8,14},{10,12},{12... | collective-permute-start | bytes 49160 | tf_op jit(solution)/shard_map/ppermute | solution.py:288
  78.5 5.3 %copy-start.1 = (bf16[64,128]{1,0:T(8,128)(2,1)}, bf16[64,128]{1,0:T(8,128)(2,1)S(1)}, u32[]{:S(2)}) copy-start(bf16[64,128]{1,0:T(8,128)(2,1)S(1)} %collective-permute-done.3.refs_1_) | copy-start | bytes 49156
  80.4 3.4 %copy-start.2 = (bf16[64,128]{1,0:T(8,128)(2,1)}, bf16[64,128]{1,0:T(8,128)(2,1)S(1)}, u32[]{:S(2)}) copy-start(bf16[64,128]{1,0:T(8,128)(2,1)S(1)} %collective-permute-done.4.refs_2_) | copy-start | bytes 49156
  83.8 0.6 copy-start.3
  91.3 6.6 %collective-permute-start.7 = (f32[1,256]{0,1:T(8,128)S(1)}, f32[1,256]{0,1:T(8,128)S(1)}, u32[]{:S(2)}, u32[]{:S(2)}) collective-permute-start(f32[1,256]{0,1:T(8,128)S(1)} %get-tuple-element.8), channel_id=1, source_target_pairs={{0,2},{2,0},{4,6},{6,4},{1,3},{3,1},{5,7},{7,5},{8,10},{10,8},{12,... | collective-permute-start | bytes 3080 | tf_op jit(solution)/shard_map/ppermute | solution.py:288
  91.3 11.9 %collective-permute-start.8 = (f32[1,256]{0,1:T(8,128)S(1)}, f32[1,256]{0,1:T(8,128)S(1)}, u32[]{:S(2)}, u32[]{:S(2)}) collective-permute-start(f32[1,256]{0,1:T(8,128)S(1)} %get-tuple-element.7), channel_id=1, source_target_pairs={{0,4},{2,6},{4,0},{6,2},{1,5},{3,7},{5,1},{7,3},{8,12},{10,14},{12... | collective-permute-start | bytes 3080 | tf_op jit(solution)/shard_map/ppermute | solution.py:288
  92.1 11.2 %collective-permute-start.9 = (f32[1,256]{0,1:T(8,128)S(1)}, f32[1,256]{0,1:T(8,128)S(1)}, u32[]{:S(2)}, u32[]{:S(2)}) collective-permute-start(f32[1,256]{0,1:T(8,128)S(1)} %get-tuple-element.6), channel_id=1, source_target_pairs={{0,6},{2,4},{4,2},{6,0},{1,7},{3,5},{5,3},{7,1},{8,14},{10,12},{12... | collective-permute-start | bytes 3080 | tf_op jit(solution)/shard_map/ppermute | solution.py:288

commit v10 on v6

v10 whole, which is shorter than its diff:
```python
import functools

import jax
import jax.numpy as jnp
from jax import lax
from jax.experimental import pallas as pl
from jax.experimental.pallas import tpu as pltpu
from jax.sharding import Mesh, PartitionSpec as P

NMID = 256
NLOW = 256
TOP = 8
REST = NMID // TOP
TURN = 4
SLOTS = 3
LANES = 128
PACK = 16


def odd_common_bits(left, right):
    return jnp.bitwise_and(lax.population_count(jnp.bitwise_and(left, right)), 1) == 1


def iota(shape, axis):
    return lax.broadcasted_iota(jnp.int32, shape, axis)


def sketch_kernel(
    place_ref, grads, words, sub_ref, out_ref,
    xbuf, wbuf, wpair, low_table, high_table, signed0, signed1, first0, first1, spots, signs, acc, sems, wsem,
    *, high_dev, scale,
):
    high_parts = out_ref.shape[0] * LANES // TOP // high_dev
    groups = high_dev // PACK
    per_high = words.shape[1]
    turns = REST // TURN
    copies = high_dev // turns
    half = LANES // 16
    signed, first = (signed0, signed1), (first0, first1)

    def grad_copy(step, h):
        slot = lax.rem(step, SLOTS)
        return pltpu.make_async_copy(
            grads.at[h, step],
            xbuf.at[slot, :, :, pl.ds(pl.multiple_of(h * LANES, LANES), LANES)],
            sems.at[slot],
        )

    def start_copies(step):
        @pl.loop(0, high_dev // 8)
        def _(n):
            for i in range(8):
                grad_copy(step, n * 8 + i).start()

    def wait_copies(step):
        slot = lax.rem(step, SLOTS)
        pltpu.make_async_copy(xbuf.at[slot], xbuf.at[slot], sems.at[slot]).wait()

    word_copy = pltpu.make_async_copy(words, wbuf.at[:, :per_high], wsem)
    word_copy.start()
    start_copies(0)
    start_copies(1)

    for table in (low_table, high_table):
        table[...] = jnp.where(
            odd_common_bits(iota(table.shape, 0), iota(table.shape, 1)), -1.0, 1.0
        ).astype(jnp.bfloat16)
    acc[...] = jnp.zeros_like(acc)
    lane16 = iota((PACK, LANES), 1)
    row16 = iota((PACK, LANES), 0)

    @pl.loop(0, groups)
    def _(g):
        entry = jnp.zeros((PACK, LANES), jnp.int32)
        for hi in range(high_parts):
            line = jnp.broadcast_to(sub_ref[pl.ds(hi * groups + g, 1), :], (PACK, LANES))
            taken = jnp.take_along_axis(line, row16 * TOP + lane16 % TOP, axis=1, mode="promise_in_bounds")
            entry = jnp.where(lane16 // TOP == hi, taken, entry)
        rows = pl.ds(pl.multiple_of(g * PACK, PACK), PACK)
        spots[rows, :] = jnp.bitwise_and(entry, NLOW - 1)
        for mid in range(REST):
            signs[mid, rows, :] = jnp.where(odd_common_bits(entry, mid * NLOW), -1.0, 1.0)

    word_copy.wait()
    lines = wbuf.reshape(high_dev * (per_high + 1), 1, LANES)

    @pl.loop(0, high_dev // 8)
    def _(n):
        for pair in range(per_high // 2):
            one, two = (
                lines[pl.ds(n * 8 * (per_high + 1) + 2 * pair + which, 8, per_high + 1), 0, :]
                for which in range(2)
            )
            wpair[pair, pl.ds(pl.multiple_of(n * 8, 8), 8), :] = jnp.bitwise_or(
                one, jnp.left_shift(two, 16)
            )

    def prepare(n, parity):
        step, i = n // turns, lax.rem(n, turns)
        slot = lax.rem(step, SLOTS)
        bits = [jnp.left_shift(1, lane16 % 16), jnp.left_shift(1, lane16 % 16 + 16)]
        for block in range(groups):
            rows = slice(block * PACK, (block + 1) * PACK)
            columns = slice(block * PACK * LANES, (block + 1) * PACK * LANES)
            for pair in range(TURN // 2):
                packed = wpair[step * (TURN // 2) + pair, rows, :]
                for l_hi in range(2):
                    spot = i * 16 + l_hi * half + lane16 // 16
                    word = jnp.take_along_axis(packed, spot, axis=1, mode="promise_in_bounds")
                    for which in range(2):
                        c = 2 * pair + which
                        value = xbuf[slot, (c * turns + i) * 2 + l_hi, :, columns]
                        value = value.reshape(PACK, LANES).astype(jnp.float32)
                        value = jnp.where(jnp.bitwise_and(word, bits[which]) != 0, value, -value)
                        signed[parity][
                            c * high_dev + block * PACK : c * high_dev + (block + 1) * PACK,
                            l_hi * LANES : (l_hi + 1) * LANES,
                        ] = value.astype(jnp.bfloat16)

    def transform_low(parity):
        first[parity][...] = jnp.dot(
            signed[parity][...], low_table[...], preferred_element_type=jnp.float32
        ).astype(jnp.bfloat16)

    def transform_high(n, parity, c):
        step, i = n // turns, lax.rem(n, turns)
        found = jnp.dot(
            high_table[...],
            first[parity][c * high_dev : (c + 1) * high_dev, :],
            preferred_element_type=jnp.float32,
        )
        spot = spots[...]
        low = jnp.bitwise_and(spot, LANES - 1)
        zero = jnp.take_along_axis(found[:, :LANES], low, axis=1, mode="promise_in_bounds")
        one = jnp.take_along_axis(found[:, LANES:], low, axis=1, mode="promise_in_bounds")
        acc[step, c] += jnp.where(spot >= LANES, one, zero) * signs[c * turns + i]

    def turn(n, parity, with_prepare, with_low, with_copies):
        if with_prepare:

            @pl.when(lax.rem(n + 2, turns) == 0)
            def _():
                wait_copies((n + 2) // turns)

        if with_copies:
            for m in range(copies):
                grad_copy((n + 2) // turns + 2, lax.rem(n + 2, turns) * copies + m).start()
        for c in range(TURN):
            transform_high(n, parity, c)
        if with_low:
            transform_low(1 - parity)
        if with_prepare:
            prepare(n + 2, parity)

    wait_copies(0)
    for n in range(2):
        for m in range(copies):
            grad_copy(2, n * copies + m).start()
        prepare(n, n)
    transform_low(0)

    last = TOP * turns
    ends = last - 2 * turns - 2

    @pl.loop(0, ends // 2)
    def _(n):
        for parity in range(2):
            turn(2 * n + parity, parity, True, True, True)

    @pl.loop(ends // 2, last // 2 - 1)
    def _(n):
        for parity in range(2):
            turn(2 * n + parity, parity, True, True, False)

    turn(last - 2, 0, False, True, False)
    turn(last - 1, 1, False, False, False)

    place = place_ref[0]
    for g in range(groups):
        rows = slice(g * PACK, (g + 1) * PACK)
        total = jnp.zeros((PACK, LANES), jnp.float32)
        for step in range(TOP):
            part = acc[step, 0, rows, :]
            for c in range(1, TURN):
                part += acc[step, c, rows, :]
            total += jnp.where(odd_common_bits(lane16 % TOP, step), -part, part)
        for hi in range(high_parts):
            taken = jnp.take_along_axis(total, hi * TOP + lane16 % TOP, axis=1, mode="promise_in_bounds")
            line = jnp.where(lane16 // TOP == row16, taken, 0.0)
            common = jnp.bitwise_and(place, hi)
            odd = jnp.bitwise_and(common ^ (common >> 1) ^ (common >> 2) ^ (common >> 3), 1)
            sign = jnp.where(odd == 1, -scale, scale)
            out_ref[hi * groups + g : hi * groups + g + 1, :] = jnp.sum(line, axis=0, keepdims=True) * sign


def partial_sketch(gradients, sign_words, sub_index, place, high_dev, scale):
    kept = sub_index.shape[0]
    grads = gradients.reshape(high_dev, TOP, 2 * REST, 1, LANES)
    words = sign_words.reshape(high_dev, -1, 1, LANES)
    return pl.pallas_call(
        functools.partial(sketch_kernel, high_dev=high_dev, scale=scale),
        out_shape=jax.ShapeDtypeStruct((kept // LANES, LANES), jnp.float32),
        in_specs=[
            pl.BlockSpec(memory_space=pltpu.SMEM),
            pl.BlockSpec(memory_space=pl.ANY),
            pl.BlockSpec(memory_space=pl.ANY),
            pl.BlockSpec(memory_space=pltpu.VMEM),
        ],
        out_specs=pl.BlockSpec(memory_space=pltpu.VMEM),
        scratch_shapes=[
            pltpu.VMEM((SLOTS, 2 * REST, 1, high_dev * LANES), jnp.bfloat16),
            pltpu.VMEM((high_dev, words.shape[1] + 1, 1, LANES), jnp.int32),
            pltpu.VMEM((words.shape[1] // 2, high_dev, LANES), jnp.int32),
            pltpu.VMEM((NLOW, NLOW), jnp.bfloat16),
            pltpu.VMEM((high_dev, high_dev), jnp.bfloat16),
            pltpu.VMEM((TURN * high_dev, NLOW), jnp.bfloat16),
            pltpu.VMEM((TURN * high_dev, NLOW), jnp.bfloat16),
            pltpu.VMEM((TURN * high_dev, NLOW), jnp.bfloat16),
            pltpu.VMEM((TURN * high_dev, NLOW), jnp.bfloat16),
            pltpu.VMEM((high_dev, LANES), jnp.int32),
            pltpu.VMEM((REST, high_dev, LANES), jnp.float32),
            pltpu.VMEM((TOP, TURN, high_dev, LANES), jnp.float32),
            pltpu.SemaphoreType.DMA((SLOTS,)),
            pltpu.SemaphoreType.DMA,
        ],
        compiler_params=pltpu.CompilerParams(vmem_limit_bytes=60 * 1024 * 1024),
        cost_estimate=pl.CostEstimate(
            flops=4 * NLOW * high_dev * NMID * NLOW, bytes_accessed=4 * gradients.size, transcendentals=0
        ),
        name="sketch",
    )(place, grads, words, sub_index.reshape(kept // LANES, LANES))


def swapped(value, axis, size, bits):
    return lax.ppermute(value, axis, [(i, i ^ bits) for i in range(size)])


def score_kernel(*refs, scale):
    *sketches, own_tests, near_tests, out_ref, lines = refs
    for n, sketch in enumerate(sketches):
        whole = sketch[...].astype(jnp.float32)
        for row in range(whole.shape[0]):
            lines[n : n + 1, row * LANES : (row + 1) * LANES] = whole[row : row + 1, :]
    left = lines[...].astype(jnp.bfloat16)
    for n, tests in enumerate([own_tests] + [near_tests.at[s] for s in range(near_tests.shape[0])]):
        found = lax.dot_general(
            left, tests[...], (((1,), (1,)), ((), ())), preferred_element_type=jnp.float32
        )
        found = found[: len(sketches)] * scale
        out_ref[:, n * tests.shape[0] : (n + 1) * tests.shape[0]] = found


def scores_of(sketches, own_tests, near_tests, scale):
    tests, kept = own_tests.shape
    count = len(sketches)
    return pl.pallas_call(
        functools.partial(score_kernel, scale=scale),
        out_shape=jax.ShapeDtypeStruct((count, tests * (1 + near_tests.shape[0])), jnp.float32),
        scratch_shapes=[pltpu.VMEM((16, kept), jnp.float32)],
        compiler_params=pltpu.CompilerParams(vmem_limit_bytes=32 * 1024 * 1024),
        name="scores",
    )(*sketches, own_tests, near_tests)


def on_device(gradients, sign_words, sub_index, test_sketch, *, mesh):
    feat_size, far_size, near_size = (mesh.shape[axis] for axis in ("feat", "far", "near"))
    local_features = gradients.shape[1]
    kept = sub_index.shape[0]
    tests = test_sketch.shape[0]
    high_dev = local_features // (NMID * NLOW)
    feature_scale = float(local_features * feat_size) ** (-0.5)
    score_scale = float(kept) ** (-0.5)
    place = lax.axis_index("feat").astype(jnp.int32).reshape(1)
    near_tests = jnp.stack([swapped(test_sketch, "near", near_size, s) for s in range(1, near_size)])
    shares = partial_sketch(gradients, sign_words, sub_index, place, high_dev, feature_scale)
    sketch = shares
    for s in range(1, feat_size):
        sketch = sketch + swapped(shares, "feat", feat_size, s)
    sketch = sketch.astype(jnp.bfloat16)
    sketches = [sketch] + [swapped(sketch, "far", far_size, s) for s in range(1, far_size)]
    scores = scores_of(sketches, test_sketch, near_tests, score_scale)
    scores = jnp.stack(
        [scores[:1]] + [swapped(scores[s : s + 1], "far", far_size, s) for s in range(1, far_size)]
    )
    scores = scores.reshape(far_size, near_size, tests)
    far, near = lax.axis_index("far"), lax.axis_index("near")
    for b in range(near_size.bit_length() - 1):
        split = scores.reshape(far_size, -1, 2, 1 << b, tests)
        scores = jnp.where(jnp.bitwise_and(near, 1 << b) != 0, split[:, :, ::-1], split)
    for b in range(far_size.bit_length() - 1):
        split = scores.reshape(-1, 2, 1 << b, near_size, tests)
        scores = jnp.where(jnp.bitwise_and(far, 1 << b) != 0, split[:, ::-1], split)
    return scores.reshape(1, -1)


def solution(mesh):
    feat_size, ex_size = mesh.shape["feat"], mesh.shape["ex"]
    far_size = min(4, ex_size)
    mesh = Mesh(mesh.devices.reshape(feat_size, far_size, ex_size // far_size), ("feat", "far", "near"))
    ex = ("far", "near")
    return jax.shard_map(
        functools.partial(on_device, mesh=mesh),
        mesh=mesh,
        in_specs=(P(ex, "feat"), P("feat"), P(), P(ex, None)),
        out_specs=P(ex, None),
        check_vma=False,
    )
```

time: 96 us -> 110 us (1.15)
  Pallas kernels: 68.5 us -> 84.1 us
  local copies, waits for them, and re-layouts: 1.63 us -> 0.04 us
    pallas_call x1, Pallas kernels: 65.7 us -> 81.3 us  [partial_sketch(): pl.pallas_call(functools.partial(sketch_kernel, high_dev=high_dev, scale=...]
    unnamed x2, local copies, waits for them, and re-layouts: 1.59 us -> 0.01 us
  transfers between devices with their start and end apart: 10 -> 10, of which waited for: 6 -> 6; matrix products, arithmetic and copies ran while one was open for 1% -> 1% of each run, Pallas kernels for 69% -> 74%
where the time goes in v10:
time: 110 us
  Pallas kernels  84.1 us (76%)
  starting transfers between devices  13.7 us (12%)
  waiting for transfers between devices  10.4 us (9%)
  other arithmetic  1.39 us (1%)
    pallas_call x1, Pallas kernels, partial_sketch(): pl.pallas_call(functools.partial(sketch_kernel, high_dev=high_dev, scale=...  81.3 us
    ppermute x10, starting transfers between devices, swapped(): return lax.ppermute(value, axis, [(i, i ^ bits) for i in range(size)])  13.7 us
    ppermute x10, waiting for transfers between devices, swapped(): return lax.ppermute(value, axis, [(i, i ^ bits) for i in range(size)])  10.4 us
    pallas_call x1, Pallas kernels, scores_of(): pl.pallas_call(functools.partial(score_kernel, scale=scale), out_shape=ja...  2.77 us
  transfers between devices with their start and end apart: 10, of which 6 were waited for; matrix products, arithmetic and copies ran while one was open for 1% of the time, Pallas kernels for 74%

profile of v10, /device:TPU:0, one launch (start us, length us, event | category | flops | bytes accessed | tf_op | source)
XLA Modules:
  0.0 109.7 jit_solution(1354147355004084801)
XLA Ops:
  0.0 2.9 %collective-permute-start.6 = (bf16[128,8192]{1,0:T(8,128)(2,1)}, bf16[128,8192]{1,0:T(8,128)(2,1)}, u32[]{:S(2)}, u32[]{:S(2)}) collective-permute-start(bf16[128,8192]{1,0:T(8,128)(2,1)} %refs_4_.1), channel_id=1, source_target_pairs={{0,1},{1,0},{2,3},{3,2},{4,5},{5,4},{6,7},{7,6},{8,9},{9,8},{10,11... | collective-permute-start | bytes 6291464 | tf_op jit(solution)/shard_map/ppermute | solution.py:235
  2.9 0.0 copy-start
  2.9 81.3 %sketch.1 = f32[64,128]{1,0:T(8,128)} custom-call(s32[1]{0:T(128)} %bitcast.place_ref, bf16[256,8,64,1,128]{4,3,2,1,0:T(2,128)(2,1)} %bitcast.1.grads, s32[256,32,1,128]{3,2,1,0:T(1,128)} %bitcast.13, s32[64,128]{1,0:T(8,128)} %bitcast.14), custom_call_target="tpu_custom_call" | custom-call | flops 17179869184 | bytes 67108864 | tf_op jit(solution)/shard_map/sketch/pallas_call | solution.py:200
  84.3 0.1 collective-permute-start
  84.3 1.6 %collective-permute-start.1 = (f32[64,128]{1,0:T(8,128)}, f32[64,128]{1,0:T(8,128)S(1)}, u32[]{:S(2)}, u32[]{:S(2)}) collective-permute-start(f32[64,128]{1,0:T(8,128)} %sketch.1), channel_id=1, source_target_pairs={{0,16},{8,24},{16,0},{24,8},{1,17},{9,25},{17,1},{25,9},{2,18},{10... | collective-permute-start | bytes 98312 | tf_op jit(solution)/shard_map/ppermute | solution.py:235
  85.9 0.3 collective-permute-start.2
  86.2 0.0 collective-permute-done
  86.2 2.3 %collective-permute-done.1 = f32[64,128]{1,0:T(8,128)S(1)} collective-permute-done((f32[64,128]{1,0:T(8,128)}, f32[64,128]{1,0:T(8,128)S(1)}, u32[]{:S(2)}, u32[]{:S(2)}) %collective-permute-start.1) | collective-permute-done | bytes 32800 | tf_op jit(solution)/shard_map/ppermute | solution.py:235
  88.5 0.9 collective-permute-done.2
  89.5 0.8 add_convert_fusion.refs_0_
  90.3 1.6 %collective-permute-start.3 = (bf16[64,128]{1,0:T(8,128)(2,1)S(1)}, bf16[64,128]{1,0:T(8,128)(2,1)S(1)}, u32[]{:S(2)}, u32[]{:S(2)}) collective-permute-start(bf16[64,128]{1,0:T(8,128)(2,1)S(1)} %add_convert_fusion.refs_0_), channel_id=1, source_target_pairs={{0,2},{2,0},{4,6},{6,4},{1,3},{3,1},{5,7},{7,5},{8,10},{10,8},{12,... | collective-permute-start | bytes 49160 | tf_op jit(solution)/shard_map/ppermute | solution.py:235
  91.9 2.6 %collective-permute-start.4 = (bf16[64,128]{1,0:T(8,128)(2,1)S(1)}, bf16[64,128]{1,0:T(8,128)(2,1)S(1)}, u32[]{:S(2)}, u32[]{:S(2)}) collective-permute-start(bf16[64,128]{1,0:T(8,128)(2,1)S(1)} %add_convert_fusion.refs_0_), channel_id=1, source_target_pairs={{0,4},{2,6},{4,0},{6,2},{1,5},{3,7},{5,1},{7,3},{8,12},{10,14},{12... | collective-permute-start | bytes 49160 | tf_op jit(solution)/shard_map/ppermute | solution.py:235
  94.5 0.2 collective-permute-start.5
  94.7 0.0 collective-permute-done.3.refs_1_
  94.7 1.9 %collective-permute-done.4.refs_2_ = bf16[64,128]{1,0:T(8,128)(2,1)S(1)} collective-permute-done((bf16[64,128]{1,0:T(8,128)(2,1)S(1)}, bf16[64,128]{1,0:T(8,128)(2,1)S(1)}, u32[]{:S(2)}, u32[]{:S(2)}) %collective-permute-start.4) | collective-permute-done | bytes 16416 | tf_op jit(solution)/shard_map/ppermute | solution.py:235
  96.6 3.4 %collective-permute-done.5.refs_3_ = bf16[64,128]{1,0:T(8,128)(2,1)S(1)} collective-permute-done((bf16[64,128]{1,0:T(8,128)(2,1)S(1)}, bf16[64,128]{1,0:T(8,128)(2,1)S(1)}, u32[]{:S(2)}, u32[]{:S(2)}) %collective-permute-start.5) | collective-permute-done | bytes 16416 | tf_op jit(solution)/shard_map/ppermute | solution.py:235
  100.0 0.0 collective-permute-done.6
  100.0 0.0 copy-done
  100.0 2.8 %scores.1 = f32[4,256]{1,0:T(4,128)S(1)} custom-call(bf16[64,128]{1,0:T(8,128)(2,1)S(1)} %add_convert_fusion.refs_0_, bf16[64,128]{1,0:T(8,128)(2,1)S(1)} %collective-permute-done.3.refs_1_, bf16[64,128]{1,0:T(8,128)(2,1)S(1)} %collective-permute-done.4.refs_2_, bf16[64,128]{1,0:T(8,128)(2,1)S(1)} %collective-permute-done.5.refs_3_, ...), custom_call_target="tpu_custom_call" | custom-call | tf_op jit(solution)/shard_map/scores/pallas_call | solution.py:256
  102.8 0.1 collective-permute-start.7
  102.9 0.8 collective-permute-start.8
  103.6 3.6 %collective-permute-start.9 = (f32[1,256]{1,0:T(1,128)S(1)}, f32[1,256]{1,0:T(1,128)S(1)}, u32[]{:S(2)}, u32[]{:S(2)}) collective-permute-start(f32[1,256]{1,0:T(1,128)S(1)} %get-tuple-element.6), channel_id=1, source_target_pairs={{0,6},{2,4},{4,2},{6,0},{1,7},{3,5},{5,3},{7,1},{8,14},{10,12},{12... | collective-permute-start | bytes 3080 | tf_op jit(solution)/shard_map/ppermute | solution.py:235
  107.3 0.0 collective-permute-done.7
  107.3 0.2 collective-permute-done.8
  107.4 1.6 %collective-permute-done.9 = f32[1,256]{1,0:T(1,128)S(1)} collective-permute-done((f32[1,256]{1,0:T(1,128)S(1)}, f32[1,256]{1,0:T(1,128)S(1)}, u32[]{:S(2)}, u32[]{:S(2)}) %collective-permute-start.9) | collective-permute-done | bytes 1056 | tf_op jit(solution)/shard_map/ppermute | solution.py:235
  109.1 0.6 reverse_select_fusion
  (5 shorter events, 0.1 us)
Async XLA Ops:
  0.0 100.0 %collective-permute-start.6 = (bf16[128,8192]{1,0:T(8,128)(2,1)}, bf16[128,8192]{1,0:T(8,128)(2,1)}, u32[]{:S(2)}, u32[]{:S(2)}) collective-permute-start(bf16[128,8192]{1,0:T(8,128)(2,1)} %refs_4_.1), channel_id=1, source_target_pairs={{0,1},{1,0},{2,3},{3,2},{4,5},{5,4},{6,7},{7,6},{8,9},{9,8},{10,11... | collective-permute-start | bytes 6291464 | tf_op jit(solution)/shard_map/ppermute | solution.py:235
  2.9 97.1 %copy-start = (bf16[128,8192]{1,0:T(8,128)(2,1)S(1)}, bf16[128,8192]{1,0:T(8,128)(2,1)}, u32[]{:S(2)}) copy-start(bf16[128,8192]{1,0:T(8,128)(2,1)} %refs_4_.1) | copy-start | bytes 6291460
  84.3 1.9 %collective-permute-start = (f32[64,128]{1,0:T(8,128)}, f32[64,128]{1,0:T(8,128)S(1)}, u32[]{:S(2)}, u32[]{:S(2)}) collective-permute-start(f32[64,128]{1,0:T(8,128)} %sketch.1), channel_id=1, source_target_pairs={{0,8},{8,0},{16,24},{24,16},{1,9},{9,1},{17,25},{25,17},{2,10},{10... | collective-permute-start | bytes 98312 | tf_op jit(solution)/shard_map/ppermute | solution.py:235
  84.3 4.2 %collective-permute-start.1 = (f32[64,128]{1,0:T(8,128)}, f32[64,128]{1,0:T(8,128)S(1)}, u32[]{:S(2)}, u32[]{:S(2)}) collective-permute-start(f32[64,128]{1,0:T(8,128)} %sketch.1), channel_id=1, source_target_pairs={{0,16},{8,24},{16,0},{24,8},{1,17},{9,25},{17,1},{25,9},{2,18},{10... | collective-permute-start | bytes 98312 | tf_op jit(solution)/shard_map/ppermute | solution.py:235
  85.9 3.6 %collective-permute-start.2 = (f32[64,128]{1,0:T(8,128)}, f32[64,128]{1,0:T(8,128)S(1)}, u32[]{:S(2)}, u32[]{:S(2)}) collective-permute-start(f32[64,128]{1,0:T(8,128)} %sketch.1), channel_id=1, source_target_pairs={{0,24},{8,16},{16,8},{24,0},{1,25},{9,17},{17,9},{25,1},{2,26},{10... | collective-permute-start | bytes 98312 | tf_op jit(solution)/shard_map/ppermute | solution.py:235
  90.3 4.5 %collective-permute-start.3 = (bf16[64,128]{1,0:T(8,128)(2,1)S(1)}, bf16[64,128]{1,0:T(8,128)(2,1)S(1)}, u32[]{:S(2)}, u32[]{:S(2)}) collective-permute-start(bf16[64,128]{1,0:T(8,128)(2,1)S(1)} %add_convert_fusion.refs_0_), channel_id=1, source_target_pairs={{0,2},{2,0},{4,6},{6,4},{1,3},{3,1},{5,7},{7,5},{8,10},{10,8},{12,... | collective-permute-start | bytes 49160 | tf_op jit(solution)/shard_map/ppermute | solution.py:235
  91.9 4.7 %collective-permute-start.4 = (bf16[64,128]{1,0:T(8,128)(2,1)S(1)}, bf16[64,128]{1,0:T(8,128)(2,1)S(1)}, u32[]{:S(2)}, u32[]{:S(2)}) collective-permute-start(bf16[64,128]{1,0:T(8,128)(2,1)S(1)} %add_convert_fusion.refs_0_), channel_id=1, source_target_pairs={{0,4},{2,6},{4,0},{6,2},{1,5},{3,7},{5,1},{7,3},{8,12},{10,14},{12... | collective-permute-start | bytes 49160 | tf_op jit(solution)/shard_map/ppermute | solution.py:235
  94.5 5.5 %collective-permute-start.5 = (bf16[64,128]{1,0:T(8,128)(2,1)S(1)}, bf16[64,128]{1,0:T(8,128)(2,1)S(1)}, u32[]{:S(2)}, u32[]{:S(2)}) collective-permute-start(bf16[64,128]{1,0:T(8,128)(2,1)S(1)} %add_convert_fusion.refs_0_), channel_id=1, source_target_pairs={{0,6},{2,4},{4,2},{6,0},{1,7},{3,5},{5,3},{7,1},{8,14},{10,12},{12... | collective-permute-start | bytes 49160 | tf_op jit(solution)/shard_map/ppermute | solution.py:235
  102.8 4.4 %collective-permute-start.7 = (f32[1,256]{1,0:T(1,128)S(1)}, f32[1,256]{1,0:T(1,128)S(1)}, u32[]{:S(2)}, u32[]{:S(2)}) collective-permute-start(f32[1,256]{1,0:T(1,128)S(1)} %get-tuple-element.8), channel_id=1, source_target_pairs={{0,2},{2,0},{4,6},{6,4},{1,3},{3,1},{5,7},{7,5},{8,10},{10,8},{12,... | collective-permute-start | bytes 3080 | tf_op jit(solution)/shard_map/ppermute | solution.py:235
  102.9 4.5 %collective-permute-start.8 = (f32[1,256]{1,0:T(1,128)S(1)}, f32[1,256]{1,0:T(1,128)S(1)}, u32[]{:S(2)}, u32[]{:S(2)}) collective-permute-start(f32[1,256]{1,0:T(1,128)S(1)} %get-tuple-element.7), channel_id=1, source_target_pairs={{0,4},{2,6},{4,0},{6,2},{1,5},{3,7},{5,1},{7,3},{8,12},{10,14},{12... | collective-permute-start | bytes 3080 | tf_op jit(solution)/shard_map/ppermute | solution.py:235
  103.6 5.4 %collective-permute-start.9 = (f32[1,256]{1,0:T(1,128)S(1)}, f32[1,256]{1,0:T(1,128)S(1)}, u32[]{:S(2)}, u32[]{:S(2)}) collective-permute-start(f32[1,256]{1,0:T(1,128)S(1)} %get-tuple-element.6), channel_id=1, source_target_pairs={{0,6},{2,4},{4,2},{6,0},{1,7},{3,5},{5,3},{7,1},{8,14},{10,12},{12... | collective-permute-start | bytes 3080 | tf_op jit(solution)/shard_map/ppermute | solution.py:235

commit v11 on v5

--- a/solution.py
+++ b/solution.py
@@ -33,7 +33,7 @@
     xbuf, wbuf, wpair, table, ybuf0, ybuf1, tbuf0, tbuf1, entries, weights, signs, acc, found_rows, sems, wsem,
     *, high_dev, scale,
 ):
-    high_parts = out_ref.shape[0]
+    high_parts = out_ref.shape[0] * LANES // TOP // high_dev
     rest = NMID // TOP
     chunks = rest // GROUP
     steps = rest // STEP
@@ -42,7 +42,6 @@
     pairs = HALVED * groups
     rounds = GROUP * TOP // PAIR
     highs = high_dev * PAIR // (STEP * TOP)
-    half = LANES // 16
     stride = high_dev + 1
     ybuf = (ybuf0, ybuf1)
     tbuf = (tbuf0, tbuf1)
@@ -57,7 +56,8 @@
             )
             then(copy)
 
-    word_copy = pltpu.make_async_copy(words, wbuf, wsem)
+    per_high = NMID * NLOW // 16 // LANES
+    word_copy = pltpu.make_async_copy(words, wbuf.at[:, :per_high], wsem)
     word_copy.start()
     for step in range(SLOTS):
         grad_copies(step, lambda copy: copy.start())
@@ -92,30 +92,48 @@
         ).astype(jnp.bfloat16)
 
     word_copy.wait()
-    per_high = NMID * NLOW // 16 // LANES
+    lines = wbuf.reshape(high_dev * (per_high + 1), 1, LANES)
+    lane8 = iota((8, LANES), 1)
+
+    def spread(both):
+        value = jnp.take_along_axis(both, lane8 % 16 * 8 + lane8 // 16, axis=1, mode="promise_in_bounds")
+        for reach, keep in ((8, 0x00FF00FF), (4, 0x0F0F0F0F), (2, 0x33333333), (1, 0x55555555)):
+            other = jnp.take_along_axis(value, jnp.bitwise_xor(lane8, reach), axis=1, mode="promise_in_bounds")
+            value = jnp.where(
+                jnp.bitwise_and(lane8, reach) == 0,
+                jnp.bitwise_or(
+                    jnp.bitwise_and(value, keep), jnp.left_shift(jnp.bitwise_and(other, keep), reach)
+                ),
+                jnp.bitwise_or(
+                    jnp.bitwise_and(value, ~keep), jnp.bitwise_and(jnp.right_shift(other, reach), keep)
+                ),
+            )
+        return value
 
     @pl.loop(0, high_dev // 8)
     def _(n):
         for c in range(chunks):
             for pair in range(TOP // 2):
-                one = wbuf[pl.ds(n * 8 * per_high + (2 * pair) * chunks + c, 8, per_high), :]
-                two = wbuf[pl.ds(n * 8 * per_high + (2 * pair + 1) * chunks + c, 8, per_high), :]
-                wpair[c, pair, pl.ds(pl.multiple_of(n * 8, 8), 8), :] = jnp.bitwise_or(
-                    one, jnp.left_shift(two, 16)
+                one, two = (
+                    lines[
+                        pl.ds(n * 8 * (per_high + 1) + (2 * pair + which) * chunks + c, 8, per_high + 1), 0, :
+                    ]
+                    for which in range(2)
                 )
-
-    def prepare(step, u):
+                wpair[c, pair, pl.ds(pl.multiple_of(n * 8, 8), 8), :] = spread(
+                    jnp.bitwise_or(one, jnp.left_shift(two, 16))
+                )
+
+    def prepare(step, u, part, parts):
         slot = step % SLOTS
         chunk = step * STEP // GROUP
-        lane8 = iota((ROWS, LANES), 1)
-        bits = [jnp.left_shift(1, lane8 % 16), jnp.left_shift(1, lane8 % 16 + 16)]
-        spot = step % (GROUP // STEP) * (16 * STEP) + iota((ROWS, LANES), 0) * half + lane8 // 16
-        for n in range(highs):
+        row = step % (GROUP // STEP) * ROWS + iota((ROWS, LANES), 0)
+        bits = [jnp.left_shift(1, row), jnp.left_shift(1, row + 16)]
+        for n in range(part * highs // parts, (part + 1) * highs // parts):
             h = u * highs + n
             values = []
             for pair in range(TOP // 2):
                 word = jnp.broadcast_to(wpair[chunk, pair, pl.ds(h, 1), :], (ROWS, LANES))
-                word = jnp.take_along_axis(word, spot, axis=1, mode="promise_in_bounds")
                 two = xbuf[slot, h, :, 2 * pair * ROWS * LANES : 2 * (pair + 1) * ROWS * LANES]
                 two = two.reshape(2 * ROWS, LANES).astype(jnp.float32)
                 for which in range(2):
@@ -131,21 +149,18 @@
             for top in range(TOP):
                 ybuf[step % 2][top, pl.ds(h, ROWS, stride), :] = values[top]
 
-    def transform_high(step, u):
-        first, i = u * PAIR % TOP, u * PAIR // TOP
+    def transform_high(step, u, n):
+        top, i = u * PAIR % TOP + n, u * PAIR // TOP
         columns = [
-            ybuf[step % 2][first + n, pl.ds((2 * i + l_hi) * stride, high_dev), :].astype(jnp.bfloat16)
-            for n in range(PAIR)
+            ybuf[step % 2][top, pl.ds((2 * i + l_hi) * stride, high_dev), :].astype(jnp.bfloat16)
             for l_hi in range(2)
         ]
         result = jnp.dot(
             table[...], jnp.concatenate(columns, axis=1), preferred_element_type=jnp.float32
-        ).astype(jnp.bfloat16)
+        )
         chunk = step * STEP // GROUP
         row = step % (GROUP // STEP) * STEP + i
-        for n in range(PAIR):
-            top = first + n
-            tbuf[chunk % 2][top // 2, n % 2 * GROUP + row] = result[:, n * NLOW : (n + 1) * NLOW]
+        tbuf[chunk % 2][top // 2, n % 2 * GROUP + row] = result.astype(jnp.bfloat16)
 
     def evaluate(chunk, e):
         j, g = e // groups, e % groups
@@ -158,12 +173,12 @@
             total += found[n * PACK : (n + 1) * PACK] * signs[e, n : n + 1, :]
         acc[e] += total * signs[e, 2 * GROUP + chunk : 2 * GROUP + chunk + 1, :]
 
-    def some_pairs(n, do):
-        if pairs >= rounds:
-            for m in range(pairs // rounds):
-                do(n * (pairs // rounds) + m)
-        else:
-            pl.when(n < pairs)(lambda: do(n))
+    def some_pairs(n, part, do):
+        if pairs >= PAIR * rounds:
+            for m in range(pairs // (PAIR * rounds)):
+                do((n * PAIR + part) * (pairs // (PAIR * rounds)) + m)
+        elif part % (PAIR * rounds // pairs) == 0:
+            do((n * PAIR + part) // (PAIR * rounds // pairs))
 
     turns = STEP * TOP // PAIR
     per_chunk = GROUP // STEP
@@ -172,7 +187,7 @@
 
     @pl.loop(0, turns)
     def _(u):
-        prepare(0, u)
+        prepare(0, u, 0, 1)
 
     for step in range(steps):
         if step + SLOTS < steps:
@@ -182,13 +197,18 @@
 
         @pl.loop(0, turns)
         def _(u):
-            if step >= per_chunk:
-                some_pairs(step % per_chunk * turns + u, functools.partial(evaluate, step // per_chunk - 1))
-            else:
-                some_pairs(step * turns + u, build)
-            transform_high(step, u)
-            if step + 1 < steps:
-                prepare(step + 1, u)
+            for part in range(PAIR):
+                if step >= per_chunk:
+                    some_pairs(
+                        step % per_chunk * turns + u,
+                        part,
+                        functools.partial(evaluate, step // per_chunk - 1),
+                    )
+                else:
+                    some_pairs(step * turns + u, part, build)
+                transform_high(step, u, part)
+                if step + 1 < steps:
+                    prepare(step + 1, u, part, PAIR)
 
     @pl.loop(0, pairs)
     def _(e):
@@ -210,7 +230,7 @@
             rows = found_rows[j, :, part * LANES : (part + 1) * LANES]
             taken = jnp.take_along_axis(rows, spot, axis=1, mode="promise_in_bounds")
             line = jnp.where(lane % TOP // 2 == j, taken, line)
-        out_ref[jnp.bitwise_xor(hi, place)] = line * sign
+        out_ref[hi * groups : (hi + 1) * groups, :] = line * sign
 
 
 def partial_sketch(gradients, sign_words, sub_index, place, high_dev, scale):
@@ -219,10 +239,10 @@
     groups = high_dev // PACK
     points = kept // (HALVED * groups)
     grads = gradients.reshape(high_dev, TOP, rest // STEP, 1, ROWS * LANES)
-    words = sign_words.reshape(-1, LANES)
+    words = sign_words.reshape(high_dev, -1, 1, LANES)
     return pl.pallas_call(
         functools.partial(sketch_kernel, high_dev=high_dev, scale=scale),
-        out_shape=jax.ShapeDtypeStruct((kept // TOP // high_dev, groups, LANES), jnp.float32),
+        out_shape=jax.ShapeDtypeStruct((kept // LANES, LANES), jnp.float32),
         in_specs=[
             pl.BlockSpec(memory_space=pltpu.SMEM),
             pl.BlockSpec(memory_space=pl.ANY),
@@ -232,7 +252,7 @@
         out_specs=pl.BlockSpec(memory_space=pltpu.VMEM),
         scratch_shapes=[
             pltpu.VMEM((SLOTS, high_dev, 1, TOP * ROWS * LANES), jnp.bfloat16),
-            pltpu.VMEM(words.shape, jnp.int32),
+            pltpu.VMEM((high_dev, words.shape[1] + 1, 1, LANES), jnp.int32),
             pltpu.VMEM((rest // GROUP, TOP // 2, high_dev, LANES), jnp.int32),
             pltpu.VMEM((high_dev, high_dev), jnp.bfloat16),
             pltpu.VMEM((TOP, ROWS * (high_dev + 1), LANES), jnp.float32),
@@ -247,13 +267,43 @@
             pltpu.SemaphoreType.DMA((SLOTS, TOP)),
             pltpu.SemaphoreType.DMA,
         ],
-        compiler_params=pltpu.CompilerParams(vmem_limit_bytes=62 * 1024 * 1024),
+        compiler_params=pltpu.CompilerParams(vmem_limit_bytes=63 * 1024 * 1024),
+        cost_estimate=pl.CostEstimate(
+            flops=4 * NLOW * high_dev * NMID * NLOW, bytes_accessed=4 * gradients.size, transcendentals=0
+        ),
         name="sketch",
     )(place, grads, words, sub_index.reshape(kept // LANES, LANES))
 
 
 def swapped(value, axis, size, bits):
     return lax.ppermute(value, axis, [(i, i ^ bits) for i in range(size)])
+
+
+def score_kernel(*refs, scale):
+    *sketches, own_tests, near_tests, out_ref, lines = refs
+    for n, sketch in enumerate(sketches):
+        whole = sketch[...].astype(jnp.float32)
+        for row in range(whole.shape[0]):
+            lines[n : n + 1, row * LANES : (row + 1) * LANES] = whole[row : row + 1, :]
+    left = lines[...].astype(jnp.bfloat16)
+    for n, tests in enumerate([own_tests] + [near_tests.at[s] for s in range(near_tests.shape[0])]):
+        found = lax.dot_general(
+            left, tests[...], (((1,), (1,)), ((), ())), preferred_element_type=jnp.float32
+        )
+        found = found[: len(sketches)] * scale
+        out_ref[:, n * tests.shape[0] : (n + 1) * tests.shape[0]] = found
+
+
+def scores_of(sketches, own_tests, near_tests, scale):
+    tests, kept = own_tests.shape
+    count = len(sketches)
+    return pl.pallas_call(
+        functools.partial(score_kernel, scale=scale),
+        out_shape=jax.ShapeDtypeStruct((count, tests * (1 + near_tests.shape[0])), jnp.float32),
+        scratch_shapes=[pltpu.VMEM((16, kept), jnp.float32)],
+        compiler_params=pltpu.CompilerParams(vmem_limit_bytes=32 * 1024 * 1024),
+        name="scores",
+    )(*sketches, own_tests, near_tests)
 
 
 def on_device(gradients, sign_words, sub_index, test_sketch, *, mesh):
@@ -264,32 +314,27 @@
     high_dev = local_features // (NMID * NLOW)
     feature_scale = float(local_features * feat_size) ** (-0.5)
     score_scale = float(kept) ** (-0.5)
-    place = lax.axis_index("feat").astype(jnp.int32)
-    own_kept = kept // feat_size
-    own_tests = lax.dynamic_slice_in_dim(test_sketch, place * own_kept, own_kept, axis=1)
-    own_tests = lax.all_gather(own_tests, "far", axis=0, tiled=True)
-    shares = partial_sketch(gradients, sign_words, sub_index, place.reshape(1), high_dev, feature_scale)
-    sketch = shares[0]
+    place = lax.axis_index("feat").astype(jnp.int32).reshape(1)
+    near_tests = jnp.stack([swapped(test_sketch, "near", near_size, s) for s in range(1, near_size)])
+    shares = partial_sketch(gradients, sign_words, sub_index, place, high_dev, feature_scale)
+    sketch = shares
     for s in range(1, feat_size):
-        sketch = sketch + swapped(shares[s], "feat", feat_size, s)
-    sketch = sketch.astype(jnp.bfloat16).reshape(1, own_kept)
-    sketches = [sketch] + [swapped(sketch, "near", near_size, s) for s in range(1, near_size)]
-    scores = jnp.einsum(
-        "ek,tk->et", jnp.concatenate(sketches, axis=0), own_tests, preferred_element_type=jnp.float32
+        sketch = sketch + swapped(shares, "feat", feat_size, s)
+    sketch = sketch.astype(jnp.bfloat16)
+    sketches = [sketch] + [swapped(sketch, "far", far_size, s) for s in range(1, far_size)]
+    scores = scores_of(sketches, test_sketch, near_tests, score_scale)
+    scores = jnp.stack(
+        [scores[:1]] + [swapped(scores[s : s + 1], "far", far_size, s) for s in range(1, far_size)]
     )
-    scores = jnp.stack(
-        [scores[0]] + [swapped(scores[s], "near", near_size, s) for s in range(1, near_size)]
-    )
-    total = scores
-    for s in range(1, feat_size):
-        total = total + swapped(scores, "feat", feat_size, s)
-    total = (total * score_scale).reshape(near_size, far_size, tests)
-    own = lax.axis_index("near")
+    scores = scores.reshape(far_size, near_size, tests)
+    far, near = lax.axis_index("far"), lax.axis_index("near")
     for b in range(near_size.bit_length() - 1):
-        split = total.reshape(-1, 2, 1 << b, far_size, tests)
-        total = jnp.where(jnp.bitwise_and(own, 1 << b) != 0, split[:, ::-1], split)
-    total = total.reshape(near_size, far_size, tests)
-    return jnp.swapaxes(total, 0, 1).reshape(1, -1)
+        split = scores.reshape(far_size, -1, 2, 1 << b, tests)
+        scores = jnp.where(jnp.bitwise_and(near, 1 << b) != 0, split[:, :, ::-1], split)
+    for b in range(far_size.bit_length() - 1):
+        split = scores.reshape(-1, 2, 1 << b, near_size, tests)
+        scores = jnp.where(jnp.bitwise_and(far, 1 << b) != 0, split[:, ::-1], split)
+    return scores.reshape(1, -1)
 
 
 def solution(mesh):

time: 98.4 us -> 107 us (1.087)
  Pallas kernels: 61.3 us -> 79.3 us
  between operations: 13.4 us -> 0.05 us
  starting transfers between devices: 8.09 us -> 13.7 us
  matrix products: 2.23 us -> 0 us
  local copies, waits for them, and re-layouts: 3.26 us -> 1.63 us
  waiting for transfers between devices: 9.05 us -> 10.4 us
    pallas_call x1, Pallas kernels: 61.3 us -> 76.5 us  [partial_sketch(): pl.pallas_call(functools.partial(sketch_kernel, high_dev=high_dev, scale=...]
    ppermute x8 -> x10, starting transfers between devices: 8.09 us -> 13.7 us  [swapped(): return lax.ppermute(value, axis, [(i, i ^ bits) for i in range(size)])]
    pallas_call x0 -> x1, Pallas kernels: none -> 2.78 us  [scores_of(): pl.pallas_call(functools.partial(score_kernel, scale=scale), out_shape=ja...]
    dot_general x1 -> x0, matrix products: 2.23 us -> none  [on_device(): jnp.einsum('ek,tk->et', jnp.concatenate(sketches, axis=0), own_tests, pre...]
    dynamic_slice x1 -> x0, local copies, waits for them, and re-layouts: 1.9 us -> none  [on_device(): lax.dynamic_slice_in_dim(test_sketch, place * own_kept, own_kept, axis=1)]
    unnamed x1 -> x2, local copies, waits for them, and re-layouts: 0.01 us -> 1.59 us
    ppermute x8 -> x10, waiting for transfers between devices: 9.03 us -> 10.4 us  [swapped(): return lax.ppermute(value, axis, [(i, i ^ bits) for i in range(size)])]
  transfers between devices with their start and end apart: 9 -> 10, of which waited for: 6 -> 6; matrix products, arithmetic and copies ran while one was open for 1% -> 1% of each run, Pallas kernels for 62% -> 72%
where the time goes in v11:
time: 107 us; the launch traced here: 106 us
  Pallas kernels  79.3 us (74%)
  starting transfers between devices  13.7 us (13%)
  waiting for transfers between devices  10.4 us (10%)
  local copies, waits for them, and re-layouts  1.63 us (2%)
  other arithmetic  1.39 us (1%)
    pallas_call x1, Pallas kernels, partial_sketch(): pl.pallas_call(functools.partial(sketch_kernel, high_dev=high_dev, scale=...  76.5 us
    ppermute x10, starting transfers between devices, swapped(): return lax.ppermute(value, axis, [(i, i ^ bits) for i in range(size)])  13.7 us
    ppermute x10, waiting for transfers between devices, swapped(): return lax.ppermute(value, axis, [(i, i ^ bits) for i in range(size)])  10.4 us
    pallas_call x1, Pallas kernels, scores_of(): pl.pallas_call(functools.partial(score_kernel, scale=scale), out_shape=ja...  2.78 us
  transfers between devices with their start and end apart: 10, of which 6 were waited for; matrix products, arithmetic and copies ran while one was open for 1% of the time, Pallas kernels for 72%

profile of v11, /device:TPU:0, one launch (start us, length us, event | category | flops | bytes accessed | tf_op | source)
XLA Modules:
  0.0 106.4 jit_solution(14875011355374016925)
XLA Ops:
  0.0 2.9 %collective-permute-start.6 = (bf16[128,8192]{1,0:T(8,128)(2,1)}, bf16[128,8192]{1,0:T(8,128)(2,1)}, u32[]{:S(2)}, u32[]{:S(2)}) collective-permute-start(bf16[128,8192]{1,0:T(8,128)(2,1)} %refs_4_.1), channel_id=1, source_target_pairs={{0,1},{1,0},{2,3},{3,2},{4,5},{5,4},{6,7},{7,6},{8,9},{9,8},{10,11... | collective-permute-start | bytes 6291464 | tf_op jit(solution)/shard_map/ppermute | solution.py:279
  2.9 76.5 %sketch.1 = f32[64,128]{1,0:T(8,128)} custom-call(s32[1]{0:T(128)} %bitcast.place_ref, bf16[256,8,8,1,1024]{4,3,2,1,0:T(2,128)(2,1)} %bitcast.1.grads, s32[256,32,1,128]{3,2,1,0:T(1,128)} %bitcast.13, s32[64,128]{1,0:T(8,128)} %bitcast.14), custom_call_target="tpu_custom_call" | custom-call | flops 17179869184 | bytes 67108864 | tf_op jit(solution)/shard_map/sketch/pallas_call | solution.py:243
  79.4 0.1 collective-permute-start
  79.5 1.6 %collective-permute-start.1 = (f32[64,128]{1,0:T(8,128)}, f32[64,128]{1,0:T(8,128)S(1)}, u32[]{:S(2)}, u32[]{:S(2)}) collective-permute-start(f32[64,128]{1,0:T(8,128)} %sketch.1), channel_id=1, source_target_pairs={{0,16},{8,24},{16,0},{24,8},{1,17},{9,25},{17,1},{25,9},{2,18},{10... | collective-permute-start | bytes 98312 | tf_op jit(solution)/shard_map/ppermute | solution.py:279
  81.1 0.3 collective-permute-start.2
  81.4 0.0 collective-permute-done
  81.4 2.3 %collective-permute-done.1 = f32[64,128]{1,0:T(8,128)S(1)} collective-permute-done((f32[64,128]{1,0:T(8,128)}, f32[64,128]{1,0:T(8,128)S(1)}, u32[]{:S(2)}, u32[]{:S(2)}) %collective-permute-start.1) | collective-permute-done | bytes 32800 | tf_op jit(solution)/shard_map/ppermute | solution.py:279
  83.7 0.9 collective-permute-done.2
  84.6 0.8 add_convert_fusion.refs_0_
  85.4 1.6 %collective-permute-start.3 = (bf16[64,128]{1,0:T(8,128)(2,1)S(1)}, bf16[64,128]{1,0:T(8,128)(2,1)S(1)}, u32[]{:S(2)}, u32[]{:S(2)}) collective-permute-start(bf16[64,128]{1,0:T(8,128)(2,1)S(1)} %add_convert_fusion.refs_0_), channel_id=1, source_target_pairs={{0,2},{2,0},{4,6},{6,4},{1,3},{3,1},{5,7},{7,5},{8,10},{10,8},{12,... | collective-permute-start | bytes 49160 | tf_op jit(solution)/shard_map/ppermute | solution.py:279
  87.1 2.6 %collective-permute-start.4 = (bf16[64,128]{1,0:T(8,128)(2,1)S(1)}, bf16[64,128]{1,0:T(8,128)(2,1)S(1)}, u32[]{:S(2)}, u32[]{:S(2)}) collective-permute-start(bf16[64,128]{1,0:T(8,128)(2,1)S(1)} %add_convert_fusion.refs_0_), channel_id=1, source_target_pairs={{0,4},{2,6},{4,0},{6,2},{1,5},{3,7},{5,1},{7,3},{8,12},{10,14},{12... | collective-permute-start | bytes 49160 | tf_op jit(solution)/shard_map/ppermute | solution.py:279
  89.7 0.2 collective-permute-start.5
  89.9 0.0 collective-permute-done.3.refs_1_
  89.9 1.9 %collective-permute-done.4.refs_2_ = bf16[64,128]{1,0:T(8,128)(2,1)S(1)} collective-permute-done((bf16[64,128]{1,0:T(8,128)(2,1)S(1)}, bf16[64,128]{1,0:T(8,128)(2,1)S(1)}, u32[]{:S(2)}, u32[]{:S(2)}) %collective-permute-start.4) | collective-permute-done | bytes 16416 | tf_op jit(solution)/shard_map/ppermute | solution.py:279
  91.8 3.4 %collective-permute-done.5.refs_3_ = bf16[64,128]{1,0:T(8,128)(2,1)S(1)} collective-permute-done((bf16[64,128]{1,0:T(8,128)(2,1)S(1)}, bf16[64,128]{1,0:T(8,128)(2,1)S(1)}, u32[]{:S(2)}, u32[]{:S(2)}) %collective-permute-start.5) | collective-permute-done | bytes 16416 | tf_op jit(solution)/shard_map/ppermute | solution.py:279
  95.2 0.0 collective-permute-done.6
  95.2 0.0 copy-start
  95.2 1.6 %copy-done = bf16[128,8192]{1,0:T(8,128)(2,1)S(1)} copy-done((bf16[128,8192]{1,0:T(8,128)(2,1)S(1)}, bf16[128,8192]{1,0:T(8,128)(2,1)}, u32[]{:S(2)}) %copy-start) | copy-done | bytes 2097176
  96.8 2.8 %scores.1 = f32[4,256]{1,0:T(4,128)S(1)} custom-call(bf16[64,128]{1,0:T(8,128)(2,1)S(1)} %add_convert_fusion.refs_0_, bf16[64,128]{1,0:T(8,128)(2,1)S(1)} %collective-permute-done.3.refs_1_, bf16[64,128]{1,0:T(8,128)(2,1)S(1)} %collective-permute-done.4.refs_2_, bf16[64,128]{1,0:T(8,128)(2,1)S(1)} %collective-permute-done.5.refs_3_, ...), custom_call_target="tpu_custom_call" | custom-call | tf_op jit(solution)/shard_map/scores/pallas_call | solution.py:300
  99.6 0.1 collective-permute-start.7
  99.6 0.8 collective-permute-start.8
  100.4 3.6 %collective-permute-start.9 = (f32[1,256]{1,0:T(1,128)S(1)}, f32[1,256]{1,0:T(1,128)S(1)}, u32[]{:S(2)}, u32[]{:S(2)}) collective-permute-start(f32[1,256]{1,0:T(1,128)S(1)} %get-tuple-element.6), channel_id=1, source_target_pairs={{0,6},{2,4},{4,2},{6,0},{1,7},{3,5},{5,3},{7,1},{8,14},{10,12},{12... | collective-permute-start | bytes 3080 | tf_op jit(solution)/shard_map/ppermute | solution.py:279
  104.0 0.0 collective-permute-done.7
  104.0 0.2 collective-permute-done.8
  104.2 1.6 %collective-permute-done.9 = f32[1,256]{1,0:T(1,128)S(1)} collective-permute-done((f32[1,256]{1,0:T(1,128)S(1)}, f32[1,256]{1,0:T(1,128)S(1)}, u32[]{:S(2)}, u32[]{:S(2)}) %collective-permute-start.9) | collective-permute-done | bytes 1056 | tf_op jit(solution)/shard_map/ppermute | solution.py:279
  105.8 0.6 reverse_select_fusion
  (5 shorter events, 0.1 us)
Async XLA Ops:
  0.0 95.2 %collective-permute-start.6 = (bf16[128,8192]{1,0:T(8,128)(2,1)}, bf16[128,8192]{1,0:T(8,128)(2,1)}, u32[]{:S(2)}, u32[]{:S(2)}) collective-permute-start(bf16[128,8192]{1,0:T(8,128)(2,1)} %refs_4_.1), channel_id=1, source_target_pairs={{0,1},{1,0},{2,3},{3,2},{4,5},{5,4},{6,7},{7,6},{8,9},{9,8},{10,11... | collective-permute-start | bytes 6291464 | tf_op jit(solution)/shard_map/ppermute | solution.py:279
  79.4 1.9 %collective-permute-start = (f32[64,128]{1,0:T(8,128)}, f32[64,128]{1,0:T(8,128)S(1)}, u32[]{:S(2)}, u32[]{:S(2)}) collective-permute-start(f32[64,128]{1,0:T(8,128)} %sketch.1), channel_id=1, source_target_pairs={{0,8},{8,0},{16,24},{24,16},{1,9},{9,1},{17,25},{25,17},{2,10},{10... | collective-permute-start | bytes 98312 | tf_op jit(solution)/shard_map/ppermute | solution.py:279
  79.5 4.2 %collective-permute-start.1 = (f32[64,128]{1,0:T(8,128)}, f32[64,128]{1,0:T(8,128)S(1)}, u32[]{:S(2)}, u32[]{:S(2)}) collective-permute-start(f32[64,128]{1,0:T(8,128)} %sketch.1), channel_id=1, source_target_pairs={{0,16},{8,24},{16,0},{24,8},{1,17},{9,25},{17,1},{25,9},{2,18},{10... | collective-permute-start | bytes 98312 | tf_op jit(solution)/shard_map/ppermute | solution.py:279
  81.1 3.6 %collective-permute-start.2 = (f32[64,128]{1,0:T(8,128)}, f32[64,128]{1,0:T(8,128)S(1)}, u32[]{:S(2)}, u32[]{:S(2)}) collective-permute-start(f32[64,128]{1,0:T(8,128)} %sketch.1), channel_id=1, source_target_pairs={{0,24},{8,16},{16,8},{24,0},{1,25},{9,17},{17,9},{25,1},{2,26},{10... | collective-permute-start | bytes 98312 | tf_op jit(solution)/shard_map/ppermute | solution.py:279
  85.4 4.5 %collective-permute-start.3 = (bf16[64,128]{1,0:T(8,128)(2,1)S(1)}, bf16[64,128]{1,0:T(8,128)(2,1)S(1)}, u32[]{:S(2)}, u32[]{:S(2)}) collective-permute-start(bf16[64,128]{1,0:T(8,128)(2,1)S(1)} %add_convert_fusion.refs_0_), channel_id=1, source_target_pairs={{0,2},{2,0},{4,6},{6,4},{1,3},{3,1},{5,7},{7,5},{8,10},{10,8},{12,... | collective-permute-start | bytes 49160 | tf_op jit(solution)/shard_map/ppermute | solution.py:279
  87.1 4.7 %collective-permute-start.4 = (bf16[64,128]{1,0:T(8,128)(2,1)S(1)}, bf16[64,128]{1,0:T(8,128)(2,1)S(1)}, u32[]{:S(2)}, u32[]{:S(2)}) collective-permute-start(bf16[64,128]{1,0:T(8,128)(2,1)S(1)} %add_convert_fusion.refs_0_), channel_id=1, source_target_pairs={{0,4},{2,6},{4,0},{6,2},{1,5},{3,7},{5,1},{7,3},{8,12},{10,14},{12... | collective-permute-start | bytes 49160 | tf_op jit(solution)/shard_map/ppermute | solution.py:279
  89.7 5.5 %collective-permute-start.5 = (bf16[64,128]{1,0:T(8,128)(2,1)S(1)}, bf16[64,128]{1,0:T(8,128)(2,1)S(1)}, u32[]{:S(2)}, u32[]{:S(2)}) collective-permute-start(bf16[64,128]{1,0:T(8,128)(2,1)S(1)} %add_convert_fusion.refs_0_), channel_id=1, source_target_pairs={{0,6},{2,4},{4,2},{6,0},{1,7},{3,5},{5,3},{7,1},{8,14},{10,12},{12... | collective-permute-start | bytes 49160 | tf_op jit(solution)/shard_map/ppermute | solution.py:279
  95.2 1.6 %copy-start = (bf16[128,8192]{1,0:T(8,128)(2,1)S(1)}, bf16[128,8192]{1,0:T(8,128)(2,1)}, u32[]{:S(2)}) copy-start(bf16[128,8192]{1,0:T(8,128)(2,1)} %refs_4_.1) | copy-start | bytes 6291460
  99.6 4.4 %collective-permute-start.7 = (f32[1,256]{1,0:T(1,128)S(1)}, f32[1,256]{1,0:T(1,128)S(1)}, u32[]{:S(2)}, u32[]{:S(2)}) collective-permute-start(f32[1,256]{1,0:T(1,128)S(1)} %get-tuple-element.8), channel_id=1, source_target_pairs={{0,2},{2,0},{4,6},{6,4},{1,3},{3,1},{5,7},{7,5},{8,10},{10,8},{12,... | collective-permute-start | bytes 3080 | tf_op jit(solution)/shard_map/ppermute | solution.py:279
  99.6 4.5 %collective-permute-start.8 = (f32[1,256]{1,0:T(1,128)S(1)}, f32[1,256]{1,0:T(1,128)S(1)}, u32[]{:S(2)}, u32[]{:S(2)}) collective-permute-start(f32[1,256]{1,0:T(1,128)S(1)} %get-tuple-element.7), channel_id=1, source_target_pairs={{0,4},{2,6},{4,0},{6,2},{1,5},{3,7},{5,1},{7,3},{8,12},{10,14},{12... | collective-permute-start | bytes 3080 | tf_op jit(solution)/shard_map/ppermute | solution.py:279
  100.4 5.4 %collective-permute-start.9 = (f32[1,256]{1,0:T(1,128)S(1)}, f32[1,256]{1,0:T(1,128)S(1)}, u32[]{:S(2)}, u32[]{:S(2)}) collective-permute-start(f32[1,256]{1,0:T(1,128)S(1)} %get-tuple-element.6), channel_id=1, source_target_pairs={{0,6},{2,4},{4,2},{6,0},{1,7},{3,5},{5,3},{7,1},{8,14},{10,12},{12... | collective-permute-start | bytes 3080 | tf_op jit(solution)/shard_map/ppermute | solution.py:279

commit v12 on v11

--- a/solution.py
+++ b/solution.py
@@ -149,18 +149,21 @@
             for top in range(TOP):
                 ybuf[step % 2][top, pl.ds(h, ROWS, stride), :] = values[top]
 
-    def transform_high(step, u, n):
-        top, i = u * PAIR % TOP + n, u * PAIR // TOP
+    def transform_high(step, u):
+        first, i = u * PAIR % TOP, u * PAIR // TOP
         columns = [
-            ybuf[step % 2][top, pl.ds((2 * i + l_hi) * stride, high_dev), :].astype(jnp.bfloat16)
+            ybuf[step % 2][first + n, pl.ds((2 * i + l_hi) * stride, high_dev), :].astype(jnp.bfloat16)
+            for n in range(PAIR)
             for l_hi in range(2)
         ]
         result = jnp.dot(
             table[...], jnp.concatenate(columns, axis=1), preferred_element_type=jnp.float32
-        )
+        ).astype(jnp.bfloat16)
         chunk = step * STEP // GROUP
         row = step % (GROUP // STEP) * STEP + i
-        tbuf[chunk % 2][top // 2, n % 2 * GROUP + row] = result.astype(jnp.bfloat16)
+        for n in range(PAIR):
+            top = first + n
+            tbuf[chunk % 2][top // 2, n % 2 * GROUP + row] = result[:, n * NLOW : (n + 1) * NLOW]
 
     def evaluate(chunk, e):
         j, g = e // groups, e % groups
@@ -206,9 +209,9 @@
                     )
                 else:
                     some_pairs(step * turns + u, part, build)
-                transform_high(step, u, part)
-                if step + 1 < steps:
-                    prepare(step + 1, u, part, PAIR)
+            transform_high(step, u)
+            if step + 1 < steps:
+                prepare(step + 1, u, 0, 1)
 
     @pl.loop(0, pairs)
     def _(e):

time: 107 us -> 107 us (level)
  no operation moved by 1% of the time
where the time goes in v12:
time: 107 us
  Pallas kernels  79.5 us (74%)
  starting transfers between devices  13.7 us (13%)
  waiting for transfers between devices  10.4 us (10%)
  local copies, waits for them, and re-layouts  1.63 us (2%)
  other arithmetic  1.39 us (1%)
    pallas_call x1, Pallas kernels, partial_sketch(): pl.pallas_call(functools.partial(sketch_kernel, high_dev=high_dev, scale=...  76.8 us
    ppermute x10, starting transfers between devices, swapped(): return lax.ppermute(value, axis, [(i, i ^ bits) for i in range(size)])  13.7 us
    ppermute x10, waiting for transfers between devices, swapped(): return lax.ppermute(value, axis, [(i, i ^ bits) for i in range(size)])  10.4 us
    pallas_call x1, Pallas kernels, scores_of(): pl.pallas_call(functools.partial(score_kernel, scale=scale), out_shape=ja...  2.78 us
  transfers between devices with their start and end apart: 10, of which 6 were waited for; matrix products, arithmetic and copies ran while one was open for 1% of the time, Pallas kernels for 72%

profile of v12, /device:TPU:0, one launch (start us, length us, event | category | flops | bytes accessed | tf_op | source)
XLA Modules:
  0.0 106.7 jit_solution(1677290469013414671)
XLA Ops:
  0.0 2.9 %collective-permute-start.6 = (bf16[128,8192]{1,0:T(8,128)(2,1)}, bf16[128,8192]{1,0:T(8,128)(2,1)}, u32[]{:S(2)}, u32[]{:S(2)}) collective-permute-start(bf16[128,8192]{1,0:T(8,128)(2,1)} %refs_4_.1), channel_id=1, source_target_pairs={{0,1},{1,0},{2,3},{3,2},{4,5},{5,4},{6,7},{7,6},{8,9},{9,8},{10,11... | collective-permute-start | bytes 6291464 | tf_op jit(solution)/shard_map/ppermute | solution.py:282
  2.9 76.8 %sketch.1 = f32[64,128]{1,0:T(8,128)} custom-call(s32[1]{0:T(128)} %bitcast.place_ref, bf16[256,8,8,1,1024]{4,3,2,1,0:T(2,128)(2,1)} %bitcast.1.grads, s32[256,32,1,128]{3,2,1,0:T(1,128)} %bitcast.13, s32[64,128]{1,0:T(8,128)} %bitcast.14), custom_call_target="tpu_custom_call" | custom-call | flops 17179869184 | bytes 67108864 | tf_op jit(solution)/shard_map/sketch/pallas_call | solution.py:246
  79.7 0.1 collective-permute-start
  79.8 1.6 %collective-permute-start.1 = (f32[64,128]{1,0:T(8,128)}, f32[64,128]{1,0:T(8,128)S(1)}, u32[]{:S(2)}, u32[]{:S(2)}) collective-permute-start(f32[64,128]{1,0:T(8,128)} %sketch.1), channel_id=1, source_target_pairs={{0,16},{8,24},{16,0},{24,8},{1,17},{9,25},{17,1},{25,9},{2,18},{10... | collective-permute-start | bytes 98312 | tf_op jit(solution)/shard_map/ppermute | solution.py:282
  81.4 0.3 collective-permute-start.2
  81.7 0.0 collective-permute-done
  81.7 2.3 %collective-permute-done.1 = f32[64,128]{1,0:T(8,128)S(1)} collective-permute-done((f32[64,128]{1,0:T(8,128)}, f32[64,128]{1,0:T(8,128)S(1)}, u32[]{:S(2)}, u32[]{:S(2)}) %collective-permute-start.1) | collective-permute-done | bytes 32800 | tf_op jit(solution)/shard_map/ppermute | solution.py:282
  84.0 0.9 collective-permute-done.2
  84.9 0.8 add_convert_fusion.refs_0_
  85.7 1.6 %collective-permute-start.3 = (bf16[64,128]{1,0:T(8,128)(2,1)S(1)}, bf16[64,128]{1,0:T(8,128)(2,1)S(1)}, u32[]{:S(2)}, u32[]{:S(2)}) collective-permute-start(bf16[64,128]{1,0:T(8,128)(2,1)S(1)} %add_convert_fusion.refs_0_), channel_id=1, source_target_pairs={{0,2},{2,0},{4,6},{6,4},{1,3},{3,1},{5,7},{7,5},{8,10},{10,8},{12,... | collective-permute-start | bytes 49160 | tf_op jit(solution)/shard_map/ppermute | solution.py:282
  87.3 2.6 %collective-permute-start.4 = (bf16[64,128]{1,0:T(8,128)(2,1)S(1)}, bf16[64,128]{1,0:T(8,128)(2,1)S(1)}, u32[]{:S(2)}, u32[]{:S(2)}) collective-permute-start(bf16[64,128]{1,0:T(8,128)(2,1)S(1)} %add_convert_fusion.refs_0_), channel_id=1, source_target_pairs={{0,4},{2,6},{4,0},{6,2},{1,5},{3,7},{5,1},{7,3},{8,12},{10,14},{12... | collective-permute-start | bytes 49160 | tf_op jit(solution)/shard_map/ppermute | solution.py:282
  89.9 0.2 collective-permute-start.5
  90.2 0.0 collective-permute-done.3.refs_1_
  90.2 1.9 %collective-permute-done.4.refs_2_ = bf16[64,128]{1,0:T(8,128)(2,1)S(1)} collective-permute-done((bf16[64,128]{1,0:T(8,128)(2,1)S(1)}, bf16[64,128]{1,0:T(8,128)(2,1)S(1)}, u32[]{:S(2)}, u32[]{:S(2)}) %collective-permute-start.4) | collective-permute-done | bytes 16416 | tf_op jit(solution)/shard_map/ppermute | solution.py:282
  92.1 3.4 %collective-permute-done.5.refs_3_ = bf16[64,128]{1,0:T(8,128)(2,1)S(1)} collective-permute-done((bf16[64,128]{1,0:T(8,128)(2,1)S(1)}, bf16[64,128]{1,0:T(8,128)(2,1)S(1)}, u32[]{:S(2)}, u32[]{:S(2)}) %collective-permute-start.5) | collective-permute-done | bytes 16416 | tf_op jit(solution)/shard_map/ppermute | solution.py:282
  95.5 0.0 collective-permute-done.6
  95.5 0.0 copy-start
  95.5 1.6 %copy-done = bf16[128,8192]{1,0:T(8,128)(2,1)S(1)} copy-done((bf16[128,8192]{1,0:T(8,128)(2,1)S(1)}, bf16[128,8192]{1,0:T(8,128)(2,1)}, u32[]{:S(2)}) %copy-start) | copy-done | bytes 2097176
  97.1 2.8 %scores.1 = f32[4,256]{1,0:T(4,128)S(1)} custom-call(bf16[64,128]{1,0:T(8,128)(2,1)S(1)} %add_convert_fusion.refs_0_, bf16[64,128]{1,0:T(8,128)(2,1)S(1)} %collective-permute-done.3.refs_1_, bf16[64,128]{1,0:T(8,128)(2,1)S(1)} %collective-permute-done.4.refs_2_, bf16[64,128]{1,0:T(8,128)(2,1)S(1)} %collective-permute-done.5.refs_3_, ...), custom_call_target="tpu_custom_call" | custom-call | tf_op jit(solution)/shard_map/scores/pallas_call | solution.py:303
  99.9 0.1 collective-permute-start.7
  99.9 0.8 collective-permute-start.8
  100.7 3.6 %collective-permute-start.9 = (f32[1,256]{1,0:T(1,128)S(1)}, f32[1,256]{1,0:T(1,128)S(1)}, u32[]{:S(2)}, u32[]{:S(2)}) collective-permute-start(f32[1,256]{1,0:T(1,128)S(1)} %get-tuple-element.6), channel_id=1, source_target_pairs={{0,6},{2,4},{4,2},{6,0},{1,7},{3,5},{5,3},{7,1},{8,14},{10,12},{12... | collective-permute-start | bytes 3080 | tf_op jit(solution)/shard_map/ppermute | solution.py:282
  104.3 0.0 collective-permute-done.7
  104.3 0.2 collective-permute-done.8
  104.4 1.6 %collective-permute-done.9 = f32[1,256]{1,0:T(1,128)S(1)} collective-permute-done((f32[1,256]{1,0:T(1,128)S(1)}, f32[1,256]{1,0:T(1,128)S(1)}, u32[]{:S(2)}, u32[]{:S(2)}) %collective-permute-start.9) | collective-permute-done | bytes 1056 | tf_op jit(solution)/shard_map/ppermute | solution.py:282
  106.1 0.6 reverse_select_fusion
  (5 shorter events, 0.1 us)
Async XLA Ops:
  0.0 95.5 %collective-permute-start.6 = (bf16[128,8192]{1,0:T(8,128)(2,1)}, bf16[128,8192]{1,0:T(8,128)(2,1)}, u32[]{:S(2)}, u32[]{:S(2)}) collective-permute-start(bf16[128,8192]{1,0:T(8,128)(2,1)} %refs_4_.1), channel_id=1, source_target_pairs={{0,1},{1,0},{2,3},{3,2},{4,5},{5,4},{6,7},{7,6},{8,9},{9,8},{10,11... | collective-permute-start | bytes 6291464 | tf_op jit(solution)/shard_map/ppermute | solution.py:282
  79.7 1.9 %collective-permute-start = (f32[64,128]{1,0:T(8,128)}, f32[64,128]{1,0:T(8,128)S(1)}, u32[]{:S(2)}, u32[]{:S(2)}) collective-permute-start(f32[64,128]{1,0:T(8,128)} %sketch.1), channel_id=1, source_target_pairs={{0,8},{8,0},{16,24},{24,16},{1,9},{9,1},{17,25},{25,17},{2,10},{10... | collective-permute-start | bytes 98312 | tf_op jit(solution)/shard_map/ppermute | solution.py:282
  79.8 4.2 %collective-permute-start.1 = (f32[64,128]{1,0:T(8,128)}, f32[64,128]{1,0:T(8,128)S(1)}, u32[]{:S(2)}, u32[]{:S(2)}) collective-permute-start(f32[64,128]{1,0:T(8,128)} %sketch.1), channel_id=1, source_target_pairs={{0,16},{8,24},{16,0},{24,8},{1,17},{9,25},{17,1},{25,9},{2,18},{10... | collective-permute-start | bytes 98312 | tf_op jit(solution)/shard_map/ppermute | solution.py:282
  81.4 3.6 %collective-permute-start.2 = (f32[64,128]{1,0:T(8,128)}, f32[64,128]{1,0:T(8,128)S(1)}, u32[]{:S(2)}, u32[]{:S(2)}) collective-permute-start(f32[64,128]{1,0:T(8,128)} %sketch.1), channel_id=1, source_target_pairs={{0,24},{8,16},{16,8},{24,0},{1,25},{9,17},{17,9},{25,1},{2,26},{10... | collective-permute-start | bytes 98312 | tf_op jit(solution)/shard_map/ppermute | solution.py:282
  85.7 4.5 %collective-permute-start.3 = (bf16[64,128]{1,0:T(8,128)(2,1)S(1)}, bf16[64,128]{1,0:T(8,128)(2,1)S(1)}, u32[]{:S(2)}, u32[]{:S(2)}) collective-permute-start(bf16[64,128]{1,0:T(8,128)(2,1)S(1)} %add_convert_fusion.refs_0_), channel_id=1, source_target_pairs={{0,2},{2,0},{4,6},{6,4},{1,3},{3,1},{5,7},{7,5},{8,10},{10,8},{12,... | collective-permute-start | bytes 49160 | tf_op jit(solution)/shard_map/ppermute | solution.py:282
  87.3 4.7 %collective-permute-start.4 = (bf16[64,128]{1,0:T(8,128)(2,1)S(1)}, bf16[64,128]{1,0:T(8,128)(2,1)S(1)}, u32[]{:S(2)}, u32[]{:S(2)}) collective-permute-start(bf16[64,128]{1,0:T(8,128)(2,1)S(1)} %add_convert_fusion.refs_0_), channel_id=1, source_target_pairs={{0,4},{2,6},{4,0},{6,2},{1,5},{3,7},{5,1},{7,3},{8,12},{10,14},{12... | collective-permute-start | bytes 49160 | tf_op jit(solution)/shard_map/ppermute | solution.py:282
  89.9 5.5 %collective-permute-start.5 = (bf16[64,128]{1,0:T(8,128)(2,1)S(1)}, bf16[64,128]{1,0:T(8,128)(2,1)S(1)}, u32[]{:S(2)}, u32[]{:S(2)}) collective-permute-start(bf16[64,128]{1,0:T(8,128)(2,1)S(1)} %add_convert_fusion.refs_0_), channel_id=1, source_target_pairs={{0,6},{2,4},{4,2},{6,0},{1,7},{3,5},{5,3},{7,1},{8,14},{10,12},{12... | collective-permute-start | bytes 49160 | tf_op jit(solution)/shard_map/ppermute | solution.py:282
  95.5 1.6 %copy-start = (bf16[128,8192]{1,0:T(8,128)(2,1)S(1)}, bf16[128,8192]{1,0:T(8,128)(2,1)}, u32[]{:S(2)}) copy-start(bf16[128,8192]{1,0:T(8,128)(2,1)} %refs_4_.1) | copy-start | bytes 6291460
  99.9 4.4 %collective-permute-start.7 = (f32[1,256]{1,0:T(1,128)S(1)}, f32[1,256]{1,0:T(1,128)S(1)}, u32[]{:S(2)}, u32[]{:S(2)}) collective-permute-start(f32[1,256]{1,0:T(1,128)S(1)} %get-tuple-element.8), channel_id=1, source_target_pairs={{0,2},{2,0},{4,6},{6,4},{1,3},{3,1},{5,7},{7,5},{8,10},{10,8},{12,... | collective-permute-start | bytes 3080 | tf_op jit(solution)/shard_map/ppermute | solution.py:282
  99.9 4.5 %collective-permute-start.8 = (f32[1,256]{1,0:T(1,128)S(1)}, f32[1,256]{1,0:T(1,128)S(1)}, u32[]{:S(2)}, u32[]{:S(2)}) collective-permute-start(f32[1,256]{1,0:T(1,128)S(1)} %get-tuple-element.7), channel_id=1, source_target_pairs={{0,4},{2,6},{4,0},{6,2},{1,5},{3,7},{5,1},{7,3},{8,12},{10,14},{12... | collective-permute-start | bytes 3080 | tf_op jit(solution)/shard_map/ppermute | solution.py:282
  100.7 5.4 %collective-permute-start.9 = (f32[1,256]{1,0:T(1,128)S(1)}, f32[1,256]{1,0:T(1,128)S(1)}, u32[]{:S(2)}, u32[]{:S(2)}) collective-permute-start(f32[1,256]{1,0:T(1,128)S(1)} %get-tuple-element.6), channel_id=1, source_target_pairs={{0,6},{2,4},{4,2},{6,0},{1,7},{3,5},{5,3},{7,1},{8,14},{10,12},{12... | collective-permute-start | bytes 3080 | tf_op jit(solution)/shard_map/ppermute | solution.py:282

commit v13 on v12

--- a/solution.py
+++ b/solution.py
@@ -110,19 +110,22 @@
             )
         return value
 
-    @pl.loop(0, high_dev // 8)
+    def spread_words(c, n):
+        for pair in range(TOP // 2):
+            one, two = (
+                lines[
+                    pl.ds(n * 8 * (per_high + 1) + (2 * pair + which) * chunks + c, 8, per_high + 1), 0, :
+                ]
+                for which in range(2)
+            )
+            wpair[c, pair, pl.ds(pl.multiple_of(n * 8, 8), 8), :] = spread(
+                jnp.bitwise_or(one, jnp.left_shift(two, 16))
+            )
+
+    @pl.loop(0, high_dev // 32)
     def _(n):
-        for c in range(chunks):
-            for pair in range(TOP // 2):
-                one, two = (
-                    lines[
-                        pl.ds(n * 8 * (per_high + 1) + (2 * pair + which) * chunks + c, 8, per_high + 1), 0, :
-                    ]
-                    for which in range(2)
-                )
-                wpair[c, pair, pl.ds(pl.multiple_of(n * 8, 8), 8), :] = spread(
-                    jnp.bitwise_or(one, jnp.left_shift(two, 16))
-                )
+        for m in range(4):
+            spread_words(0, 4 * n + m)
 
     def prepare(step, u, part, parts):
         slot = step % SLOTS
@@ -200,6 +203,13 @@
 
         @pl.loop(0, turns)
         def _(u):
+            later, part, parts = {0: (1, 0, 1), 1: (2, 0, 2), 2: (2, 1, 2), 3: (3, 0, 2), 4: (3, 1, 2)}.get(
+                step, (chunks, 0, 1)
+            )
+            if later < chunks:
+                count = high_dev // 8 // parts // turns
+                for m in range(count):
+                    spread_words(later, (part * turns + u) * count + m)
             for part in range(PAIR):
                 if step >= per_chunk:
                     some_pairs(

time: 107 us -> 100 us (0.935)
  Pallas kernels: 79.5 us -> 72.8 us
    pallas_call x1, Pallas kernels: 76.8 us -> 70 us  [partial_sketch(): pl.pallas_call(functools.partial(sketch_kernel, high_dev=high_dev, scale=...]
  transfers between devices with their start and end apart: 10 -> 10, of which waited for: 6 -> 6; matrix products, arithmetic and copies ran while one was open for 1% -> 1% of each run, Pallas kernels for 72% -> 70%
where the time goes in v13:
time: 100 us
  Pallas kernels  72.8 us (73%)
  starting transfers between devices  13.7 us (14%)
  waiting for transfers between devices  10.4 us (10%)
  local copies, waits for them, and re-layouts  1.63 us (2%)
  other arithmetic  1.39 us (1%)
    pallas_call x1, Pallas kernels, partial_sketch(): pl.pallas_call(functools.partial(sketch_kernel, high_dev=high_dev, scale=...  70 us
    ppermute x10, starting transfers between devices, swapped(): return lax.ppermute(value, axis, [(i, i ^ bits) for i in range(size)])  13.7 us
    ppermute x10, waiting for transfers between devices, swapped(): return lax.ppermute(value, axis, [(i, i ^ bits) for i in range(size)])  10.4 us
    pallas_call x1, Pallas kernels, scores_of(): pl.pallas_call(functools.partial(score_kernel, scale=scale), out_shape=ja...  2.78 us
  transfers between devices with their start and end apart: 10, of which 6 were waited for; matrix products, arithmetic and copies ran while one was open for 1% of the time, Pallas kernels for 70%

profile of v13, /device:TPU:0, one launch (start us, length us, event | category | flops | bytes accessed | tf_op | source)
XLA Modules:
  0.0 100.0 jit_solution(14501646077639972241)
XLA Ops:
  0.0 2.9 %collective-permute-start.6 = (bf16[128,8192]{1,0:T(8,128)(2,1)}, bf16[128,8192]{1,0:T(8,128)(2,1)}, u32[]{:S(2)}, u32[]{:S(2)}) collective-permute-start(bf16[128,8192]{1,0:T(8,128)(2,1)} %refs_4_.1), channel_id=1, source_target_pairs={{0,1},{1,0},{2,3},{3,2},{4,5},{5,4},{6,7},{7,6},{8,9},{9,8},{10,11... | collective-permute-start | bytes 6291464 | tf_op jit(solution)/shard_map/ppermute | solution.py:292
  2.9 70.0 %sketch.1 = f32[64,128]{1,0:T(8,128)} custom-call(s32[1]{0:T(128)} %bitcast.place_ref, bf16[256,8,8,1,1024]{4,3,2,1,0:T(2,128)(2,1)} %bitcast.1.grads, s32[256,32,1,128]{3,2,1,0:T(1,128)} %bitcast.13, s32[64,128]{1,0:T(8,128)} %bitcast.14), custom_call_target="tpu_custom_call" | custom-call | flops 17179869184 | bytes 67108864 | tf_op jit(solution)/shard_map/sketch/pallas_call | solution.py:256
  73.0 0.1 collective-permute-start
  73.1 1.6 %collective-permute-start.1 = (f32[64,128]{1,0:T(8,128)}, f32[64,128]{1,0:T(8,128)S(1)}, u32[]{:S(2)}, u32[]{:S(2)}) collective-permute-start(f32[64,128]{1,0:T(8,128)} %sketch.1), channel_id=1, source_target_pairs={{0,16},{8,24},{16,0},{24,8},{1,17},{9,25},{17,1},{25,9},{2,18},{10... | collective-permute-start | bytes 98312 | tf_op jit(solution)/shard_map/ppermute | solution.py:292
  74.7 0.3 collective-permute-start.2
  74.9 0.0 collective-permute-done
  74.9 2.3 %collective-permute-done.1 = f32[64,128]{1,0:T(8,128)S(1)} collective-permute-done((f32[64,128]{1,0:T(8,128)}, f32[64,128]{1,0:T(8,128)S(1)}, u32[]{:S(2)}, u32[]{:S(2)}) %collective-permute-start.1) | collective-permute-done | bytes 32800 | tf_op jit(solution)/shard_map/ppermute | solution.py:292
  77.3 1.0 collective-permute-done.2
  78.2 0.8 add_convert_fusion.refs_0_
  79.0 1.6 %collective-permute-start.3 = (bf16[64,128]{1,0:T(8,128)(2,1)S(1)}, bf16[64,128]{1,0:T(8,128)(2,1)S(1)}, u32[]{:S(2)}, u32[]{:S(2)}) collective-permute-start(bf16[64,128]{1,0:T(8,128)(2,1)S(1)} %add_convert_fusion.refs_0_), channel_id=1, source_target_pairs={{0,2},{2,0},{4,6},{6,4},{1,3},{3,1},{5,7},{7,5},{8,10},{10,8},{12,... | collective-permute-start | bytes 49160 | tf_op jit(solution)/shard_map/ppermute | solution.py:292
  80.6 2.6 %collective-permute-start.4 = (bf16[64,128]{1,0:T(8,128)(2,1)S(1)}, bf16[64,128]{1,0:T(8,128)(2,1)S(1)}, u32[]{:S(2)}, u32[]{:S(2)}) collective-permute-start(bf16[64,128]{1,0:T(8,128)(2,1)S(1)} %add_convert_fusion.refs_0_), channel_id=1, source_target_pairs={{0,4},{2,6},{4,0},{6,2},{1,5},{3,7},{5,1},{7,3},{8,12},{10,14},{12... | collective-permute-start | bytes 49160 | tf_op jit(solution)/shard_map/ppermute | solution.py:292
  83.2 0.2 collective-permute-start.5
  83.4 0.0 collective-permute-done.3.refs_1_
  83.4 1.9 %collective-permute-done.4.refs_2_ = bf16[64,128]{1,0:T(8,128)(2,1)S(1)} collective-permute-done((bf16[64,128]{1,0:T(8,128)(2,1)S(1)}, bf16[64,128]{1,0:T(8,128)(2,1)S(1)}, u32[]{:S(2)}, u32[]{:S(2)}) %collective-permute-start.4) | collective-permute-done | bytes 16416 | tf_op jit(solution)/shard_map/ppermute | solution.py:292
  85.3 3.4 %collective-permute-done.5.refs_3_ = bf16[64,128]{1,0:T(8,128)(2,1)S(1)} collective-permute-done((bf16[64,128]{1,0:T(8,128)(2,1)S(1)}, bf16[64,128]{1,0:T(8,128)(2,1)S(1)}, u32[]{:S(2)}, u32[]{:S(2)}) %collective-permute-start.5) | collective-permute-done | bytes 16416 | tf_op jit(solution)/shard_map/ppermute | solution.py:292
  88.7 0.0 collective-permute-done.6
  88.7 0.0 copy-start
  88.7 1.6 %copy-done = bf16[128,8192]{1,0:T(8,128)(2,1)S(1)} copy-done((bf16[128,8192]{1,0:T(8,128)(2,1)S(1)}, bf16[128,8192]{1,0:T(8,128)(2,1)}, u32[]{:S(2)}) %copy-start) | copy-done | bytes 2097176
  90.3 2.8 %scores.1 = f32[4,256]{1,0:T(4,128)S(1)} custom-call(bf16[64,128]{1,0:T(8,128)(2,1)S(1)} %add_convert_fusion.refs_0_, bf16[64,128]{1,0:T(8,128)(2,1)S(1)} %collective-permute-done.3.refs_1_, bf16[64,128]{1,0:T(8,128)(2,1)S(1)} %collective-permute-done.4.refs_2_, bf16[64,128]{1,0:T(8,128)(2,1)S(1)} %collective-permute-done.5.refs_3_, ...), custom_call_target="tpu_custom_call" | custom-call | tf_op jit(solution)/shard_map/scores/pallas_call | solution.py:313
  93.1 0.1 collective-permute-start.7
  93.2 0.8 collective-permute-start.8
  94.0 3.6 %collective-permute-start.9 = (f32[1,256]{1,0:T(1,128)S(1)}, f32[1,256]{1,0:T(1,128)S(1)}, u32[]{:S(2)}, u32[]{:S(2)}) collective-permute-start(f32[1,256]{1,0:T(1,128)S(1)} %get-tuple-element.6), channel_id=1, source_target_pairs={{0,6},{2,4},{4,2},{6,0},{1,7},{3,5},{5,3},{7,1},{8,14},{10,12},{12... | collective-permute-start | bytes 3080 | tf_op jit(solution)/shard_map/ppermute | solution.py:292
  97.6 0.0 collective-permute-done.7
  97.6 0.2 collective-permute-done.8
  97.7 1.6 %collective-permute-done.9 = f32[1,256]{1,0:T(1,128)S(1)} collective-permute-done((f32[1,256]{1,0:T(1,128)S(1)}, f32[1,256]{1,0:T(1,128)S(1)}, u32[]{:S(2)}, u32[]{:S(2)}) %collective-permute-start.9) | collective-permute-done | bytes 1056 | tf_op jit(solution)/shard_map/ppermute | solution.py:292
  99.4 0.6 reverse_select_fusion
  (5 shorter events, 0.1 us)
Async XLA Ops:
  0.0 88.7 %collective-permute-start.6 = (bf16[128,8192]{1,0:T(8,128)(2,1)}, bf16[128,8192]{1,0:T(8,128)(2,1)}, u32[]{:S(2)}, u32[]{:S(2)}) collective-permute-start(bf16[128,8192]{1,0:T(8,128)(2,1)} %refs_4_.1), channel_id=1, source_target_pairs={{0,1},{1,0},{2,3},{3,2},{4,5},{5,4},{6,7},{7,6},{8,9},{9,8},{10,11... | collective-permute-start | bytes 6291464 | tf_op jit(solution)/shard_map/ppermute | solution.py:292
  73.0 1.9 %collective-permute-start = (f32[64,128]{1,0:T(8,128)}, f32[64,128]{1,0:T(8,128)S(1)}, u32[]{:S(2)}, u32[]{:S(2)}) collective-permute-start(f32[64,128]{1,0:T(8,128)} %sketch.1), channel_id=1, source_target_pairs={{0,8},{8,0},{16,24},{24,16},{1,9},{9,1},{17,25},{25,17},{2,10},{10... | collective-permute-start | bytes 98312 | tf_op jit(solution)/shard_map/ppermute | solution.py:292
  73.1 4.2 %collective-permute-start.1 = (f32[64,128]{1,0:T(8,128)}, f32[64,128]{1,0:T(8,128)S(1)}, u32[]{:S(2)}, u32[]{:S(2)}) collective-permute-start(f32[64,128]{1,0:T(8,128)} %sketch.1), channel_id=1, source_target_pairs={{0,16},{8,24},{16,0},{24,8},{1,17},{9,25},{17,1},{25,9},{2,18},{10... | collective-permute-start | bytes 98312 | tf_op jit(solution)/shard_map/ppermute | solution.py:292
  74.7 3.6 %collective-permute-start.2 = (f32[64,128]{1,0:T(8,128)}, f32[64,128]{1,0:T(8,128)S(1)}, u32[]{:S(2)}, u32[]{:S(2)}) collective-permute-start(f32[64,128]{1,0:T(8,128)} %sketch.1), channel_id=1, source_target_pairs={{0,24},{8,16},{16,8},{24,0},{1,25},{9,17},{17,9},{25,1},{2,26},{10... | collective-permute-start | bytes 98312 | tf_op jit(solution)/shard_map/ppermute | solution.py:292
  79.0 4.5 %collective-permute-start.3 = (bf16[64,128]{1,0:T(8,128)(2,1)S(1)}, bf16[64,128]{1,0:T(8,128)(2,1)S(1)}, u32[]{:S(2)}, u32[]{:S(2)}) collective-permute-start(bf16[64,128]{1,0:T(8,128)(2,1)S(1)} %add_convert_fusion.refs_0_), channel_id=1, source_target_pairs={{0,2},{2,0},{4,6},{6,4},{1,3},{3,1},{5,7},{7,5},{8,10},{10,8},{12,... | collective-permute-start | bytes 49160 | tf_op jit(solution)/shard_map/ppermute | solution.py:292
  80.6 4.7 %collective-permute-start.4 = (bf16[64,128]{1,0:T(8,128)(2,1)S(1)}, bf16[64,128]{1,0:T(8,128)(2,1)S(1)}, u32[]{:S(2)}, u32[]{:S(2)}) collective-permute-start(bf16[64,128]{1,0:T(8,128)(2,1)S(1)} %add_convert_fusion.refs_0_), channel_id=1, source_target_pairs={{0,4},{2,6},{4,0},{6,2},{1,5},{3,7},{5,1},{7,3},{8,12},{10,14},{12... | collective-permute-start | bytes 49160 | tf_op jit(solution)/shard_map/ppermute | solution.py:292
  83.2 5.5 %collective-permute-start.5 = (bf16[64,128]{1,0:T(8,128)(2,1)S(1)}, bf16[64,128]{1,0:T(8,128)(2,1)S(1)}, u32[]{:S(2)}, u32[]{:S(2)}) collective-permute-start(bf16[64,128]{1,0:T(8,128)(2,1)S(1)} %add_convert_fusion.refs_0_), channel_id=1, source_target_pairs={{0,6},{2,4},{4,2},{6,0},{1,7},{3,5},{5,3},{7,1},{8,14},{10,12},{12... | collective-permute-start | bytes 49160 | tf_op jit(solution)/shard_map/ppermute | solution.py:292
  88.7 1.6 %copy-start = (bf16[128,8192]{1,0:T(8,128)(2,1)S(1)}, bf16[128,8192]{1,0:T(8,128)(2,1)}, u32[]{:S(2)}) copy-start(bf16[128,8192]{1,0:T(8,128)(2,1)} %refs_4_.1) | copy-start | bytes 6291460
  93.1 4.4 %collective-permute-start.7 = (f32[1,256]{1,0:T(1,128)S(1)}, f32[1,256]{1,0:T(1,128)S(1)}, u32[]{:S(2)}, u32[]{:S(2)}) collective-permute-start(f32[1,256]{1,0:T(1,128)S(1)} %get-tuple-element.8), channel_id=1, source_target_pairs={{0,2},{2,0},{4,6},{6,4},{1,3},{3,1},{5,7},{7,5},{8,10},{10,8},{12,... | collective-permute-start | bytes 3080 | tf_op jit(solution)/shard_map/ppermute | solution.py:292
  93.2 4.5 %collective-permute-start.8 = (f32[1,256]{1,0:T(1,128)S(1)}, f32[1,256]{1,0:T(1,128)S(1)}, u32[]{:S(2)}, u32[]{:S(2)}) collective-permute-start(f32[1,256]{1,0:T(1,128)S(1)} %get-tuple-element.7), channel_id=1, source_target_pairs={{0,4},{2,6},{4,0},{6,2},{1,5},{3,7},{5,1},{7,3},{8,12},{10,14},{12... | collective-permute-start | bytes 3080 | tf_op jit(solution)/shard_map/ppermute | solution.py:292
  94.0 5.4 %collective-permute-start.9 = (f32[1,256]{1,0:T(1,128)S(1)}, f32[1,256]{1,0:T(1,128)S(1)}, u32[]{:S(2)}, u32[]{:S(2)}) collective-permute-start(f32[1,256]{1,0:T(1,128)S(1)} %get-tuple-element.6), channel_id=1, source_target_pairs={{0,6},{2,4},{4,2},{6,0},{1,7},{3,5},{5,3},{7,1},{8,14},{10,12},{12... | collective-permute-start | bytes 3080 | tf_op jit(solution)/shard_map/ppermute | solution.py:292

commit v14 on v13

--- a/solution.py
+++ b/solution.py
@@ -57,7 +57,7 @@
             then(copy)
 
     per_high = NMID * NLOW // 16 // LANES
-    word_copy = pltpu.make_async_copy(words, wbuf.at[:, :per_high], wsem)
+    word_copy = pltpu.make_async_copy(words, wbuf, wsem)
     word_copy.start()
     for step in range(SLOTS):
         grad_copies(step, lambda copy: copy.start())
@@ -92,51 +92,34 @@
         ).astype(jnp.bfloat16)
 
     word_copy.wait()
-    lines = wbuf.reshape(high_dev * (per_high + 1), 1, LANES)
-    lane8 = iota((8, LANES), 1)
-
-    def spread(both):
-        value = jnp.take_along_axis(both, lane8 % 16 * 8 + lane8 // 16, axis=1, mode="promise_in_bounds")
-        for reach, keep in ((8, 0x00FF00FF), (4, 0x0F0F0F0F), (2, 0x33333333), (1, 0x55555555)):
-            other = jnp.take_along_axis(value, jnp.bitwise_xor(lane8, reach), axis=1, mode="promise_in_bounds")
-            value = jnp.where(
-                jnp.bitwise_and(lane8, reach) == 0,
-                jnp.bitwise_or(
-                    jnp.bitwise_and(value, keep), jnp.left_shift(jnp.bitwise_and(other, keep), reach)
-                ),
-                jnp.bitwise_or(
-                    jnp.bitwise_and(value, ~keep), jnp.bitwise_and(jnp.right_shift(other, reach), keep)
-                ),
-            )
-        return value
-
-    def spread_words(c, n):
+
+    def pair_words(c, n):
         for pair in range(TOP // 2):
             one, two = (
-                lines[
-                    pl.ds(n * 8 * (per_high + 1) + (2 * pair + which) * chunks + c, 8, per_high + 1), 0, :
-                ]
+                wbuf[pl.ds(n * 8 * per_high + (2 * pair + which) * chunks + c, 8, per_high), :]
                 for which in range(2)
             )
-            wpair[c, pair, pl.ds(pl.multiple_of(n * 8, 8), 8), :] = spread(
-                jnp.bitwise_or(one, jnp.left_shift(two, 16))
+            wpair[c, pair, pl.ds(pl.multiple_of(n * 8, 8), 8), :] = jnp.bitwise_or(
+                one, jnp.left_shift(two, 16)
             )
 
     @pl.loop(0, high_dev // 32)
     def _(n):
         for m in range(4):
-            spread_words(0, 4 * n + m)
+            pair_words(0, 4 * n + m)
 
     def prepare(step, u, part, parts):
         slot = step % SLOTS
         chunk = step * STEP // GROUP
-        row = step % (GROUP // STEP) * ROWS + iota((ROWS, LANES), 0)
-        bits = [jnp.left_shift(1, row), jnp.left_shift(1, row + 16)]
+        lane8 = iota((ROWS, LANES), 1)
+        bits = [jnp.left_shift(1, lane8 % 16), jnp.left_shift(1, lane8 % 16 + 16)]
+        spot = step % (GROUP // STEP) * (16 * STEP) + iota((ROWS, LANES), 0) * 8 + lane8 // 16
         for n in range(part * highs // parts, (part + 1) * highs // parts):
             h = u * highs + n
             values = []
             for pair in range(TOP // 2):
                 word = jnp.broadcast_to(wpair[chunk, pair, pl.ds(h, 1), :], (ROWS, LANES))
+                word = jnp.take_along_axis(word, spot, axis=1, mode="promise_in_bounds")
                 two = xbuf[slot, h, :, 2 * pair * ROWS * LANES : 2 * (pair + 1) * ROWS * LANES]
                 two = two.reshape(2 * ROWS, LANES).astype(jnp.float32)
                 for which in range(2):
@@ -209,7 +192,7 @@
             if later < chunks:
                 count = high_dev // 8 // parts // turns
                 for m in range(count):
-                    spread_words(later, (part * turns + u) * count + m)
+                    pair_words(later, (part * turns + u) * count + m)
             for part in range(PAIR):
                 if step >= per_chunk:
                     some_pairs(
@@ -252,7 +235,7 @@
     groups = high_dev // PACK
     points = kept // (HALVED * groups)
     grads = gradients.reshape(high_dev, TOP, rest // STEP, 1, ROWS * LANES)
-    words = sign_words.reshape(high_dev, -1, 1, LANES)
+    words = sign_words.reshape(-1, LANES)
     return pl.pallas_call(
         functools.partial(sketch_kernel, high_dev=high_dev, scale=scale),
         out_shape=jax.ShapeDtypeStruct((kept // LANES, LANES), jnp.float32),
@@ -265,7 +248,7 @@
         out_specs=pl.BlockSpec(memory_space=pltpu.VMEM),
         scratch_shapes=[
             pltpu.VMEM((SLOTS, high_dev, 1, TOP * ROWS * LANES), jnp.bfloat16),
-            pltpu.VMEM((high_dev, words.shape[1] + 1, 1, LANES), jnp.int32),
+            pltpu.VMEM(words.shape, jnp.int32),
             pltpu.VMEM((rest // GROUP, TOP // 2, high_dev, LANES), jnp.int32),
             pltpu.VMEM((high_dev, high_dev), jnp.bfloat16),
             pltpu.VMEM((TOP, ROWS * (high_dev + 1), LANES), jnp.float32),

time: 100 us -> 91.8 us (0.918)
  Pallas kernels: 72.8 us -> 64.3 us
    pallas_call x1, Pallas kernels: 70 us -> 61.5 us  [partial_sketch(): pl.pallas_call(functools.partial(sketch_kernel, high_dev=high_dev, scale=...]
  transfers between devices with their start and end apart: 10 -> 10, of which waited for: 6 -> 6; matrix products, arithmetic and copies ran while one was open for 1% -> 1% of each run, Pallas kernels for 70% -> 67%
where the time goes in v14:
time: 91.8 us; the launch traced here: 91.5 us
  Pallas kernels  64.3 us (70%)
  starting transfers between devices  13.7 us (15%)
  waiting for transfers between devices  10.4 us (11%)
  local copies, waits for them, and re-layouts  1.63 us (2%)
  other arithmetic  1.39 us (2%)
    pallas_call x1, Pallas kernels, partial_sketch(): pl.pallas_call(functools.partial(sketch_kernel, high_dev=high_dev, scale=...  61.5 us
    ppermute x10, starting transfers between devices, swapped(): return lax.ppermute(value, axis, [(i, i ^ bits) for i in range(size)])  13.7 us
    ppermute x10, waiting for transfers between devices, swapped(): return lax.ppermute(value, axis, [(i, i ^ bits) for i in range(size)])  10.4 us
    pallas_call x1, Pallas kernels, scores_of(): pl.pallas_call(functools.partial(score_kernel, scale=scale), out_shape=ja...  2.78 us
  transfers between devices with their start and end apart: 10, of which 6 were waited for; matrix products, arithmetic and copies ran while one was open for 1% of the time, Pallas kernels for 67%

profile of v14, /device:TPU:0, one launch (start us, length us, event | category | flops | bytes accessed | tf_op | source)
XLA Modules:
  0.0 91.5 jit_solution(16833492156246952247)
XLA Ops:
  0.0 2.9 %collective-permute-start.6 = (bf16[128,8192]{1,0:T(8,128)(2,1)}, bf16[128,8192]{1,0:T(8,128)(2,1)}, u32[]{:S(2)}, u32[]{:S(2)}) collective-permute-start(bf16[128,8192]{1,0:T(8,128)(2,1)} %refs_4_.1), channel_id=1, source_target_pairs={{0,1},{1,0},{2,3},{3,2},{4,5},{5,4},{6,7},{7,6},{8,9},{9,8},{10,11... | collective-permute-start | bytes 6291464 | tf_op jit(solution)/shard_map/ppermute | solution.py:275
  2.9 61.5 %sketch.1 = f32[64,128]{1,0:T(8,128)} custom-call(s32[1]{0:T(128)} %bitcast.place_ref, bf16[256,8,8,1,1024]{4,3,2,1,0:T(2,128)(2,1)} %bitcast.1.grads, s32[8192,128]{1,0:T(8,128)} %bitcast.13, s32[64,128]{1,0:T(8,128)} %bitcast.14), custom_call_target="tpu_custom_call" | custom-call | flops 17179869184 | bytes 67108864 | tf_op jit(solution)/shard_map/sketch/pallas_call | solution.py:239
  64.5 0.1 collective-permute-start
  64.5 1.6 %collective-permute-start.1 = (f32[64,128]{1,0:T(8,128)}, f32[64,128]{1,0:T(8,128)S(1)}, u32[]{:S(2)}, u32[]{:S(2)}) collective-permute-start(f32[64,128]{1,0:T(8,128)} %sketch.1), channel_id=1, source_target_pairs={{0,16},{8,24},{16,0},{24,8},{1,17},{9,25},{17,1},{25,9},{2,18},{10... | collective-permute-start | bytes 98312 | tf_op jit(solution)/shard_map/ppermute | solution.py:275
  66.1 0.3 collective-permute-start.2
  66.4 0.0 collective-permute-done
  66.4 2.3 %collective-permute-done.1 = f32[64,128]{1,0:T(8,128)S(1)} collective-permute-done((f32[64,128]{1,0:T(8,128)}, f32[64,128]{1,0:T(8,128)S(1)}, u32[]{:S(2)}, u32[]{:S(2)}) %collective-permute-start.1) | collective-permute-done | bytes 32800 | tf_op jit(solution)/shard_map/ppermute | solution.py:275
  68.7 0.9 %collective-permute-done.2 = f32[64,128]{1,0:T(8,128)S(1)} collective-permute-done((f32[64,128]{1,0:T(8,128)}, f32[64,128]{1,0:T(8,128)S(1)}, u32[]{:S(2)}, u32[]{:S(2)}) %collective-permute-start.2) | collective-permute-done | bytes 32800 | tf_op jit(solution)/shard_map/ppermute | solution.py:275
  69.7 0.8 add_convert_fusion.refs_0_
  70.4 1.6 %collective-permute-start.3 = (bf16[64,128]{1,0:T(8,128)(2,1)S(1)}, bf16[64,128]{1,0:T(8,128)(2,1)S(1)}, u32[]{:S(2)}, u32[]{:S(2)}) collective-permute-start(bf16[64,128]{1,0:T(8,128)(2,1)S(1)} %add_convert_fusion.refs_0_), channel_id=1, source_target_pairs={{0,2},{2,0},{4,6},{6,4},{1,3},{3,1},{5,7},{7,5},{8,10},{10,8},{12,... | collective-permute-start | bytes 49160 | tf_op jit(solution)/shard_map/ppermute | solution.py:275
  72.1 2.6 %collective-permute-start.4 = (bf16[64,128]{1,0:T(8,128)(2,1)S(1)}, bf16[64,128]{1,0:T(8,128)(2,1)S(1)}, u32[]{:S(2)}, u32[]{:S(2)}) collective-permute-start(bf16[64,128]{1,0:T(8,128)(2,1)S(1)} %add_convert_fusion.refs_0_), channel_id=1, source_target_pairs={{0,4},{2,6},{4,0},{6,2},{1,5},{3,7},{5,1},{7,3},{8,12},{10,14},{12... | collective-permute-start | bytes 49160 | tf_op jit(solution)/shard_map/ppermute | solution.py:275
  74.7 0.2 collective-permute-start.5
  74.9 0.0 collective-permute-done.3.refs_1_
  74.9 1.9 %collective-permute-done.4.refs_2_ = bf16[64,128]{1,0:T(8,128)(2,1)S(1)} collective-permute-done((bf16[64,128]{1,0:T(8,128)(2,1)S(1)}, bf16[64,128]{1,0:T(8,128)(2,1)S(1)}, u32[]{:S(2)}, u32[]{:S(2)}) %collective-permute-start.4) | collective-permute-done | bytes 16416 | tf_op jit(solution)/shard_map/ppermute | solution.py:275
  76.8 3.4 %collective-permute-done.5.refs_3_ = bf16[64,128]{1,0:T(8,128)(2,1)S(1)} collective-permute-done((bf16[64,128]{1,0:T(8,128)(2,1)S(1)}, bf16[64,128]{1,0:T(8,128)(2,1)S(1)}, u32[]{:S(2)}, u32[]{:S(2)}) %collective-permute-start.5) | collective-permute-done | bytes 16416 | tf_op jit(solution)/shard_map/ppermute | solution.py:275
  80.2 0.0 collective-permute-done.6
  80.2 0.0 copy-start
  80.2 1.6 %copy-done = bf16[128,8192]{1,0:T(8,128)(2,1)S(1)} copy-done((bf16[128,8192]{1,0:T(8,128)(2,1)S(1)}, bf16[128,8192]{1,0:T(8,128)(2,1)}, u32[]{:S(2)}) %copy-start) | copy-done | bytes 2097176
  81.8 2.8 %scores.1 = f32[4,256]{1,0:T(4,128)S(1)} custom-call(bf16[64,128]{1,0:T(8,128)(2,1)S(1)} %add_convert_fusion.refs_0_, bf16[64,128]{1,0:T(8,128)(2,1)S(1)} %collective-permute-done.3.refs_1_, bf16[64,128]{1,0:T(8,128)(2,1)S(1)} %collective-permute-done.4.refs_2_, bf16[64,128]{1,0:T(8,128)(2,1)S(1)} %collective-permute-done.5.refs_3_, ...), custom_call_target="tpu_custom_call" | custom-call | tf_op jit(solution)/shard_map/scores/pallas_call | solution.py:296
  84.6 0.1 collective-permute-start.7
  84.7 0.8 collective-permute-start.8
  85.4 3.6 %collective-permute-start.9 = (f32[1,256]{1,0:T(1,128)S(1)}, f32[1,256]{1,0:T(1,128)S(1)}, u32[]{:S(2)}, u32[]{:S(2)}) collective-permute-start(f32[1,256]{1,0:T(1,128)S(1)} %get-tuple-element.6), channel_id=1, source_target_pairs={{0,6},{2,4},{4,2},{6,0},{1,7},{3,5},{5,3},{7,1},{8,14},{10,12},{12... | collective-permute-start | bytes 3080 | tf_op jit(solution)/shard_map/ppermute | solution.py:275
  89.0 0.0 collective-permute-done.7
  89.0 0.2 collective-permute-done.8
  89.2 1.6 %collective-permute-done.9 = f32[1,256]{1,0:T(1,128)S(1)} collective-permute-done((f32[1,256]{1,0:T(1,128)S(1)}, f32[1,256]{1,0:T(1,128)S(1)}, u32[]{:S(2)}, u32[]{:S(2)}) %collective-permute-start.9) | collective-permute-done | bytes 1056 | tf_op jit(solution)/shard_map/ppermute | solution.py:275
  90.9 0.6 reverse_select_fusion
  (5 shorter events, 0.1 us)
Async XLA Ops:
  0.0 80.2 %collective-permute-start.6 = (bf16[128,8192]{1,0:T(8,128)(2,1)}, bf16[128,8192]{1,0:T(8,128)(2,1)}, u32[]{:S(2)}, u32[]{:S(2)}) collective-permute-start(bf16[128,8192]{1,0:T(8,128)(2,1)} %refs_4_.1), channel_id=1, source_target_pairs={{0,1},{1,0},{2,3},{3,2},{4,5},{5,4},{6,7},{7,6},{8,9},{9,8},{10,11... | collective-permute-start | bytes 6291464 | tf_op jit(solution)/shard_map/ppermute | solution.py:275
  64.5 1.9 %collective-permute-start = (f32[64,128]{1,0:T(8,128)}, f32[64,128]{1,0:T(8,128)S(1)}, u32[]{:S(2)}, u32[]{:S(2)}) collective-permute-start(f32[64,128]{1,0:T(8,128)} %sketch.1), channel_id=1, source_target_pairs={{0,8},{8,0},{16,24},{24,16},{1,9},{9,1},{17,25},{25,17},{2,10},{10... | collective-permute-start | bytes 98312 | tf_op jit(solution)/shard_map/ppermute | solution.py:275
  64.5 4.2 %collective-permute-start.1 = (f32[64,128]{1,0:T(8,128)}, f32[64,128]{1,0:T(8,128)S(1)}, u32[]{:S(2)}, u32[]{:S(2)}) collective-permute-start(f32[64,128]{1,0:T(8,128)} %sketch.1), channel_id=1, source_target_pairs={{0,16},{8,24},{16,0},{24,8},{1,17},{9,25},{17,1},{25,9},{2,18},{10... | collective-permute-start | bytes 98312 | tf_op jit(solution)/shard_map/ppermute | solution.py:275
  66.1 3.6 %collective-permute-start.2 = (f32[64,128]{1,0:T(8,128)}, f32[64,128]{1,0:T(8,128)S(1)}, u32[]{:S(2)}, u32[]{:S(2)}) collective-permute-start(f32[64,128]{1,0:T(8,128)} %sketch.1), channel_id=1, source_target_pairs={{0,24},{8,16},{16,8},{24,0},{1,25},{9,17},{17,9},{25,1},{2,26},{10... | collective-permute-start | bytes 98312 | tf_op jit(solution)/shard_map/ppermute | solution.py:275
  70.4 4.5 %collective-permute-start.3 = (bf16[64,128]{1,0:T(8,128)(2,1)S(1)}, bf16[64,128]{1,0:T(8,128)(2,1)S(1)}, u32[]{:S(2)}, u32[]{:S(2)}) collective-permute-start(bf16[64,128]{1,0:T(8,128)(2,1)S(1)} %add_convert_fusion.refs_0_), channel_id=1, source_target_pairs={{0,2},{2,0},{4,6},{6,4},{1,3},{3,1},{5,7},{7,5},{8,10},{10,8},{12,... | collective-permute-start | bytes 49160 | tf_op jit(solution)/shard_map/ppermute | solution.py:275
  72.1 4.7 %collective-permute-start.4 = (bf16[64,128]{1,0:T(8,128)(2,1)S(1)}, bf16[64,128]{1,0:T(8,128)(2,1)S(1)}, u32[]{:S(2)}, u32[]{:S(2)}) collective-permute-start(bf16[64,128]{1,0:T(8,128)(2,1)S(1)} %add_convert_fusion.refs_0_), channel_id=1, source_target_pairs={{0,4},{2,6},{4,0},{6,2},{1,5},{3,7},{5,1},{7,3},{8,12},{10,14},{12... | collective-permute-start | bytes 49160 | tf_op jit(solution)/shard_map/ppermute | solution.py:275
  74.7 5.5 %collective-permute-start.5 = (bf16[64,128]{1,0:T(8,128)(2,1)S(1)}, bf16[64,128]{1,0:T(8,128)(2,1)S(1)}, u32[]{:S(2)}, u32[]{:S(2)}) collective-permute-start(bf16[64,128]{1,0:T(8,128)(2,1)S(1)} %add_convert_fusion.refs_0_), channel_id=1, source_target_pairs={{0,6},{2,4},{4,2},{6,0},{1,7},{3,5},{5,3},{7,1},{8,14},{10,12},{12... | collective-permute-start | bytes 49160 | tf_op jit(solution)/shard_map/ppermute | solution.py:275
  80.2 1.6 %copy-start = (bf16[128,8192]{1,0:T(8,128)(2,1)S(1)}, bf16[128,8192]{1,0:T(8,128)(2,1)}, u32[]{:S(2)}) copy-start(bf16[128,8192]{1,0:T(8,128)(2,1)} %refs_4_.1) | copy-start | bytes 6291460
  84.6 4.4 %collective-permute-start.7 = (f32[1,256]{1,0:T(1,128)S(1)}, f32[1,256]{1,0:T(1,128)S(1)}, u32[]{:S(2)}, u32[]{:S(2)}) collective-permute-start(f32[1,256]{1,0:T(1,128)S(1)} %get-tuple-element.8), channel_id=1, source_target_pairs={{0,2},{2,0},{4,6},{6,4},{1,3},{3,1},{5,7},{7,5},{8,10},{10,8},{12,... | collective-permute-start | bytes 3080 | tf_op jit(solution)/shard_map/ppermute | solution.py:275
  84.7 4.5 %collective-permute-start.8 = (f32[1,256]{1,0:T(1,128)S(1)}, f32[1,256]{1,0:T(1,128)S(1)}, u32[]{:S(2)}, u32[]{:S(2)}) collective-permute-start(f32[1,256]{1,0:T(1,128)S(1)} %get-tuple-element.7), channel_id=1, source_target_pairs={{0,4},{2,6},{4,0},{6,2},{1,5},{3,7},{5,1},{7,3},{8,12},{10,14},{12... | collective-permute-start | bytes 3080 | tf_op jit(solution)/shard_map/ppermute | solution.py:275
  85.4 5.4 %collective-permute-start.9 = (f32[1,256]{1,0:T(1,128)S(1)}, f32[1,256]{1,0:T(1,128)S(1)}, u32[]{:S(2)}, u32[]{:S(2)}) collective-permute-start(f32[1,256]{1,0:T(1,128)S(1)} %get-tuple-element.6), channel_id=1, source_target_pairs={{0,6},{2,4},{4,2},{6,0},{1,7},{3,5},{5,3},{7,1},{8,14},{10,12},{12... | collective-permute-start | bytes 3080 | tf_op jit(solution)/shard_map/ppermute | solution.py:275

commit v15 on v14

--- a/solution.py
+++ b/solution.py
@@ -13,6 +13,7 @@
 GROUP = 8
 STEP = 4
 SLOTS = 2
+CUTS = 4
 ROWS = 2 * STEP
 HALVED = TOP // 2
 LANES = 128
@@ -46,21 +47,31 @@
     ybuf = (ybuf0, ybuf1)
     tbuf = (tbuf0, tbuf1)
 
-    def grad_copies(step, then):
+    def grad_copies(step, start):
         slot = step % SLOTS
-        for top in range(TOP):
-            copy = pltpu.make_async_copy(
-                grads.at[:, top, step],
-                xbuf.at[slot, :, :, top * ROWS * LANES : (top + 1) * ROWS * LANES],
-                sems.at[slot, top],
-            )
-            then(copy)
+        part = high_dev // CUTS
+        for cut in range(CUTS):
+            for top in range(TOP):
+                copy = pltpu.make_async_copy(
+                    grads.at[cut * part : (cut + 1) * part, top, step],
+                    xbuf.at[
+                        slot,
+                        cut * part : (cut + 1) * part,
+                        :,
+                        top * ROWS * LANES : (top + 1) * ROWS * LANES,
+                    ],
+                    sems.at[slot, cut, top],
+                )
+                if start:
+                    copy.start(priority=top % 2)
+                else:
+                    copy.wait()
 
     per_high = NMID * NLOW // 16 // LANES
     word_copy = pltpu.make_async_copy(words, wbuf, wsem)
     word_copy.start()
     for step in range(SLOTS):
-        grad_copies(step, lambda copy: copy.start())
+        grad_copies(step, True)
 
     table[...] = jnp.where(
         odd_common_bits(iota(table.shape, 0), iota(table.shape, 1)), -1.0, 1.0
@@ -172,7 +183,7 @@
     turns = STEP * TOP // PAIR
     per_chunk = GROUP // STEP
 
-    grad_copies(0, lambda copy: copy.wait())
+    grad_copies(0, False)
 
     @pl.loop(0, turns)
     def _(u):
@@ -180,9 +191,9 @@
 
     for step in range(steps):
         if step + SLOTS < steps:
-            grad_copies(step + SLOTS, lambda copy: copy.start())
+            grad_copies(step + SLOTS, True)
         if step + 1 < steps:
-            grad_copies(step + 1, lambda copy: copy.wait())
+            grad_copies(step + 1, False)
 
         @pl.loop(0, turns)
         def _(u):
@@ -260,7 +271,7 @@
             pltpu.VMEM((HALVED * groups, 24, points), jnp.float32),
             pltpu.VMEM((HALVED * groups, PACK, points), jnp.float32),
             pltpu.VMEM((HALVED, groups, points), jnp.float32),
-            pltpu.SemaphoreType.DMA((SLOTS, TOP)),
+            pltpu.SemaphoreType.DMA((SLOTS, CUTS, TOP)),
             pltpu.SemaphoreType.DMA,
         ],
         compiler_params=pltpu.CompilerParams(vmem_limit_bytes=63 * 1024 * 1024),

time: 91.8 us -> 91 us (level)
  no operation moved by 1% of the time
where the time goes in v15:
time: 91 us; the launch traced here: 90.6 us
  Pallas kernels  63.5 us (70%)
  starting transfers between devices  13.7 us (15%)
  waiting for transfers between devices  10.4 us (11%)
  local copies, waits for them, and re-layouts  1.63 us (2%)
  other arithmetic  1.39 us (2%)
    pallas_call x1, Pallas kernels, partial_sketch(): pl.pallas_call(functools.partial(sketch_kernel, high_dev=high_dev, scale=...  60.7 us
    ppermute x10, starting transfers between devices, swapped(): return lax.ppermute(value, axis, [(i, i ^ bits) for i in range(size)])  13.7 us
    ppermute x10, waiting for transfers between devices, swapped(): return lax.ppermute(value, axis, [(i, i ^ bits) for i in range(size)])  10.4 us
    pallas_call x1, Pallas kernels, scores_of(): pl.pallas_call(functools.partial(score_kernel, scale=scale), out_shape=ja...  2.78 us
  transfers between devices with their start and end apart: 10, of which 6 were waited for; matrix products, arithmetic and copies ran while one was open for 1% of the time, Pallas kernels for 67%

profile of v15, /device:TPU:0, one launch (start us, length us, event | category | flops | bytes accessed | tf_op | source)
XLA Modules:
  0.0 90.6 jit_solution(10936933074614426851)
XLA Ops:
  0.0 2.9 %collective-permute-start.6 = (bf16[128,8192]{1,0:T(8,128)(2,1)}, bf16[128,8192]{1,0:T(8,128)(2,1)}, u32[]{:S(2)}, u32[]{:S(2)}) collective-permute-start(bf16[128,8192]{1,0:T(8,128)(2,1)} %refs_4_.1), channel_id=1, source_target_pairs={{0,1},{1,0},{2,3},{3,2},{4,5},{5,4},{6,7},{7,6},{8,9},{9,8},{10,11... | collective-permute-start | bytes 6291464 | tf_op jit(solution)/shard_map/ppermute | solution.py:286
  2.9 60.7 %sketch.1 = f32[64,128]{1,0:T(8,128)} custom-call(s32[1]{0:T(128)} %bitcast.place_ref, bf16[256,8,8,1,1024]{4,3,2,1,0:T(2,128)(2,1)} %bitcast.1.grads, s32[8192,128]{1,0:T(8,128)} %bitcast.13, s32[64,128]{1,0:T(8,128)} %bitcast.14), custom_call_target="tpu_custom_call" | custom-call | flops 17179869184 | bytes 67108864 | tf_op jit(solution)/shard_map/sketch/pallas_call | solution.py:250
  63.6 0.1 collective-permute-start
  63.7 1.6 %collective-permute-start.1 = (f32[64,128]{1,0:T(8,128)}, f32[64,128]{1,0:T(8,128)S(1)}, u32[]{:S(2)}, u32[]{:S(2)}) collective-permute-start(f32[64,128]{1,0:T(8,128)} %sketch.1), channel_id=1, source_target_pairs={{0,16},{8,24},{16,0},{24,8},{1,17},{9,25},{17,1},{25,9},{2,18},{10... | collective-permute-start | bytes 98312 | tf_op jit(solution)/shard_map/ppermute | solution.py:286
  65.3 0.3 collective-permute-start.2
  65.6 0.0 collective-permute-done
  65.6 2.3 %collective-permute-done.1 = f32[64,128]{1,0:T(8,128)S(1)} collective-permute-done((f32[64,128]{1,0:T(8,128)}, f32[64,128]{1,0:T(8,128)S(1)}, u32[]{:S(2)}, u32[]{:S(2)}) %collective-permute-start.1) | collective-permute-done | bytes 32800 | tf_op jit(solution)/shard_map/ppermute | solution.py:286
  67.9 1.0 %collective-permute-done.2 = f32[64,128]{1,0:T(8,128)S(1)} collective-permute-done((f32[64,128]{1,0:T(8,128)}, f32[64,128]{1,0:T(8,128)S(1)}, u32[]{:S(2)}, u32[]{:S(2)}) %collective-permute-start.2) | collective-permute-done | bytes 32800 | tf_op jit(solution)/shard_map/ppermute | solution.py:286
  68.9 0.8 add_convert_fusion.refs_0_
  69.6 1.6 %collective-permute-start.3 = (bf16[64,128]{1,0:T(8,128)(2,1)S(1)}, bf16[64,128]{1,0:T(8,128)(2,1)S(1)}, u32[]{:S(2)}, u32[]{:S(2)}) collective-permute-start(bf16[64,128]{1,0:T(8,128)(2,1)S(1)} %add_convert_fusion.refs_0_), channel_id=1, source_target_pairs={{0,2},{2,0},{4,6},{6,4},{1,3},{3,1},{5,7},{7,5},{8,10},{10,8},{12,... | collective-permute-start | bytes 49160 | tf_op jit(solution)/shard_map/ppermute | solution.py:286
  71.3 2.6 %collective-permute-start.4 = (bf16[64,128]{1,0:T(8,128)(2,1)S(1)}, bf16[64,128]{1,0:T(8,128)(2,1)S(1)}, u32[]{:S(2)}, u32[]{:S(2)}) collective-permute-start(bf16[64,128]{1,0:T(8,128)(2,1)S(1)} %add_convert_fusion.refs_0_), channel_id=1, source_target_pairs={{0,4},{2,6},{4,0},{6,2},{1,5},{3,7},{5,1},{7,3},{8,12},{10,14},{12... | collective-permute-start | bytes 49160 | tf_op jit(solution)/shard_map/ppermute | solution.py:286
  73.9 0.2 collective-permute-start.5
  74.1 0.0 collective-permute-done.3.refs_1_
  74.1 1.9 %collective-permute-done.4.refs_2_ = bf16[64,128]{1,0:T(8,128)(2,1)S(1)} collective-permute-done((bf16[64,128]{1,0:T(8,128)(2,1)S(1)}, bf16[64,128]{1,0:T(8,128)(2,1)S(1)}, u32[]{:S(2)}, u32[]{:S(2)}) %collective-permute-start.4) | collective-permute-done | bytes 16416 | tf_op jit(solution)/shard_map/ppermute | solution.py:286
  76.0 3.4 %collective-permute-done.5.refs_3_ = bf16[64,128]{1,0:T(8,128)(2,1)S(1)} collective-permute-done((bf16[64,128]{1,0:T(8,128)(2,1)S(1)}, bf16[64,128]{1,0:T(8,128)(2,1)S(1)}, u32[]{:S(2)}, u32[]{:S(2)}) %collective-permute-start.5) | collective-permute-done | bytes 16416 | tf_op jit(solution)/shard_map/ppermute | solution.py:286
  79.4 0.0 collective-permute-done.6
  79.4 0.0 copy-start
  79.4 1.6 %copy-done = bf16[128,8192]{1,0:T(8,128)(2,1)S(1)} copy-done((bf16[128,8192]{1,0:T(8,128)(2,1)S(1)}, bf16[128,8192]{1,0:T(8,128)(2,1)}, u32[]{:S(2)}) %copy-start) | copy-done | bytes 2097176
  81.0 2.8 %scores.1 = f32[4,256]{1,0:T(4,128)S(1)} custom-call(bf16[64,128]{1,0:T(8,128)(2,1)S(1)} %add_convert_fusion.refs_0_, bf16[64,128]{1,0:T(8,128)(2,1)S(1)} %collective-permute-done.3.refs_1_, bf16[64,128]{1,0:T(8,128)(2,1)S(1)} %collective-permute-done.4.refs_2_, bf16[64,128]{1,0:T(8,128)(2,1)S(1)} %collective-permute-done.5.refs_3_, ...), custom_call_target="tpu_custom_call" | custom-call | tf_op jit(solution)/shard_map/scores/pallas_call | solution.py:307
  83.8 0.1 collective-permute-start.7
  83.8 0.8 collective-permute-start.8
  84.6 3.6 %collective-permute-start.9 = (f32[1,256]{1,0:T(1,128)S(1)}, f32[1,256]{1,0:T(1,128)S(1)}, u32[]{:S(2)}, u32[]{:S(2)}) collective-permute-start(f32[1,256]{1,0:T(1,128)S(1)} %get-tuple-element.6), channel_id=1, source_target_pairs={{0,6},{2,4},{4,2},{6,0},{1,7},{3,5},{5,3},{7,1},{8,14},{10,12},{12... | collective-permute-start | bytes 3080 | tf_op jit(solution)/shard_map/ppermute | solution.py:286
  88.2 0.0 collective-permute-done.7
  88.2 0.2 collective-permute-done.8
  88.4 1.6 %collective-permute-done.9 = f32[1,256]{1,0:T(1,128)S(1)} collective-permute-done((f32[1,256]{1,0:T(1,128)S(1)}, f32[1,256]{1,0:T(1,128)S(1)}, u32[]{:S(2)}, u32[]{:S(2)}) %collective-permute-start.9) | collective-permute-done | bytes 1056 | tf_op jit(solution)/shard_map/ppermute | solution.py:286
  90.0 0.6 reverse_select_fusion
  (5 shorter events, 0.1 us)
Async XLA Ops:
  0.0 79.4 %collective-permute-start.6 = (bf16[128,8192]{1,0:T(8,128)(2,1)}, bf16[128,8192]{1,0:T(8,128)(2,1)}, u32[]{:S(2)}, u32[]{:S(2)}) collective-permute-start(bf16[128,8192]{1,0:T(8,128)(2,1)} %refs_4_.1), channel_id=1, source_target_pairs={{0,1},{1,0},{2,3},{3,2},{4,5},{5,4},{6,7},{7,6},{8,9},{9,8},{10,11... | collective-permute-start | bytes 6291464 | tf_op jit(solution)/shard_map/ppermute | solution.py:286
  63.6 1.9 %collective-permute-start = (f32[64,128]{1,0:T(8,128)}, f32[64,128]{1,0:T(8,128)S(1)}, u32[]{:S(2)}, u32[]{:S(2)}) collective-permute-start(f32[64,128]{1,0:T(8,128)} %sketch.1), channel_id=1, source_target_pairs={{0,8},{8,0},{16,24},{24,16},{1,9},{9,1},{17,25},{25,17},{2,10},{10... | collective-permute-start | bytes 98312 | tf_op jit(solution)/shard_map/ppermute | solution.py:286
  63.7 4.2 %collective-permute-start.1 = (f32[64,128]{1,0:T(8,128)}, f32[64,128]{1,0:T(8,128)S(1)}, u32[]{:S(2)}, u32[]{:S(2)}) collective-permute-start(f32[64,128]{1,0:T(8,128)} %sketch.1), channel_id=1, source_target_pairs={{0,16},{8,24},{16,0},{24,8},{1,17},{9,25},{17,1},{25,9},{2,18},{10... | collective-permute-start | bytes 98312 | tf_op jit(solution)/shard_map/ppermute | solution.py:286
  65.3 3.6 %collective-permute-start.2 = (f32[64,128]{1,0:T(8,128)}, f32[64,128]{1,0:T(8,128)S(1)}, u32[]{:S(2)}, u32[]{:S(2)}) collective-permute-start(f32[64,128]{1,0:T(8,128)} %sketch.1), channel_id=1, source_target_pairs={{0,24},{8,16},{16,8},{24,0},{1,25},{9,17},{17,9},{25,1},{2,26},{10... | collective-permute-start | bytes 98312 | tf_op jit(solution)/shard_map/ppermute | solution.py:286
  69.6 4.5 %collective-permute-start.3 = (bf16[64,128]{1,0:T(8,128)(2,1)S(1)}, bf16[64,128]{1,0:T(8,128)(2,1)S(1)}, u32[]{:S(2)}, u32[]{:S(2)}) collective-permute-start(bf16[64,128]{1,0:T(8,128)(2,1)S(1)} %add_convert_fusion.refs_0_), channel_id=1, source_target_pairs={{0,2},{2,0},{4,6},{6,4},{1,3},{3,1},{5,7},{7,5},{8,10},{10,8},{12,... | collective-permute-start | bytes 49160 | tf_op jit(solution)/shard_map/ppermute | solution.py:286
  71.3 4.7 %collective-permute-start.4 = (bf16[64,128]{1,0:T(8,128)(2,1)S(1)}, bf16[64,128]{1,0:T(8,128)(2,1)S(1)}, u32[]{:S(2)}, u32[]{:S(2)}) collective-permute-start(bf16[64,128]{1,0:T(8,128)(2,1)S(1)} %add_convert_fusion.refs_0_), channel_id=1, source_target_pairs={{0,4},{2,6},{4,0},{6,2},{1,5},{3,7},{5,1},{7,3},{8,12},{10,14},{12... | collective-permute-start | bytes 49160 | tf_op jit(solution)/shard_map/ppermute | solution.py:286
  73.9 5.5 %collective-permute-start.5 = (bf16[64,128]{1,0:T(8,128)(2,1)S(1)}, bf16[64,128]{1,0:T(8,128)(2,1)S(1)}, u32[]{:S(2)}, u32[]{:S(2)}) collective-permute-start(bf16[64,128]{1,0:T(8,128)(2,1)S(1)} %add_convert_fusion.refs_0_), channel_id=1, source_target_pairs={{0,6},{2,4},{4,2},{6,0},{1,7},{3,5},{5,3},{7,1},{8,14},{10,12},{12... | collective-permute-start | bytes 49160 | tf_op jit(solution)/shard_map/ppermute | solution.py:286
  79.4 1.6 %copy-start = (bf16[128,8192]{1,0:T(8,128)(2,1)S(1)}, bf16[128,8192]{1,0:T(8,128)(2,1)}, u32[]{:S(2)}) copy-start(bf16[128,8192]{1,0:T(8,128)(2,1)} %refs_4_.1) | copy-start | bytes 6291460
  83.8 4.4 %collective-permute-start.7 = (f32[1,256]{1,0:T(1,128)S(1)}, f32[1,256]{1,0:T(1,128)S(1)}, u32[]{:S(2)}, u32[]{:S(2)}) collective-permute-start(f32[1,256]{1,0:T(1,128)S(1)} %get-tuple-element.8), channel_id=1, source_target_pairs={{0,2},{2,0},{4,6},{6,4},{1,3},{3,1},{5,7},{7,5},{8,10},{10,8},{12,... | collective-permute-start | bytes 3080 | tf_op jit(solution)/shard_map/ppermute | solution.py:286
  83.8 4.5 %collective-permute-start.8 = (f32[1,256]{1,0:T(1,128)S(1)}, f32[1,256]{1,0:T(1,128)S(1)}, u32[]{:S(2)}, u32[]{:S(2)}) collective-permute-start(f32[1,256]{1,0:T(1,128)S(1)} %get-tuple-element.7), channel_id=1, source_target_pairs={{0,4},{2,6},{4,0},{6,2},{1,5},{3,7},{5,1},{7,3},{8,12},{10,14},{12... | collective-permute-start | bytes 3080 | tf_op jit(solution)/shard_map/ppermute | solution.py:286
  84.6 5.4 %collective-permute-start.9 = (f32[1,256]{1,0:T(1,128)S(1)}, f32[1,256]{1,0:T(1,128)S(1)}, u32[]{:S(2)}, u32[]{:S(2)}) collective-permute-start(f32[1,256]{1,0:T(1,128)S(1)} %get-tuple-element.6), channel_id=1, source_target_pairs={{0,6},{2,4},{4,2},{6,0},{1,7},{3,5},{5,3},{7,1},{8,14},{10,12},{12... | collective-permute-start | bytes 3080 | tf_op jit(solution)/shard_map/ppermute | solution.py:286
